TPU v7x, 32 devices: a whole 2x2x4 slice. The times are simulated.
32 devices in a mesh: tile: 16 (over z, y, x), band: 2 (over core).
Axes of the slice: x: 2, y: 2, z: 4, core: 2. Of those that a mesh axis runs over, the one named last changes fastest.
Arguments:
- concentration: float32 [4, 24, 128, 512], P(None, 'band', 'tile'), may hold values from -6 to 6
- adjoint_later: float32 [4, 24, 128, 512], P(None, 'band', 'tile'), may hold values from -6 to 6
- courant_east: float32 [24, 128, 512], P('band', 'tile'), may hold values from -0.25 to 0.25
- courant_north: float32 [24, 128, 512], P('band', 'tile'), may hold values from -0.25 to 0.25
- diffusivity: float32 [24, 128, 512], P('band', 'tile'), may hold values from 1 to 100
- tracer_factor: float32 [4], replicated, may hold values from 0.5 to 2
- sounding_cell: int32 [4096], P('tile'), may hold values from -1 to 4095, as said below
- sounding_value: float32 [4096], P('tile'), may hold values from -6 to 6
- sounding_precision: float32 [4096], P('tile'), may hold values from 0.2 to 2
- sounding_weight: float32 [4096, 24], P('tile', 'band')
Outputs:
- adjoint_earlier: float32 [4, 24, 128, 512], P(None, 'band', 'tile')
Inputs may be any that keep to these rules, and one draw needn't show every extreme that they name: `sounding_cell`: slots come in blocks of 16, one block for each pair of owner and tile (tile = block index modulo 16); in a block the live slots come first and the rest hold -1. Every owner fills at least one block completely, and one tile receives full blocks from every owner.
All inputs are finite; a program needn't handle non-finite values.
Results may differ from a plain program's by a relative error of at most 0.0003.
Values sent between devices are 32-bit elements; how exact they have to be, the bound alone decides.
No kernel may reach another device: no remote copies, remote signals or barrier semaphores. Data moves between devices by JAX's collectives and lax.ppermute only.
A program may use at most 64 MiB of HBM per device.

v0:
```python
import jax
import jax.numpy as jnp
from jax import lax
from jax.sharding import PartitionSpec as P

STEPS = 2


def with_halo(block, sides, width):
    for axis, dim in sides:
        count = lax.axis_size(axis)
        forward = [(i, i + 1) for i in range(count - 1)]
        forward.append((count - 1, 0))
        backward = [(target, source) for source, target in forward]
        low = lax.ppermute(
            lax.slice_in_dim(block, block.shape[dim] - width, None, axis=dim), axis, forward
        )
        high = lax.ppermute(lax.slice_in_dim(block, 0, width, axis=dim), axis, backward)
        block = jnp.concatenate([low, block, high], axis=dim)
    return block


def passed_along(x, axis, by):
    devices = lax.axis_size(axis)
    return lax.ppermute(x, axis, [(i, (i + by) % devices) for i in range(devices)])


def solve_column(centre, coupling_down, coupling_up, sources):
    depth = len(centre)
    ratios = []
    sweeps = [[] for member in sources]
    for height in range(depth):
        if height == 0:
            divisor = centre[0]
        else:
            divisor = centre[height] - coupling_down[height] * ratios[height - 1]
        ratios.append(coupling_up[height] / divisor)
        member = 0
        amount = sources[member][height]
        if height > 0:
            amount = amount + coupling_down[height] * sweeps[member][height - 1]
        sweeps[member].append(amount / divisor)
    member = 0
    column = [None] * depth
    column[depth - 1] = sweeps[member][depth - 1]
    for height in range(depth - 2, -1, -1):
        column[height] = sweeps[member][height] + ratios[height] * column[height + 1]
    results = [column]
    return results


def column_matrix(below_first, interfaces):
    coupling_down = [below_first] + interfaces[:-1]
    centre = [1.0 + coupling_down[height] + interfaces[height] for height in range(len(interfaces))]
    return (centre, coupling_down, interfaces)


def advect_sides(
    adjoint,
    east_side,
    west_side,
    north_side,
    south_side,
    east_face,
    west_face,
    north_face,
    south_face,
):
    return (
        adjoint
        + jnp.maximum(east_face, 0.0) * (east_side - adjoint)
        + jnp.minimum(west_face, 0.0) * (adjoint - west_side)
        + jnp.maximum(north_face, 0.0) * (north_side - adjoint)
        + jnp.minimum(south_face, 0.0) * (adjoint - south_side)
    )


def advect_back(adjoint, east_face, west_face, north_face, south_face):
    padded = with_halo(adjoint, (("tile", 2),), 1)
    zero_row = jnp.zeros_like(adjoint[..., :1])
    north_side = jnp.concatenate([adjoint[..., 1:], zero_row], axis=3)
    south_side = jnp.concatenate([zero_row, adjoint[..., :-1]], axis=3)
    return advect_sides(
        adjoint,
        padded[:, :, 2:, :],
        padded[:, :, :-2, :],
        north_side,
        south_side,
        east_face,
        west_face,
        north_face,
        south_face,
    )


def per_device(
    concentration,
    adjoint_later,
    courant_east,
    courant_north,
    diffusivity,
    tracer_factor,
    sounding_cell,
    sounding_value,
    sounding_precision,
    sounding_weight,
):
    tracers, band_levels, tile_cols, tile_rows = concentration.shape
    cell_float = sounding_cell.astype(jnp.float32)
    cell_moved, value_here, precision_here, weight_here = (
        lax.all_to_all(cell_float, "tile", split_axis=0, concat_axis=0, tiled=True),
        lax.all_to_all(sounding_value, "tile", split_axis=0, concat_axis=0, tiled=True),
        lax.all_to_all(sounding_precision, "tile", split_axis=0, concat_axis=0, tiled=True),
        lax.all_to_all(sounding_weight, "tile", split_axis=0, concat_axis=0, tiled=True),
    )
    cells_here = cell_moved.astype(jnp.int32)
    total = jnp.sum(concentration, axis=0).reshape(band_levels, tile_cols * tile_rows)
    live = cells_here >= 0
    safe_cells = jnp.maximum(cells_here, 0)
    picked = jnp.take(total, safe_cells, axis=1)
    weight_levels = weight_here.T
    partial_sum = jnp.sum(weight_levels * picked, axis=0)
    column_mean = lax.psum(partial_sum, "band")
    misfit = jnp.where(live, precision_here * (column_mean - value_here), 0.0)
    contribution = weight_levels * misfit[None, :]
    forcing = (
        jnp.zeros((band_levels, tile_cols * tile_rows), jnp.float32)
        .at[:, safe_cells]
        .add(contribution)
    )
    adjoint = adjoint_later + forcing.reshape(band_levels, tile_cols, tile_rows)[None]
    west_edge = passed_along(courant_east[:, -1:, :], "tile", 1)
    west_face = jnp.concatenate([west_edge, courant_east[:, :-1, :]], axis=1)
    latitude = lax.broadcasted_iota(jnp.int32, courant_north.shape, 2)
    north_face = jnp.where(latitude == tile_rows - 1, 0.0, courant_north)
    south_face = jnp.concatenate(
        [jnp.zeros_like(north_face[..., :1]), north_face[..., :-1]], axis=2
    )
    scale_tracer = tracer_factor[:, None, None]
    diffusion_full = lax.all_to_all(diffusivity, "band", split_axis=1, concat_axis=0, tiled=True)
    full_levels = diffusion_full.shape[0]
    interfaces = [scale_tracer * diffusion_full[height] for height in range(full_levels - 1)]
    interfaces.append(jnp.zeros_like(interfaces[0]))
    centre, coupling_down, coupling_up = column_matrix(jnp.zeros_like(interfaces[0]), interfaces)
    for step_at in range(STEPS):
        columns = lax.all_to_all(adjoint, "band", split_axis=2, concat_axis=1, tiled=True)
        solved_columns = solve_column(
            centre,
            coupling_down,
            coupling_up,
            [[columns[:, height] for height in range(full_levels)]],
        )[0]
        solved = lax.all_to_all(
            jnp.stack(solved_columns, axis=1), "band", split_axis=1, concat_axis=2, tiled=True
        )
        adjoint = advect_back(solved, courant_east, west_face, north_face, south_face)
    return adjoint


def solution(mesh):
    return jax.shard_map(
        per_device,
        mesh=mesh,
        in_specs=(
            P(None, "band", "tile", None),
            P(None, "band", "tile", None),
            P("band", "tile", None),
            P("band", "tile", None),
            P("band", "tile", None),
            P(),
            P("tile"),
            P("tile"),
            P("tile"),
            P("tile", "band"),
        ),
        out_specs=P(None, "band", "tile", None),
        check_vma=False,
    )
```

profile of v0, /device:TPU:0, one launch (start us, length us, event | category | flops | bytes accessed | tf_op | source)
XLA Modules:
  0.0 111.4 jit_solution(16344647888158245558)
XLA Ops:
  1.1 3.0 %collective-permute-start.1 = (f32[12,1,512]{2,1,0:T(1,128)S(1)}, f32[12,1,512]{2,1,0:T(1,128)S(1)}, u32[]{:S(2)}, u32[]{:S(2)}) collective-permute-start(f32[12,1,512]{2,1,0:T(1,128)S(1)} %slice.311), channel_id=1, source_target_pairs={{0,2},{2,4},{4,6},{6,8},{8,10},{10,12},{12,14},{14,16},{16,18},{18... | collective-permute-start | bytes 73736 | tf_op jit(solution)/shard_map/ppermute | solution.py:25
  4.1 1.7 %copy.34 = f32[12,8,512]{2,0,1:T(8,128)} copy(f32[12,8,512]{2,1,0:T(8,128)} %param.14) | data formatting | bytes 393216 | tf_op args[4]
  5.8 3.4 %all-to-all-start.5 = ((f32[12,8,512]{2,0,1:T(8,128)}), f32[12,8,512]{2,0,1:T(8,128)S(1)}, u32[]{:S(2)}, u32[]{:S(2)}) async-start(f32[12,8,512]{2,0,1:T(8,128)} %copy.34), calls=%async_computation.5 | async-start | bytes 524288 | tf_op jit(solution)/shard_map/all_to_all | solution.py:140
  10.8 5.9 %all-to-all-start = ((f32[16,16,1]{1,2,0:T(1,128)}), f32[16,16,1]{1,2,0:T(1,128)S(1)}, u32[]{:S(2)}, u32[]{:S(2)}) async-start(f32[16,16,1]{1,2,0:T(1,128)} %bitcast), calls=%async_computation | async-start | bytes 16384 | tf_op jit(solution)/shard_map/all_to_all | solution.py:111
  21.0 3.0 %all-to-all-done = f32[16,16,1]{1,2,0:T(1,128)S(1)} async-done(((f32[16,16,1]{1,2,0:T(1,128)}), f32[16,16,1]{1,2,0:T(1,128)S(1)}, u32[]{:S(2)}, u32[]{:S(2)}) %all-to-all-start) | async-done | bytes 1056 | tf_op jit(solution)/shard_map/all_to_all | solution.py:111
  24.0 3.9 %all-to-all-start.2 = ((f32[16,16,1]{1,2,0:T(1,128)}), f32[16,16,1]{1,2,0:T(1,128)S(1)}, u32[]{:S(2)}, u32[]{:S(2)}) async-start(f32[16,16,1]{1,2,0:T(1,128)} %bitcast.3), calls=%async_computation.2 | async-start | bytes 16384 | tf_op jit(solution)/shard_map/all_to_all | solution.py:113
  28.0 7.2 %all-to-all-done.2 = f32[16,16,1]{1,2,0:T(1,128)S(1)} async-done(((f32[16,16,1]{1,2,0:T(1,128)}), f32[16,16,1]{1,2,0:T(1,128)S(1)}, u32[]{:S(2)}, u32[]{:S(2)}) %all-to-all-start.2) | async-done | bytes 1056 | tf_op jit(solution)/shard_map/all_to_all | solution.py:113
  35.2 3.4 %all-to-all-start.3 = ((f32[16,16,1]{1,2,0:T(1,128)}), f32[16,16,1]{1,2,0:T(1,128)S(1)}, u32[]{:S(2)}, u32[]{:S(2)}) async-start(f32[16,16,1]{1,2,0:T(1,128)} %bitcast.5), calls=%async_computation.3 | async-start | bytes 16384 | tf_op jit(solution)/shard_map/all_to_all | solution.py:112
  38.7 7.1 %all-to-all-done.3 = f32[16,16,1]{1,2,0:T(1,128)S(1)} async-done(((f32[16,16,1]{1,2,0:T(1,128)}), f32[16,16,1]{1,2,0:T(1,128)S(1)}, u32[]{:S(2)}, u32[]{:S(2)}) %all-to-all-start.3) | async-done | bytes 1056 | tf_op jit(solution)/shard_map/all_to_all | solution.py:112
  45.8 3.5 %all-to-all-start.1 = ((f32[16,1,192]{2,1,0:T(1,128)}), f32[16,1,192]{2,1,0:T(1,128)S(1)}, u32[]{:S(2)}, u32[]{:S(2)}) async-start(f32[16,1,192]{2,1,0:T(1,128)} %reshape.518), calls=%async_computation.1 | async-start | bytes 32768 | tf_op jit(solution)/shard_map/all_to_all | solution.py:114
  52.3 4.4 %all-to-all-done.1 = f32[16,1,192]{2,1,0:T(1,128)S(1)} async-done(((f32[16,1,192]{2,1,0:T(1,128)}), f32[16,1,192]{2,1,0:T(1,128)S(1)}, u32[]{:S(2)}, u32[]{:S(2)}) %all-to-all-start.1) | async-done | bytes 12320 | tf_op jit(solution)/shard_map/all_to_all | solution.py:114
  58.1 2.5 %psum.7 = f32[256]{0:T(256)S(1)} all-reduce(f32[256]{0:T(256)S(1)} %fusion.18), channel_id=1, replica_groups=mesh['tile'=16,'band'=2] {'band'}, use_global_device_ids=true, to_apply=%region_2.3 | all-reduce | flops 256 | bytes 2048 | tf_op jit(solution)/shard_map/psum | solution.py:123
  60.7 2.2 %scatter_custom_fusion = f32[12,4096]{0,1:T(8,128)S(1)} fusion(s32[256]{0:T(256)S(1)} %reshape.483, f32[256,12]{1,0:T(8,128)S(1)} %bitcast_multiply_fusion, f32[]{:T(128)} %constant.8.clone.1), kind=kCustom, calls=%fused_computation.3 | custom fusion | flops 3072 | bytes 196612 | tf_op jit(solution)/shard_map/scatter-add | solution.py:129
  63.6 1.6 %copy_add_fusion = f32[4,12,8,512]{3,1,0,2:T(8,128)S(1)} fusion(f32[4,12,8,512]{3,2,1,0:T(8,128)} %param.11, f32[12,8,512]{2,0,1:T(8,128)S(1)} %copy.31), kind=kLoop, calls=%fused_computation.2 | loop fusion | flops 196608 | bytes 1769472 | tf_op jit(solution)/shard_map/add | solution.py:131
  65.2 4.6 %all_to_all.135 = f32[4,12,8,512]{3,1,0,2:T(8,128)S(1)} all-to-all(f32[4,12,8,512]{3,1,0,2:T(8,128)S(1)} %copy_add_fusion), channel_id=1, replica_groups=mesh['tile'=16,'band'=2] {'band'}, dimensions={2} | all-to-all | bytes 1572864 | tf_op jit(solution)/shard_map/all_to_all | solution.py:146
  72.9 4.4 %all_to_all.136 = f32[4,24,4,512]{3,2,0,1:T(4,128)S(1)} all-to-all(f32[4,24,4,512]{3,2,0,1:T(4,128)S(1)} %copy.36), channel_id=1, replica_groups=mesh['tile'=16,'band'=2] {'band'}, dimensions={1} | all-to-all | bytes 1572864 | tf_op jit(solution)/shard_map/all_to_all | solution.py:153
  80.2 3.6 %collective-permute-done = f32[4,12,1,512]{3,0,2,1:T(4,128)S(1)} collective-permute-done((f32[4,12,1,512]{3,0,2,1:T(4,128)S(1)}, f32[4,12,1,512]{3,0,2,1:T(4,128)S(1)}, u32[]{:S(2)}, u32[]{:S(2)}) %collective-permute-start) | collective-permute-done | bytes 98336 | tf_op jit(solution)/shard_map/ppermute | solution.py:18
  83.7 3.5 %collective-permute-done.2 = f32[4,12,1,512]{3,0,2,1:T(4,128)S(1)} collective-permute-done((f32[4,12,1,512]{3,0,2,1:T(4,128)S(1)}, f32[4,12,1,512]{3,0,2,1:T(4,128)S(1)}, u32[]{:S(2)}, u32[]{:S(2)}) %collective-permute-start.2) | collective-permute-done | bytes 98336 | tf_op jit(solution)/shard_map/ppermute | solution.py:15
  87.3 1.1 %fusion.14 = f32[4,12,8,512]{3,0,2,1:T(4,128)S(1)} fusion(f32[4,12,8,512]{3,0,2,1:T(4,128)S(1)} %bitcast.83, f32[4,12,1,512]{3,0,2,1:T(4,128)S(1)} %collective-permute-done.2, f32[4,12,1,512]{3,0,2,1:T(4,128)S(1)} %collective-permute-done, f32[4,12,8,511]{3,0,2,1:T(4,128)S(1)} %get-tuple-element.88, f32[4,12,8,511]{3,0,2,1:T(4,128)S(1)} %get-tuple-element.87, ...), kind=kLoop, calls=%fused_computation.20 | loop fusion | flops 2752512 | bytes 4125696 | tf_op jit(solution)/shard_map/add | solution.py:70
  88.5 4.4 %all_to_all.137 = f32[4,12,8,512]{3,0,1,2:T(4,128)S(1)} all-to-all(f32[4,12,8,512]{3,0,1,2:T(4,128)S(1)} %copy.39), channel_id=1, replica_groups=mesh['tile'=16,'band'=2] {'band'}, dimensions={2} | all-to-all | bytes 1572864 | tf_op jit(solution)/shard_map/all_to_all | solution.py:146
  95.9 4.4 %all_to_all.138 = f32[4,24,4,512]{3,2,0,1:T(4,128)S(1)} all-to-all(f32[4,24,4,512]{3,2,0,1:T(4,128)S(1)} %copy.41), channel_id=1, replica_groups=mesh['tile'=16,'band'=2] {'band'}, dimensions={1} | all-to-all | bytes 1572864 | tf_op jit(solution)/shard_map/all_to_all | solution.py:153
  101.0 1.7 %collective-permute-start.4 = (f32[4,12,1,512]{3,0,2,1:T(4,128)S(1)}, f32[4,12,1,512]{3,0,2,1:T(4,128)S(1)}, u32[]{:S(2)}, u32[]{:S(2)}) collective-permute-start(f32[4,12,1,512]{3,0,2,1:T(4,128)S(1)} %get-tuple-element.86), channel_id=1, source_target_pairs={{0,2},{2,4},{4,6},{6,8},{8,10},{10,12},{12,14},{14,16},{16,18},{18... | collective-permute-start | bytes 294920 | tf_op jit(solution)/shard_map/ppermute | solution.py:15
  103.1 3.1 %collective-permute-done.3 = f32[4,12,1,512]{3,0,2,1:T(4,128)S(1)} collective-permute-done((f32[4,12,1,512]{3,0,2,1:T(4,128)S(1)}, f32[4,12,1,512]{3,0,2,1:T(4,128)S(1)}, u32[]{:S(2)}, u32[]{:S(2)}) %collective-permute-start.3) | collective-permute-done | bytes 98336 | tf_op jit(solution)/shard_map/ppermute | solution.py:18
  106.3 2.9 %collective-permute-done.4 = f32[4,12,1,512]{3,0,2,1:T(4,128)S(1)} collective-permute-done((f32[4,12,1,512]{3,0,2,1:T(4,128)S(1)}, f32[4,12,1,512]{3,0,2,1:T(4,128)S(1)}, u32[]{:S(2)}, u32[]{:S(2)}) %collective-permute-start.4) | collective-permute-done | bytes 98336 | tf_op jit(solution)/shard_map/ppermute | solution.py:15
  (115 shorter events, 24.4 us)
Async XLA Ops:
  0.0 17.9 %copy-start = (f32[12,8,512]{2,1,0:T(8,128)S(1)}, f32[12,8,512]{2,1,0:T(8,128)}, u32[]{:S(2)}) copy-start(f32[12,8,512]{2,1,0:T(8,128)} %param.12) | copy-start | bytes 589828
  0.0 18.0 %copy-start.4 = (f32[256]{0:T(256)S(1)}, f32[256]{0:T(256)}, u32[]{:S(2)}) copy-start(f32[256]{0:T(256)} %param.17) | copy-start | bytes 3076
  0.0 18.7 %copy-start.5 = (f32[256]{0:T(256)S(1)}, f32[256]{0:T(256)}, u32[]{:S(2)}) copy-start(f32[256]{0:T(256)} %param.18) | copy-start | bytes 3076
  0.0 19.4 %copy-start.3 = (f32[256,12]{0,1:T(8,128)S(1)}, f32[256,12]{0,1:T(8,128)}, u32[]{:S(2)}) copy-start(f32[256,12]{0,1:T(8,128)} %param.19) | copy-start | bytes 36868
  0.0 20.2 %copy-start.1 = (f32[4,12,8,512]{3,2,1,0:T(8,128)S(1)}, f32[4,12,8,512]{3,2,1,0:T(8,128)}, u32[]{:S(2)}) copy-start(f32[4,12,8,512]{3,2,1,0:T(8,128)} %param.10) | copy-start | bytes 2359300
  1.1 79.1 %collective-permute-start.1 = (f32[12,1,512]{2,1,0:T(1,128)S(1)}, f32[12,1,512]{2,1,0:T(1,128)S(1)}, u32[]{:S(2)}, u32[]{:S(2)}) collective-permute-start(f32[12,1,512]{2,1,0:T(1,128)S(1)} %slice.311), channel_id=1, source_target_pairs={{0,2},{2,4},{4,6},{6,8},{8,10},{10,12},{12,14},{14,16},{16,18},{18... | collective-permute-start | bytes 73736 | tf_op jit(solution)/shard_map/ppermute | solution.py:25
  5.8 5.0 %all-to-all-start.5 = ((f32[12,8,512]{2,0,1:T(8,128)}), f32[12,8,512]{2,0,1:T(8,128)S(1)}, u32[]{:S(2)}, u32[]{:S(2)}) async-start(f32[12,8,512]{2,0,1:T(8,128)} %copy.34), calls=%async_computation.5 | async-start | bytes 524288 | tf_op jit(solution)/shard_map/all_to_all | solution.py:140
  10.8 13.2 %all-to-all-start = ((f32[16,16,1]{1,2,0:T(1,128)}), f32[16,16,1]{1,2,0:T(1,128)S(1)}, u32[]{:S(2)}, u32[]{:S(2)}) async-start(f32[16,16,1]{1,2,0:T(1,128)} %bitcast), calls=%async_computation | async-start | bytes 16384 | tf_op jit(solution)/shard_map/all_to_all | solution.py:111
  24.0 11.2 %all-to-all-start.2 = ((f32[16,16,1]{1,2,0:T(1,128)}), f32[16,16,1]{1,2,0:T(1,128)S(1)}, u32[]{:S(2)}, u32[]{:S(2)}) async-start(f32[16,16,1]{1,2,0:T(1,128)} %bitcast.3), calls=%async_computation.2 | async-start | bytes 16384 | tf_op jit(solution)/shard_map/all_to_all | solution.py:113
  35.2 10.7 %all-to-all-start.3 = ((f32[16,16,1]{1,2,0:T(1,128)}), f32[16,16,1]{1,2,0:T(1,128)S(1)}, u32[]{:S(2)}, u32[]{:S(2)}) async-start(f32[16,16,1]{1,2,0:T(1,128)} %bitcast.5), calls=%async_computation.3 | async-start | bytes 16384 | tf_op jit(solution)/shard_map/all_to_all | solution.py:112
  45.8 10.8 %all-to-all-start.1 = ((f32[16,1,192]{2,1,0:T(1,128)}), f32[16,1,192]{2,1,0:T(1,128)S(1)}, u32[]{:S(2)}, u32[]{:S(2)}) async-start(f32[16,1,192]{2,1,0:T(1,128)} %reshape.518), calls=%async_computation.1 | async-start | bytes 32768 | tf_op jit(solution)/shard_map/all_to_all | solution.py:114
  65.2 5.1 %copy-start.2 = (f32[4]{0:T(128)S(1)}, f32[4]{0:T(128)}, u32[]{:S(2)}) copy-start(f32[4]{0:T(128)} %param.15) | copy-start | bytes 52
  78.1 5.7 %collective-permute-start = (f32[4,12,1,512]{3,0,2,1:T(4,128)S(1)}, f32[4,12,1,512]{3,0,2,1:T(4,128)S(1)}, u32[]{:S(2)}, u32[]{:S(2)}) collective-permute-start(f32[4,12,1,512]{3,0,2,1:T(4,128)S(1)} %get-tuple-element.89), channel_id=1, source_target_pairs={{2,0},{4,2},{6,4},{8,6},{10,8},{12,10},{14,12},{16,14},{18,16},{20... | collective-permute-start | bytes 294920 | tf_op jit(solution)/shard_map/ppermute | solution.py:18
  79.1 8.2 %collective-permute-start.2 = (f32[4,12,1,512]{3,0,2,1:T(4,128)S(1)}, f32[4,12,1,512]{3,0,2,1:T(4,128)S(1)}, u32[]{:S(2)}, u32[]{:S(2)}) collective-permute-start(f32[4,12,1,512]{3,0,2,1:T(4,128)S(1)} %get-tuple-element.90), channel_id=1, source_target_pairs={{0,2},{2,4},{4,6},{6,8},{8,10},{10,12},{12,14},{14,16},{16,18},{18... | collective-permute-start | bytes 294920 | tf_op jit(solution)/shard_map/ppermute | solution.py:15
  100.6 5.7 %collective-permute-start.3 = (f32[4,12,1,512]{3,0,2,1:T(4,128)S(1)}, f32[4,12,1,512]{3,0,2,1:T(4,128)S(1)}, u32[]{:S(2)}, u32[]{:S(2)}) collective-permute-start(f32[4,12,1,512]{3,0,2,1:T(4,128)S(1)} %get-tuple-element.85), channel_id=1, source_target_pairs={{2,0},{4,2},{6,4},{8,6},{10,8},{12,10},{14,12},{16,14},{18,16},{20... | collective-permute-start | bytes 294920 | tf_op jit(solution)/shard_map/ppermute | solution.py:18
  101.0 8.2 %collective-permute-start.4 = (f32[4,12,1,512]{3,0,2,1:T(4,128)S(1)}, f32[4,12,1,512]{3,0,2,1:T(4,128)S(1)}, u32[]{:S(2)}, u32[]{:S(2)}) collective-permute-start(f32[4,12,1,512]{3,0,2,1:T(4,128)S(1)} %get-tuple-element.86), channel_id=1, source_target_pairs={{0,2},{2,4},{4,6},{6,8},{8,10},{10,12},{12,14},{14,16},{16,18},{18... | collective-permute-start | bytes 294920 | tf_op jit(solution)/shard_map/ppermute | solution.py:15
where the time goes:
time: 112 us; the launch traced here: 111 us
  waiting for transfers between devices  35 us (31%)
  starting transfers between devices  27.3 us (24%)
  blocking collectives  20.1 us (18%)
  other arithmetic  14.9 us (13%)
  local copies, waits for them, and re-layouts  13.6 us (12%)
    all_to_all x2, blocking collectives, per_device(): lax.all_to_all(adjoint, 'band', split_axis=2, concat_axis=1, tiled=True)  8.94 us
    all_to_all x2, blocking collectives, per_device(): lax.all_to_all(jnp.stack(solved_columns, axis=1), 'band', split_axis=1, c...  8.73 us
    all_to_all x1, waiting for transfers between devices, per_device(): lax.all_to_all(sounding_precision, 'tile', split_axis=0, concat_axis=0, t...  7.19 us
    all_to_all x1, waiting for transfers between devices, per_device(): lax.all_to_all(sounding_value, 'tile', split_axis=0, concat_axis=0, tiled...  7.12 us
    ppermute x2, waiting for transfers between devices, with_halo(): lax.ppermute(lax.slice_in_dim(block, 0, width, axis=dim), axis, backward)  6.68 us
    ppermute x2, waiting for transfers between devices, with_halo(): lax.ppermute(lax.slice_in_dim(block, block.shape[dim] - width, None, axis...  6.45 us
    all_to_all x1, starting transfers between devices, per_device(): lax.all_to_all(cell_float, 'tile', split_axis=0, concat_axis=0, tiled=True)  5.94 us
    all_to_all x1, waiting for transfers between devices, per_device(): lax.all_to_all(sounding_weight, 'tile', split_axis=0, concat_axis=0, tile...  4.39 us
  transfers between devices with their start and end apart: 10, of which 9 were waited for; matrix products, arithmetic and copies ran while one was open for 17% of the time, Pallas kernels for 0%

commit v1 on v0

v1 whole, which is shorter than its diff:
```python
import functools

import jax
import jax.numpy as jnp
from jax import lax
from jax.experimental import pallas as pl
from jax.experimental.pallas import tpu as pltpu
from jax.sharding import PartitionSpec as P


LANES = 128
PAIR = 32
HALF = 16
MIB = 1 << 20


def where_am_i():
    return lax.axis_index("band")


def sublane(shape):
    return lax.broadcasted_iota(jnp.int32, shape, len(shape) - 2)


def lane(shape):
    return lax.broadcasted_iota(jnp.int32, shape, len(shape) - 1)


def packed_rows(members, base):
    place = sublane(members[0].shape)
    out = members[0]
    for q in range(1, 4):
        pick = (((place + 2 * q) & 7) >> 1) == (base >> 1)
        out = jnp.where(pick, pltpu.roll(members[q], 8 - 2 * q, 0), out)
    return out


def unpacked_rows(packed, q):
    return packed if q == 0 else pltpu.roll(packed, 2 * q, 0)


def pack_kernel(
    conc,
    adj,
    east,
    north,
    diff,
    cell,
    value,
    precision,
    weight,
    coef,
    coef_one,
    coef_two,
    adj_one,
    adj_two,
    message,
    fields,
):
    tracers, levels, cols, rows = conc.shape
    blocks = cell.shape[0]
    for h in range(3):
        for j in range(blocks):
            fields[h, j, 0:4, :] = weight[4 * h : 4 * h + 4, LANES * j : LANES * (j + 1)]
    for j in range(blocks):
        fields[3, j, 0:1, :] = cell[j : j + 1, :].astype(jnp.float32)
        fields[3, j, 1:2, :] = value[j : j + 1, :]
        fields[3, j, 2:3, :] = precision[j : j + 1, :]
        fields[3, j, 3:4, :] = jnp.zeros((1, LANES), jnp.float32)
    at = lane((4, LANES))
    for h in range(4):
        for j in range(blocks):
            near = pltpu.roll(fields[h, j, 0:4, :], LANES - HALF, 1)
            after = pltpu.roll(fields[h, (j + 1) % blocks, 0:4, :], LANES - HALF, 1)
            fields[h, j, 4:8, :] = jnp.where(at < LANES - HALF, near, after)
    at = lane((8, LANES))
    place = sublane((8, LANES))
    edge = jnp.where(place < 4, float((cols - 2) * rows), float(2 * rows))
    is_cell = ((place & 3) == 0) & (at >= 96)
    for t in range(message.shape[0]):
        j, i = t // 8, t % 8
        parts = []
        for h in range(4):
            if i:
                part = pltpu.roll(fields[h, j], (32 * h - HALF * (i - 1)) % LANES, 1)
            else:
                turn = (32 * h + HALF) % LANES
                before = pltpu.roll(fields[h, (j - 1) % blocks], turn, 1)
                here = pltpu.roll(fields[h, j], turn, 1)
                part = jnp.where((at & 31) < HALF, before, here)
            parts.append(part)
        both = jnp.where(
            at < 64,
            jnp.where(at < 32, parts[0], parts[1]),
            jnp.where(at < 96, parts[2], parts[3]),
        )
        drop = ((at < 112) & (both < edge)) | ((at >= 112) & (both >= edge))
        message[t] = jnp.where(drop & is_cell, -1.0, both)

    band = where_am_i()
    one = jnp.where(band == 0, cols - 2, 0)
    two = jnp.where(band == 0, 0, cols - 2)

    def level(at_level, carry):
        total = conc[0, at_level]
        for tr in range(1, tracers):
            total = total + conc[tr, at_level]
        members = [total, diff[at_level], east[at_level], north[at_level]]
        for q in range(4):
            coef[q, at_level] = members[q]
        coef_one[at_level] = packed_rows(members, one)
        coef_two[at_level] = packed_rows(members, two)
        members = [adj[tr, at_level] for tr in range(tracers)]
        adj_one[at_level] = packed_rows(members, one)
        adj_two[at_level] = packed_rows(members, two)
        return carry

    lax.fori_loop(0, levels, level, 0, unroll=2)


def three_parts(x):
    first = x.astype(jnp.bfloat16)
    rest = x - first.astype(jnp.float32)
    second = rest.astype(jnp.bfloat16)
    third = (rest - second.astype(jnp.float32)).astype(jnp.bfloat16)
    return first, second, third


def exact_dot(x, onehot, dims):
    out = None
    for part in three_parts(x):
        term = lax.dot_general(part, onehot, (dims, ((), ())), preferred_element_type=jnp.float32)
        out = term if out is None else out + term
    return out


def prepare_kernel(
    factor,
    coef_own,
    coef_other,
    edge_own,
    edge_other,
    slots,
    forcing,
    centre,
    east_part,
    west_part,
    north_part,
    south_part,
    inverse,
    lower,
    ratio,
    total,
    diff,
):
    _, band_levels, cols, rows = coef_own.shape
    levels = 2 * band_levels
    tracers = inverse.shape[0]
    band = where_am_i()
    place = sublane((cols, rows))
    at = lane((cols, rows))
    outside = (place >> 1) == jnp.where(band == 0, (cols - 2) >> 1, 0)

    def assemble(coef, edge, first):
        def level(j, carry):
            packed = edge[j]
            t, d, e, n = [
                jnp.where(outside, unpacked_rows(packed, q), coef[q, j]) for q in range(4)
            ]
            n = jnp.where(at == rows - 1, 0.0, n)
            to_east = jnp.maximum(e, 0.0)
            to_west = jnp.minimum(pltpu.roll(e, 1, 0), 0.0)
            to_north = jnp.maximum(n, 0.0)
            to_south = jnp.minimum(pltpu.roll(n, 1, 1), 0.0)
            g = first + j
            total[g] = t
            diff[g] = d
            east_part[g] = to_east
            west_part[g] = -to_west
            north_part[g] = to_north
            south_part[g] = -to_south
            centre[g] = ((1.0 - to_east) + to_west) + (to_south - to_north)
            return carry

        lax.fori_loop(0, band_levels, level, 0, unroll=2)

    assemble(coef_own, edge_own, band * band_levels)
    assemble(coef_other, edge_other, (1 - band) * band_levels)

    zero = jnp.zeros((cols, rows), jnp.float32)

    def factorise(g, carry):
        d = jnp.where(g < levels - 1, diff[g], 0.0)
        out = []
        for tr in range(tracers):
            above, before = carry[tr]
            kappa = factor[tr] * d
            inv = 1.0 / (((1.0 + above) + kappa) - above * before)
            now = kappa * inv
            inverse[tr, g] = inv
            lower[tr, g] = above * inv
            ratio[tr, g] = now
            out.append((kappa, now))
        return tuple(out)

    lax.fori_loop(0, levels, factorise, tuple((zero, zero) for _ in range(tracers)))

    sources = slots.shape[0]
    chunk = min(16, sources)
    wide = chunk * PAIR
    block_at = lane((8, LANES)) >> 5

    def gathered(first, h):
        pieces = []
        for v in range(chunk // 4):
            out = None
            for i in range(4):
                part = slots[first + 4 * v + i]
                turn = (32 * (i - h)) % LANES
                part = pltpu.roll(part, turn, 1) if turn else part
                out = part if out is None else jnp.where(block_at == i, part, out)
            pieces.append(out)
        return jnp.concatenate(pieces, axis=1)

    def soundings(c):
        fields = [gathered(c * chunk, h) for h in range(4)]
        cell = fields[3][0:1].astype(jnp.int32)
        value = fields[3][1:2]
        precision = fields[3][2:3]
        y = cell & (rows - 1)
        x = lax.shift_right_arithmetic(cell, rows.bit_length() - 1)
        onehot = jnp.where(sublane((rows, wide)) == y, 1.0, 0.0).astype(jnp.bfloat16)
        on_column = jnp.where(sublane((cols, wide)) == x, 1.0, 0.0)
        weights = []
        for g in range(levels):
            side, l = g // band_levels, g % band_levels
            weights.append(fields[l // 4][4 * side + l % 4 : 4 * side + l % 4 + 1])
        picked = exact_dot(total[...].reshape(levels * cols, rows), onehot, ((1,), (0,)))
        mean = weights[0] * picked[0:cols]
        for g in range(1, levels):
            mean = mean + weights[g] * picked[g * cols : (g + 1) * cols]
        mean = jnp.sum(mean * on_column, axis=0, keepdims=True)
        misfit = (precision * (mean - value)) * on_column
        spread = jnp.concatenate([weights[g] * misfit for g in range(levels)], axis=0)
        added = exact_dot(spread, onehot, ((1,), (1,)))
        return added.reshape(levels, cols, rows)

    forcing[...] = soundings(0)
    if sources > chunk:

        def more(c, carry):
            forcing[...] += soundings(c)
            return carry

        lax.fori_loop(1, sources // chunk, more, 0)


def solve_kernel(
    adj_own,
    adj_other,
    edge_own,
    edge_other,
    forcing,
    centre,
    east_part,
    west_part,
    north_part,
    south_part,
    inverse,
    lower,
    ratio,
    kept,
    sent,
    state,
):
    tracers, band_levels, cols, rows = adj_own.shape
    levels = 2 * band_levels
    band = where_am_i()
    place = sublane((cols, rows))
    outside = (place >> 1) == jnp.where(band == 0, (cols - 2) >> 1, 0)
    zeros = tuple(jnp.zeros((cols, rows), jnp.float32) for _ in range(tracers))

    def first_sweep(adj, edge, first, carry):
        def level(j, carry):
            g = first + j
            packed = edge[j]
            force = forcing[g]
            out = []
            for tr in range(tracers):
                a = jnp.where(outside, unpacked_rows(packed, tr), adj[tr, j]) + force
                now = a * inverse[tr, g] + lower[tr, g] * carry[tr]
                state[tr, g] = now
                out.append(now)
            return tuple(out)

        return lax.fori_loop(0, band_levels, level, carry, unroll=2)

    @pl.when(band == 0)
    def _():
        carry = first_sweep(adj_own, edge_own, 0, zeros)
        first_sweep(adj_other, edge_other, band_levels, carry)

    @pl.when(band != 0)
    def _():
        carry = first_sweep(adj_other, edge_other, 0, zeros)
        first_sweep(adj_own, edge_own, band_levels, carry)

    def back_and_advect():
        def level(i, carry):
            g = levels - 1 - i
            mid, e, w, n, s = centre[g], east_part[g], west_part[g], north_part[g], south_part[g]
            out = []
            for tr in range(tracers):
                a = state[tr, g] + ratio[tr, g] * carry[tr]
                out.append(a)
                along = e * pltpu.roll(a, cols - 1, 0) + w * pltpu.roll(a, 1, 0)
                across = n * pltpu.roll(a, rows - 1, 1) + s * pltpu.roll(a, 1, 1)
                state[tr, g] = mid * a + (along + across)
            return tuple(out)

        lax.fori_loop(0, levels, level, zeros)

    def forward():
        def level(g, carry):
            out = []
            for tr in range(tracers):
                now = state[tr, g] * inverse[tr, g] + lower[tr, g] * carry[tr]
                state[tr, g] = now
                out.append(now)
            return tuple(out)

        lax.fori_loop(0, levels, level, zeros, unroll=2)

    back_and_advect()
    forward()
    back_and_advect()

    half = band_levels // 2
    mine = (place >> 2) == band
    own_first = band * band_levels
    other_first = (1 - band) * band_levels

    def hand_out(j, carry):
        for tr in range(tracers):
            kept[tr, j] = state[tr, own_first + j]
            kept[tr, j + half] = state[tr, own_first + j + half]
            sent[tr, j] = jnp.where(
                mine,
                state[tr, other_first + j],
                pltpu.roll(state[tr, other_first + j + half], 4, 0),
            )
        return carry

    lax.fori_loop(0, half, hand_out, 0)


def join_kernel(kept, received, out):
    tracers, band_levels, cols, rows = kept.shape
    half = band_levels // 2
    mine = (sublane((cols, rows)) >> 2) == where_am_i()

    def level(j, carry):
        for tr in range(tracers):
            got = received[tr, j]
            out[tr, j] = jnp.where(mine, kept[tr, j], got)
            out[tr, j + half] = jnp.where(mine, kept[tr, j + half], pltpu.roll(got, 4, 0))
        return carry

    lax.fori_loop(0, half, level, 0)


def f32(*shape):
    return jax.ShapeDtypeStruct(shape, jnp.float32)


def call(kernel, outs, scratch, ops, limit, smem=0):
    vmem = pl.BlockSpec(memory_space=pltpu.VMEM)
    scalars = pl.BlockSpec(memory_space=pltpu.SMEM)

    def run(*args):
        moved = sum(4 * a.size for a in args) + sum(4 * o.size for o in outs)
        return pl.pallas_call(
            kernel,
            out_shape=outs,
            in_specs=[scalars] * smem + [vmem] * (len(args) - smem),
            out_specs=[vmem] * len(outs),
            scratch_shapes=scratch,
            compiler_params=pltpu.CompilerParams(vmem_limit_bytes=limit * MIB),
            cost_estimate=pl.CostEstimate(flops=ops, bytes_accessed=moved, transcendentals=0),
        )(*args)

    return run


def per_device(
    tiles,
    concentration,
    adjoint_later,
    courant_east,
    courant_north,
    diffusivity,
    tracer_factor,
    sounding_cell,
    sounding_value,
    sounding_precision,
    sounding_weight,
):
    tracers, band_levels, cols, rows = concentration.shape
    levels = 2 * band_levels
    blocks = sounding_cell.shape[0] // LANES
    field = f32(band_levels, cols, rows)
    deep = f32(levels, cols, rows)
    full = f32(tracers, levels, cols, rows)

    coef, coef_one, coef_two, adj_one, adj_two, message = call(
        pack_kernel,
        [f32(4, band_levels, cols, rows)] + [field] * 4 + [f32(tiles, 8, LANES)],
        [pltpu.VMEM((4, blocks, 8, LANES), jnp.float32)],
        10**6,
        16,
    )(
        concentration,
        adjoint_later,
        courant_east,
        courant_north,
        diffusivity,
        sounding_cell.reshape(blocks, LANES),
        sounding_value.reshape(blocks, LANES),
        sounding_precision.reshape(blocks, LANES),
        sounding_weight.T,
    )

    both = ("tile", "band")
    same = [(2 * t, 2 * ((t + 1) % tiles)) for t in range(tiles)]
    same += [(2 * t + 1, 2 * ((t - 1) % tiles) + 1) for t in range(tiles)]
    cross = [(2 * t + 1, 2 * ((t + 1) % tiles)) for t in range(tiles)]
    cross += [(2 * t, 2 * ((t - 1) % tiles) + 1) for t in range(tiles)]
    swap = [(0, 1), (1, 0)]

    coef_edge_own = lax.ppermute(coef_one, both, same)
    coef_edge_other = lax.ppermute(coef_two, both, cross)
    coef_other = lax.ppermute(coef, "band", swap)
    slots = lax.all_to_all(
        message.reshape(2 * tiles, 4, LANES), both, split_axis=0, concat_axis=0, tiled=True
    ).reshape(tiles, 8, LANES)
    adj_other = lax.ppermute(adjoint_later, "band", swap)
    adj_edge_own = lax.ppermute(adj_one, both, same)
    adj_edge_other = lax.ppermute(adj_two, both, cross)

    ready = call(
        prepare_kernel,
        [deep] * 6 + [full] * 3,
        [pltpu.VMEM((levels, cols, rows), jnp.float32)] * 2,
        10**8,
        32,
        smem=1,
    )(tracer_factor, coef, coef_other, coef_edge_own, coef_edge_other, slots)

    kept, sent = call(
        solve_kernel,
        [f32(tracers, band_levels, cols, rows), f32(tracers, band_levels // 2, cols, rows)],
        [pltpu.VMEM((tracers, levels, cols, rows), jnp.float32)],
        10**7,
        24,
    )(adjoint_later, adj_other, adj_edge_own, adj_edge_other, *ready)
    received = lax.ppermute(sent, "band", swap)
    return call(join_kernel, [f32(tracers, band_levels, cols, rows)], [], 10**5, 8)(kept, received)[0]


def solution(mesh):
    return jax.shard_map(
        functools.partial(per_device, mesh.shape["tile"]),
        mesh=mesh,
        in_specs=(
            P(None, "band", "tile", None),
            P(None, "band", "tile", None),
            P("band", "tile", None),
            P("band", "tile", None),
            P("band", "tile", None),
            P(),
            P("tile"),
            P("tile"),
            P("tile"),
            P("tile", "band"),
        ),
        out_specs=P(None, "band", "tile", None),
        check_vma=False,
    )
```

time: 112 us -> 49.8 us (0.44)
  waiting for transfers between devices: 35 us -> 6.68 us
  starting transfers between devices: 27.3 us -> 11.8 us
  other arithmetic: 14.9 us -> 0 us
  Pallas kernels: 0 us -> 13.2 us
  blocking collectives: 20.1 us -> 10.9 us
  local copies, waits for them, and re-layouts: 13.6 us -> 6.68 us
    all_to_all x5 -> x0, waiting for transfers between devices: 21.9 us -> none  [the longest x1 7.19 us: per_device(): lax.all_to_all(sounding_precision, 'tile', split_axis=0, concat_axis=0, t...]
    all_to_all x5 -> x0, starting transfers between devices: 20.2 us -> none  [the longest x1 5.94 us: per_device(): lax.all_to_all(cell_float, 'tile', split_axis=0, concat_axis=0, tiled=True)]
    pallas_call x0 -> x4, Pallas kernels: none -> 13.2 us  [run(): pl.pallas_call(kernel, out_shape=outs, in_specs=[scalars] * smem + [vmem]...]
    all_to_all x4 -> x1, blocking collectives: 17.7 us -> 10.9 us  [per_device(): lax.all_to_all(message.reshape(2 * tiles, 4, LANES), both, split_axis=0,...]
    ppermute x5 -> x7, waiting for transfers between devices: 13.1 us -> 6.68 us  [the longest x1 5.06 us: per_device(): coef_edge_own = lax.ppermute(coef_one, both, same)]
    all_to_all x13 -> x0, local copies, waits for them, and re-layouts: 5.12 us -> none  [the longest x3 1.28 us: per_device(): lax.all_to_all(sounding_precision, 'tile', split_axis=0, concat_axis=0, t...]
    ppermute x5 -> x7, starting transfers between devices: 7.16 us -> 11.8 us  [the longest x1 3.93 us: per_device(): coef_edge_other = lax.ppermute(coef_two, both, cross)]
    add x3 -> x0, other arithmetic: 3.91 us -> none  [the longest x2 2.27 us: advect_sides(): adjoint + jnp.maximum(east_face, 0.0) * (east_side - adjoint)]
  transfers between devices with their start and end apart: 10 -> 7, of which waited for: 9 -> 2; matrix products, arithmetic and copies ran while one was open for 17% -> 0% of each run, Pallas kernels for 0% -> 7%
where the time goes in v1:
time: 49.8 us; the launch traced here: 49.3 us
  Pallas kernels  13.2 us (27%)
  starting transfers between devices  11.8 us (24%)
  blocking collectives  10.9 us (22%)
  local copies, waits for them, and re-layouts  6.68 us (13%)
  waiting for transfers between devices  6.68 us (13%)
    pallas_call x4, Pallas kernels, run(): pl.pallas_call(kernel, out_shape=outs, in_specs=[scalars] * smem + [vmem]...  13.2 us
    all_to_all x1, blocking collectives, per_device(): lax.all_to_all(message.reshape(2 * tiles, 4, LANES), both, split_axis=0,...  10.9 us
    unnamed x18, local copies, waits for them, and re-layouts  6.68 us
    ppermute x1, waiting for transfers between devices, per_device(): coef_edge_own = lax.ppermute(coef_one, both, same)  5.06 us
    ppermute x1, starting transfers between devices, per_device(): coef_edge_other = lax.ppermute(coef_two, both, cross)  3.93 us
    ppermute x1, starting transfers between devices, per_device(): coef_edge_own = lax.ppermute(coef_one, both, same)  2.92 us
    ppermute x1, starting transfers between devices, per_device(): adj_edge_other = lax.ppermute(adj_two, both, cross)  2.71 us
    ppermute x1, waiting for transfers between devices, per_device(): received = lax.ppermute(sent, 'band', swap)  1.6 us
  transfers between devices with their start and end apart: 7, of which 2 were waited for; matrix products, arithmetic and copies ran while one was open for 0% of the time, Pallas kernels for 7%

profile of v1, /device:TPU:0, one launch (start us, length us, event | category | flops | bytes accessed | tf_op | source)
XLA Modules:
  0.0 49.3 jit_solution(17340300385287023763)
XLA Ops:
  0.0 1.1 %copy-done = f32[4,12,8,512]{3,2,1,0:T(8,128)S(1)} copy-done((f32[4,12,8,512]{3,2,1,0:T(8,128)S(1)}, f32[4,12,8,512]{3,2,1,0:T(8,128)}, u32[]{:S(2)}) %copy-start) | copy-done | bytes 786456
  1.2 0.9 %copy-done.1 = f32[12,8,512]{2,1,0:T(8,128)S(1)} copy-done((f32[12,8,512]{2,1,0:T(8,128)S(1)}, f32[12,8,512]{2,1,0:T(8,128)}, u32[]{:S(2)}) %copy-start.1) | copy-done | bytes 196632
  2.1 0.9 %copy-done.2 = f32[12,8,512]{2,1,0:T(8,128)S(1)} copy-done((f32[12,8,512]{2,1,0:T(8,128)S(1)}, f32[12,8,512]{2,1,0:T(8,128)}, u32[]{:S(2)}) %copy-start.2) | copy-done | bytes 196632
  3.0 0.9 %copy-done.3 = f32[12,8,512]{2,1,0:T(8,128)S(1)} copy-done((f32[12,8,512]{2,1,0:T(8,128)S(1)}, f32[12,8,512]{2,1,0:T(8,128)}, u32[]{:S(2)}) %copy-start.3) | copy-done | bytes 196632
  3.9 0.7 %copy-done.4 = f32[256,12]{0,1:T(8,128)S(1)} copy-done((f32[256,12]{0,1:T(8,128)S(1)}, f32[256,12]{0,1:T(8,128)}, u32[]{:S(2)}) %copy-start.4) | copy-done | bytes 12312
  4.7 0.7 %copy-done.5 = s32[256]{0:T(256)S(1)} copy-done((s32[256]{0:T(256)S(1)}, s32[256]{0:T(256)}, u32[]{:S(2)}) %copy-start.5) | copy-done | bytes 1048
  5.3 0.7 %copy-done.6 = f32[256]{0:T(256)S(1)} copy-done((f32[256]{0:T(256)S(1)}, f32[256]{0:T(256)}, u32[]{:S(2)}) %copy-start.6) | copy-done | bytes 1048
  6.0 0.7 %copy-done.7 = f32[256]{0:T(256)S(1)} copy-done((f32[256]{0:T(256)S(1)}, f32[256]{0:T(256)}, u32[]{:S(2)}) %copy-start.7) | copy-done | bytes 1048
  6.7 1.5 %shard_map.100 = (f32[4,12,8,512]{3,2,1,0:T(8,128)S(1)}, f32[12,8,512]{2,1,0:T(8,128)S(1)}, f32[12,8,512]{2,1,0:T(8,128)S(1)}, f32[12,8,512]{2,1,0:T(8,128)S(1)}...) custom-call(f32[4,12,8,512]{3,2,1,0:T(8,128)S(1)} %copy-done, f32[4,12,8,512]{3,2,1,0:T(8,128)} %adj_own.1, ...), custom_call_target="tpu_custom_call" | custom-call | flops 1000000 | bytes 3816448 | tf_op jit(solution)/shard_map/pallas_call | solution.py:382
  8.2 0.5 %collective-permute-start.3 = (f32[4,12,8,512]{3,2,1,0:T(8,128)S(1)}, f32[4,12,8,512]{3,2,1,0:T(8,128)S(1)}, u32[]{:S(2)}, u32[]{:S(2)}) collective-permute-start(f32[4,12,8,512]{3,2,1,0:T(8,128)S(1)} %get-tuple-element.24.coef_own), channel_id=1, source_target_pairs={{0,1},{1,0},{2,3},{3,2},{4,5},{5,4},{6,7},{7,6},{8,9},{9,8},{10,11... | collective-permute-start | bytes 2359304 | tf_op jit(solution)/shard_map/ppermute | solution.py:442
  8.7 0.1 collective-permute-start
  8.8 2.9 %collective-permute-start.4 = (f32[12,8,512]{2,1,0:T(8,128)S(1)}, f32[12,8,512]{2,1,0:T(8,128)S(1)}, u32[]{:S(2)}, u32[]{:S(2)}) collective-permute-start(f32[12,8,512]{2,1,0:T(8,128)S(1)} %get-tuple-element.25), channel_id=1, source_target_pairs={{0,2},{2,4},{4,6},{6,8},{8,10},{10,12},{12,14},{14,16},{16,18},{18... | collective-permute-start | bytes 589832 | tf_op jit(solution)/shard_map/ppermute | solution.py:440
  11.7 3.9 %collective-permute-start.5 = (f32[12,8,512]{2,1,0:T(8,128)S(1)}, f32[12,8,512]{2,1,0:T(8,128)S(1)}, u32[]{:S(2)}, u32[]{:S(2)}) collective-permute-start(f32[12,8,512]{2,1,0:T(8,128)S(1)} %get-tuple-element.26), channel_id=1, source_target_pairs={{1,2},{3,4},{5,6},{7,8},{9,10},{11,12},{13,14},{15,16},{17,18},{19... | collective-permute-start | bytes 589832 | tf_op jit(solution)/shard_map/ppermute | solution.py:441
  15.7 1.5 %collective-permute-start.1 = (f32[12,8,512]{2,1,0:T(8,128)S(1)}, f32[12,8,512]{2,1,0:T(8,128)S(1)}, u32[]{:S(2)}, u32[]{:S(2)}) collective-permute-start(f32[12,8,512]{2,1,0:T(8,128)S(1)} %get-tuple-element.22), channel_id=1, source_target_pairs={{0,2},{2,4},{4,6},{6,8},{8,10},{10,12},{12,14},{14,16},{16,18},{18... | collective-permute-start | bytes 589832 | tf_op jit(solution)/shard_map/ppermute | solution.py:447
  17.2 5.1 %collective-permute-done.4.edge_own = f32[12,8,512]{2,1,0:T(8,128)S(1)} collective-permute-done((f32[12,8,512]{2,1,0:T(8,128)S(1)}, f32[12,8,512]{2,1,0:T(8,128)S(1)}, u32[]{:S(2)}, u32[]{:S(2)}) %collective-permute-start.4) | collective-permute-done | bytes 196640 | tf_op jit(solution)/shard_map/ppermute | solution.py:440
  22.2 2.7 %collective-permute-start.2 = (f32[12,8,512]{2,1,0:T(8,128)S(1)}, f32[12,8,512]{2,1,0:T(8,128)S(1)}, u32[]{:S(2)}, u32[]{:S(2)}) collective-permute-start(f32[12,8,512]{2,1,0:T(8,128)S(1)} %get-tuple-element.23), channel_id=1, source_target_pairs={{1,2},{3,4},{5,6},{7,8},{9,10},{11,12},{13,14},{15,16},{17,18},{19... | collective-permute-start | bytes 589832 | tf_op jit(solution)/shard_map/ppermute | solution.py:448
  24.9 10.9 %all_to_all.5 = f32[32,4,128]{2,1,0:T(4,128)S(1)} all-to-all(f32[32,4,128]{2,1,0:T(4,128)S(1)} %bitcast.7), channel_id=1, replica_groups=mesh['tile'=16,'band'=2] {'tile','band'}, dimensions={0} | all-to-all | bytes 131072 | tf_op jit(solution)/shard_map/all_to_all | solution.py:443
  35.8 3.5 %shard_map.101 = (f32[24,8,512]{2,1,0:T(8,128)S(1)}, f32[24,8,512]{2,1,0:T(8,128)S(1)}, f32[24,8,512]{2,1,0:T(8,128)S(1)}, f32[24,8,512]{2,1,0:T(8,128)S(1)}, f3...) custom-call(f32[4]{0:T(128)S(1)} %copy-done.8, ...), custom_call_target="tpu_custom_call" | custom-call | flops 100000000 | bytes 9109520 | tf_op jit(solution)/shard_map/pallas_call | solution.py:382
  39.3 0.0 collective-permute-done.2.edge_other
  39.3 0.0 collective-permute-done.adj_other
  39.3 7.3 %shard_map.102 = (f32[4,12,8,512]{3,2,1,0:T(8,128)S(1)}, f32[4,6,8,512]{3,2,1,0:T(8,128)S(1)}) custom-call(f32[4,12,8,512]{3,2,1,0:T(8,128)} %adj_own.1, f32[4,12,8,512]{3,2,1,0:T(8,128)S(1)} %collective-permute-done.adj_other, f32[12,8,512]{2,1,0:T(8,128)S(1)} %collective-permute-done.1.edge_own, f32[12,8,512]{2,1,0:T(8,128)S(1)} %collective-permute-done.2.edge_other, ...), custom_call_target="tpu_custom_call" | custom-call | flops 10000000 | bytes 10223616 | tf_op jit(solution)/shard_map/pallas_call | solution.py:382
  46.6 0.2 collective-permute-start.6
  46.8 1.6 %collective-permute-done.6.received = f32[4,6,8,512]{3,2,1,0:T(8,128)S(1)} collective-permute-done((f32[4,6,8,512]{3,2,1,0:T(8,128)S(1)}, f32[4,6,8,512]{3,2,1,0:T(8,128)S(1)}, u32[]{:S(2)}, u32[]{:S(2)}) %collective-permute-start.6) | collective-permute-done | bytes 393248 | tf_op jit(solution)/shard_map/ppermute | solution.py:466
  48.4 1.0 %shard_map.103 = f32[4,12,8,512]{3,2,1,0:T(8,128)} custom-call(f32[4,12,8,512]{3,2,1,0:T(8,128)S(1)} %get-tuple-element.37.kept, f32[4,6,8,512]{3,2,1,0:T(8,128)S(1)} %collective-permute-done.6.received), custom_call_target="tpu_custom_call" | custom-call | flops 100000 | bytes 1966080 | tf_op jit(solution)/shard_map/pallas_call | solution.py:382
  (13 shorter events, 0.0 us)
Async XLA Ops:
  0.0 35.8 %copy-start.8 = (f32[4]{0:T(128)S(1)}, f32[4]{0:T(128)}, u32[]{:S(2)}) copy-start(f32[4]{0:T(128)} %factor.1) | copy-start | bytes 52
  0.0 1.1 %copy-start = (f32[4,12,8,512]{3,2,1,0:T(8,128)S(1)}, f32[4,12,8,512]{3,2,1,0:T(8,128)}, u32[]{:S(2)}) copy-start(f32[4,12,8,512]{3,2,1,0:T(8,128)} %conc.1) | copy-start | bytes 2359300
  1.1 0.9 %copy-start.1 = (f32[12,8,512]{2,1,0:T(8,128)S(1)}, f32[12,8,512]{2,1,0:T(8,128)}, u32[]{:S(2)}) copy-start(f32[12,8,512]{2,1,0:T(8,128)} %east.1) | copy-start | bytes 589828
  2.1 0.9 %copy-start.2 = (f32[12,8,512]{2,1,0:T(8,128)S(1)}, f32[12,8,512]{2,1,0:T(8,128)}, u32[]{:S(2)}) copy-start(f32[12,8,512]{2,1,0:T(8,128)} %north.1) | copy-start | bytes 589828
  3.0 0.9 %copy-start.3 = (f32[12,8,512]{2,1,0:T(8,128)S(1)}, f32[12,8,512]{2,1,0:T(8,128)}, u32[]{:S(2)}) copy-start(f32[12,8,512]{2,1,0:T(8,128)} %diff.1) | copy-start | bytes 589828
  3.9 0.7 %copy-start.4 = (f32[256,12]{0,1:T(8,128)S(1)}, f32[256,12]{0,1:T(8,128)}, u32[]{:S(2)}) copy-start(f32[256,12]{0,1:T(8,128)} %param.19) | copy-start | bytes 36868
  4.7 0.7 %copy-start.5 = (s32[256]{0:T(256)S(1)}, s32[256]{0:T(256)}, u32[]{:S(2)}) copy-start(s32[256]{0:T(256)} %param.16) | copy-start | bytes 3076
  5.3 0.7 %copy-start.6 = (f32[256]{0:T(256)S(1)}, f32[256]{0:T(256)}, u32[]{:S(2)}) copy-start(f32[256]{0:T(256)} %param.17) | copy-start | bytes 3076
  6.0 0.7 %copy-start.7 = (f32[256]{0:T(256)S(1)}, f32[256]{0:T(256)}, u32[]{:S(2)}) copy-start(f32[256]{0:T(256)} %param.18) | copy-start | bytes 3076
  8.2 27.6 %collective-permute-start.3 = (f32[4,12,8,512]{3,2,1,0:T(8,128)S(1)}, f32[4,12,8,512]{3,2,1,0:T(8,128)S(1)}, u32[]{:S(2)}, u32[]{:S(2)}) collective-permute-start(f32[4,12,8,512]{3,2,1,0:T(8,128)S(1)} %get-tuple-element.24.coef_own), channel_id=1, source_target_pairs={{0,1},{1,0},{2,3},{3,2},{4,5},{5,4},{6,7},{7,6},{8,9},{9,8},{10,11... | collective-permute-start | bytes 2359304 | tf_op jit(solution)/shard_map/ppermute | solution.py:442
  8.7 30.6 %collective-permute-start = (f32[4,12,8,512]{3,2,1,0:T(8,128)}, f32[4,12,8,512]{3,2,1,0:T(8,128)S(1)}, u32[]{:S(2)}, u32[]{:S(2)}) collective-permute-start(f32[4,12,8,512]{3,2,1,0:T(8,128)} %adj_own.1), channel_id=1, source_target_pairs={{0,1},{1,0},{2,3},{3,2},{4,5},{5,4},{6,7},{7,6},{8,9},{9,8},{10,11... | collective-permute-start | bytes 2359304 | tf_op jit(solution)/shard_map/ppermute | solution.py:446
  8.8 13.4 %collective-permute-start.4 = (f32[12,8,512]{2,1,0:T(8,128)S(1)}, f32[12,8,512]{2,1,0:T(8,128)S(1)}, u32[]{:S(2)}, u32[]{:S(2)}) collective-permute-start(f32[12,8,512]{2,1,0:T(8,128)S(1)} %get-tuple-element.25), channel_id=1, source_target_pairs={{0,2},{2,4},{4,6},{6,8},{8,10},{10,12},{12,14},{14,16},{16,18},{18... | collective-permute-start | bytes 589832 | tf_op jit(solution)/shard_map/ppermute | solution.py:440
  11.7 24.1 %collective-permute-start.5 = (f32[12,8,512]{2,1,0:T(8,128)S(1)}, f32[12,8,512]{2,1,0:T(8,128)S(1)}, u32[]{:S(2)}, u32[]{:S(2)}) collective-permute-start(f32[12,8,512]{2,1,0:T(8,128)S(1)} %get-tuple-element.26), channel_id=1, source_target_pairs={{1,2},{3,4},{5,6},{7,8},{9,10},{11,12},{13,14},{15,16},{17,18},{19... | collective-permute-start | bytes 589832 | tf_op jit(solution)/shard_map/ppermute | solution.py:441
  15.7 23.6 %collective-permute-start.1 = (f32[12,8,512]{2,1,0:T(8,128)S(1)}, f32[12,8,512]{2,1,0:T(8,128)S(1)}, u32[]{:S(2)}, u32[]{:S(2)}) collective-permute-start(f32[12,8,512]{2,1,0:T(8,128)S(1)} %get-tuple-element.22), channel_id=1, source_target_pairs={{0,2},{2,4},{4,6},{6,8},{8,10},{10,12},{12,14},{14,16},{16,18},{18... | collective-permute-start | bytes 589832 | tf_op jit(solution)/shard_map/ppermute | solution.py:447
  22.2 17.1 %collective-permute-start.2 = (f32[12,8,512]{2,1,0:T(8,128)S(1)}, f32[12,8,512]{2,1,0:T(8,128)S(1)}, u32[]{:S(2)}, u32[]{:S(2)}) collective-permute-start(f32[12,8,512]{2,1,0:T(8,128)S(1)} %get-tuple-element.23), channel_id=1, source_target_pairs={{1,2},{3,4},{5,6},{7,8},{9,10},{11,12},{13,14},{15,16},{17,18},{19... | collective-permute-start | bytes 589832 | tf_op jit(solution)/shard_map/ppermute | solution.py:448
  46.6 1.8 %collective-permute-start.6 = (f32[4,6,8,512]{3,2,1,0:T(8,128)S(1)}, f32[4,6,8,512]{3,2,1,0:T(8,128)S(1)}, u32[]{:S(2)}, u32[]{:S(2)}) collective-permute-start(f32[4,6,8,512]{3,2,1,0:T(8,128)S(1)} %get-tuple-element.38), channel_id=1, source_target_pairs={{0,1},{1,0},{2,3},{3,2},{4,5},{5,4},{6,7},{7,6},{8,9},{9,8},{10,11... | collective-permute-start | bytes 1179656 | tf_op jit(solution)/shard_map/ppermute | solution.py:466

commit v2 on v1

--- a/solution.py
+++ b/solution.py
@@ -40,25 +40,47 @@
 
 
 def pack_kernel(
-    conc,
-    adj,
-    east,
-    north,
-    diff,
-    cell,
-    value,
-    precision,
-    weight,
-    coef,
+    conc_at,
+    adj_at,
+    east_at,
+    north_at,
+    diff_at,
+    cell_at,
+    value_at,
+    precision_at,
+    weight_at,
+    block,
     coef_one,
     coef_two,
     adj_one,
     adj_two,
     message,
+    conc,
+    cell,
+    value,
+    precision,
+    weight,
     fields,
+    done,
 ):
     tracers, levels, cols, rows = conc.shape
     blocks = cell.shape[0]
+    moves = [
+        (cell_at, cell),
+        (value_at, value),
+        (precision_at, precision),
+        (weight_at, weight),
+        (conc_at, conc),
+        (diff_at, block.at[1]),
+        (east_at, block.at[2]),
+        (north_at, block.at[3]),
+        (adj_at, block.at[4 : 4 + tracers]),
+    ]
+    copies = [pltpu.make_async_copy(a, b, done.at[i]) for i, (a, b) in enumerate(moves)]
+    for copy in copies:
+        copy.start()
+    for copy in copies[:4]:
+        copy.wait()
     for h in range(3):
         for j in range(blocks):
             fields[h, j, 0:4, :] = weight[4 * h : 4 * h + 4, LANES * j : LANES * (j + 1)]
@@ -101,16 +123,18 @@
     one = jnp.where(band == 0, cols - 2, 0)
     two = jnp.where(band == 0, 0, cols - 2)
 
+    for copy in copies[4:]:
+        copy.wait()
+
     def level(at_level, carry):
         total = conc[0, at_level]
         for tr in range(1, tracers):
             total = total + conc[tr, at_level]
-        members = [total, diff[at_level], east[at_level], north[at_level]]
-        for q in range(4):
-            coef[q, at_level] = members[q]
+        block[0, at_level] = total
+        members = [total] + [block[q, at_level] for q in range(1, 4)]
         coef_one[at_level] = packed_rows(members, one)
         coef_two[at_level] = packed_rows(members, two)
-        members = [adj[tr, at_level] for tr in range(tracers)]
+        members = [block[4 + tr, at_level] for tr in range(tracers)]
         adj_one[at_level] = packed_rows(members, one)
         adj_two[at_level] = packed_rows(members, two)
         return carry
@@ -153,7 +177,7 @@
     total,
     diff,
 ):
-    _, band_levels, cols, rows = coef_own.shape
+    band_levels, cols, rows = coef_own.shape[1:]
     levels = 2 * band_levels
     tracers = inverse.shape[0]
     band = where_am_i()
@@ -256,8 +280,8 @@
 
 
 def solve_kernel(
-    adj_own,
-    adj_other,
+    block_own,
+    block_other,
     edge_own,
     edge_other,
     forcing,
@@ -273,21 +297,22 @@
     sent,
     state,
 ):
-    tracers, band_levels, cols, rows = adj_own.shape
+    tracers = kept.shape[0]
+    band_levels, cols, rows = block_own.shape[1:]
     levels = 2 * band_levels
     band = where_am_i()
     place = sublane((cols, rows))
     outside = (place >> 1) == jnp.where(band == 0, (cols - 2) >> 1, 0)
     zeros = tuple(jnp.zeros((cols, rows), jnp.float32) for _ in range(tracers))
 
-    def first_sweep(adj, edge, first, carry):
+    def first_sweep(block, edge, first, carry):
         def level(j, carry):
             g = first + j
             packed = edge[j]
             force = forcing[g]
             out = []
             for tr in range(tracers):
-                a = jnp.where(outside, unpacked_rows(packed, tr), adj[tr, j]) + force
+                a = jnp.where(outside, unpacked_rows(packed, tr), block[4 + tr, j]) + force
                 now = a * inverse[tr, g] + lower[tr, g] * carry[tr]
                 state[tr, g] = now
                 out.append(now)
@@ -297,13 +322,13 @@
 
     @pl.when(band == 0)
     def _():
-        carry = first_sweep(adj_own, edge_own, 0, zeros)
-        first_sweep(adj_other, edge_other, band_levels, carry)
+        carry = first_sweep(block_own, edge_own, 0, zeros)
+        first_sweep(block_other, edge_other, band_levels, carry)
 
     @pl.when(band != 0)
     def _():
-        carry = first_sweep(adj_other, edge_other, 0, zeros)
-        first_sweep(adj_own, edge_own, band_levels, carry)
+        carry = first_sweep(block_other, edge_other, 0, zeros)
+        first_sweep(block_own, edge_own, band_levels, carry)
 
     def back_and_advect():
         def level(i, carry):
@@ -318,7 +343,7 @@
                 state[tr, g] = mid * a + (along + across)
             return tuple(out)
 
-        lax.fori_loop(0, levels, level, zeros)
+        lax.fori_loop(0, levels, level, zeros, unroll=4)
 
     def forward():
         def level(g, carry):
@@ -373,7 +398,7 @@
     return jax.ShapeDtypeStruct(shape, jnp.float32)
 
 
-def call(kernel, outs, scratch, ops, limit, smem=0):
+def call(kernel, outs, scratch, ops, limit, smem=0, space=pltpu.VMEM):
     vmem = pl.BlockSpec(memory_space=pltpu.VMEM)
     scalars = pl.BlockSpec(memory_space=pltpu.SMEM)
 
@@ -382,7 +407,7 @@
         return pl.pallas_call(
             kernel,
             out_shape=outs,
-            in_specs=[scalars] * smem + [vmem] * (len(args) - smem),
+            in_specs=[scalars] * smem + [pl.BlockSpec(memory_space=space)] * (len(args) - smem),
             out_specs=[vmem] * len(outs),
             scratch_shapes=scratch,
             compiler_params=pltpu.CompilerParams(vmem_limit_bytes=limit * MIB),
@@ -412,12 +437,21 @@
     deep = f32(levels, cols, rows)
     full = f32(tracers, levels, cols, rows)
 
-    coef, coef_one, coef_two, adj_one, adj_two, message = call(
+    block, coef_one, coef_two, adj_one, adj_two, message = call(
         pack_kernel,
-        [f32(4, band_levels, cols, rows)] + [field] * 4 + [f32(tiles, 8, LANES)],
-        [pltpu.VMEM((4, blocks, 8, LANES), jnp.float32)],
+        [f32(4 + tracers, band_levels, cols, rows)] + [field] * 4 + [f32(tiles, 8, LANES)],
+        [
+            pltpu.VMEM((tracers, band_levels, cols, rows), jnp.float32),
+            pltpu.VMEM((blocks, LANES), jnp.int32),
+            pltpu.VMEM((blocks, LANES), jnp.float32),
+            pltpu.VMEM((blocks, LANES), jnp.float32),
+            pltpu.VMEM((band_levels, blocks * LANES), jnp.float32),
+            pltpu.VMEM((4, blocks, 8, LANES), jnp.float32),
+            pltpu.SemaphoreType.DMA((9,)),
+        ],
         10**6,
-        16,
+        54,
+        space=pltpu.HBM,
     )(
         concentration,
         adjoint_later,
@@ -439,13 +473,12 @@
 
     coef_edge_own = lax.ppermute(coef_one, both, same)
     coef_edge_other = lax.ppermute(coef_two, both, cross)
-    coef_other = lax.ppermute(coef, "band", swap)
+    adj_edge_own = lax.ppermute(adj_one, both, same)
+    adj_edge_other = lax.ppermute(adj_two, both, cross)
+    block_other = lax.ppermute(block, "band", swap)
     slots = lax.all_to_all(
         message.reshape(2 * tiles, 4, LANES), both, split_axis=0, concat_axis=0, tiled=True
     ).reshape(tiles, 8, LANES)
-    adj_other = lax.ppermute(adjoint_later, "band", swap)
-    adj_edge_own = lax.ppermute(adj_one, both, same)
-    adj_edge_other = lax.ppermute(adj_two, both, cross)
 
     ready = call(
         prepare_kernel,
@@ -454,7 +487,7 @@
         10**8,
         32,
         smem=1,
-    )(tracer_factor, coef, coef_other, coef_edge_own, coef_edge_other, slots)
+    )(tracer_factor, block, block_other, coef_edge_own, coef_edge_other, slots)
 
     kept, sent = call(
         solve_kernel,
@@ -462,7 +495,7 @@
         [pltpu.VMEM((tracers, levels, cols, rows), jnp.float32)],
         10**7,
         24,
-    )(adjoint_later, adj_other, adj_edge_own, adj_edge_other, *ready)
+    )(block, block_other, adj_edge_own, adj_edge_other, *ready)
     received = lax.ppermute(sent, "band", swap)
     return call(join_kernel, [f32(tracers, band_levels, cols, rows)], [], 10**5, 8)(kept, received)[0]
 

time: 49.8 us -> 40.6 us (0.82)
  local copies, waits for them, and re-layouts: 6.68 us -> 1.41 us
  waiting for transfers between devices: 6.68 us -> 1.72 us
  blocking collectives: 10.9 us -> 14.5 us
  starting transfers between devices: 11.8 us -> 8.93 us
  Pallas kernels: 13.2 us -> 13.7 us
    unnamed x18 -> x6, local copies, waits for them, and re-layouts: 6.68 us -> 1.41 us
    ppermute x1, waiting for transfers between devices: 5.06 us -> 0.01 us  [per_device(): coef_edge_own = lax.ppermute(coef_one, both, same)]
    all_to_all x1, blocking collectives: 10.9 us -> 14.5 us  [per_device(): lax.all_to_all(message.reshape(2 * tiles, 4, LANES), both, split_axis=0,...]
    ppermute x1, starting transfers between devices: 2.71 us -> 0.01 us  [per_device(): adj_edge_other = lax.ppermute(adj_two, both, cross)]
    pallas_call x4, Pallas kernels: 13.2 us -> 13.7 us  [run(): pl.pallas_call(kernel, out_shape=outs, in_specs=[scalars] * smem + [pl.Bl...]
  transfers between devices with their start and end apart: 7 -> 6, of which waited for: 2 -> 1; matrix products, arithmetic and copies ran while one was open for 0% -> 0% of each run, Pallas kernels for 7% -> 9%
where the time goes in v2:
time: 40.6 us; the launch traced here: 40.4 us
  blocking collectives  14.5 us (36%)
  Pallas kernels  13.7 us (34%)
  starting transfers between devices  8.93 us (22%)
  waiting for transfers between devices  1.72 us (4%)
  local copies, waits for them, and re-layouts  1.41 us (3%)
    all_to_all x1, blocking collectives, per_device(): lax.all_to_all(message.reshape(2 * tiles, 4, LANES), both, split_axis=0,...  14.5 us
    pallas_call x4, Pallas kernels, run(): pl.pallas_call(kernel, out_shape=outs, in_specs=[scalars] * smem + [pl.Bl...  13.7 us
    ppermute x1, starting transfers between devices, per_device(): coef_edge_other = lax.ppermute(coef_two, both, cross)  4.3 us
    ppermute x1, starting transfers between devices, per_device(): coef_edge_own = lax.ppermute(coef_one, both, same)  2.55 us
    ppermute x1, waiting for transfers between devices, per_device(): received = lax.ppermute(sent, 'band', swap)  1.71 us
    ppermute x1, starting transfers between devices, per_device(): adj_edge_own = lax.ppermute(adj_one, both, same)  1.49 us
    unnamed x6, local copies, waits for them, and re-layouts  1.41 us
  transfers between devices with their start and end apart: 6, of which 1 were waited for; matrix products, arithmetic and copies ran while one was open for 0% of the time, Pallas kernels for 9%

profile of v2, /device:TPU:0, one launch (start us, length us, event | category | flops | bytes accessed | tf_op | source)
XLA Modules:
  0.0 40.4 jit_solution(13020458576225319217)
XLA Ops:
  0.0 0.0 copy-start.2
  0.0 3.3 %shard_map.100 = (f32[8,12,8,512]{3,2,1,0:T(8,128)}, f32[12,8,512]{2,1,0:T(8,128)}, f32[12,8,512]{2,1,0:T(8,128)}, f32[12,8,512]{2,1,0:T(8,128)}, f32[12,8,512]{2,1,0:T(8,128)}, /*index=5*/f32[16,8,128]{2,1,0:T(8,128)}) custom-call(f32[4,12,8,512]{3,2,1,0:T(8,128)} %conc_at.1, f32[4,12,8,512]{3,2,1,0:T(8,128)} %adj_at.1, f32[12,8,512]{2,1,0:T(8,128)} %east_at.1, ...), custom_call_target="tpu_custom_call" | custom-call | flops 1000000 | bytes 4602880 | tf_op jit(solution)/shard_map/pallas_call | solution.py:407
  3.3 0.5 %collective-permute-start = (f32[8,12,8,512]{3,2,1,0:T(8,128)}, f32[8,12,8,512]{3,2,1,0:T(8,128)S(1)}, u32[]{:S(2)}, u32[]{:S(2)}) collective-permute-start(f32[8,12,8,512]{3,2,1,0:T(8,128)} %get-tuple-element.22.coef_own.block_own), channel_id=1, source_target_pairs={{0,1},{1,0},{2,3},{3,2},{4,5},{5,4},{6,7},{7,6},{8,9},{9,8},{10,11... | collective-permute-start | bytes 4718600 | tf_op jit(solution)/shard_map/ppermute | solution.py:478
  3.8 2.6 %collective-permute-start.3 = (f32[12,8,512]{2,1,0:T(8,128)}, f32[12,8,512]{2,1,0:T(8,128)S(1)}, u32[]{:S(2)}, u32[]{:S(2)}) collective-permute-start(f32[12,8,512]{2,1,0:T(8,128)} %get-tuple-element.25), channel_id=1, source_target_pairs={{0,2},{2,4},{4,6},{6,8},{8,10},{10,12},{12,14},{14,16},{16,18},{18... | collective-permute-start | bytes 589832 | tf_op jit(solution)/shard_map/ppermute | solution.py:474
  6.3 4.3 %collective-permute-start.4 = (f32[12,8,512]{2,1,0:T(8,128)}, f32[12,8,512]{2,1,0:T(8,128)S(1)}, u32[]{:S(2)}, u32[]{:S(2)}) collective-permute-start(f32[12,8,512]{2,1,0:T(8,128)} %get-tuple-element.26), channel_id=1, source_target_pairs={{1,2},{3,4},{5,6},{7,8},{9,10},{11,12},{13,14},{15,16},{17,18},{19... | collective-permute-start | bytes 589832 | tf_op jit(solution)/shard_map/ppermute | solution.py:475
  10.6 1.5 %collective-permute-start.1 = (f32[12,8,512]{2,1,0:T(8,128)}, f32[12,8,512]{2,1,0:T(8,128)S(1)}, u32[]{:S(2)}, u32[]{:S(2)}) collective-permute-start(f32[12,8,512]{2,1,0:T(8,128)} %get-tuple-element.23), channel_id=1, source_target_pairs={{0,2},{2,4},{4,6},{6,8},{8,10},{10,12},{12,14},{14,16},{16,18},{18... | collective-permute-start | bytes 589832 | tf_op jit(solution)/shard_map/ppermute | solution.py:476
  12.1 0.0 collective-permute-start.2
  12.1 14.5 %all_to_all.5 = f32[32,4,128]{2,1,0:T(4,128)S(1)} all-to-all(f32[32,4,128]{2,1,0:T(4,128)} %bitcast.7), channel_id=1, replica_groups=mesh['tile'=16,'band'=2] {'tile','band'}, dimensions={0} | all-to-all | bytes 131072 | tf_op jit(solution)/shard_map/all_to_all | solution.py:479
  26.6 0.0 collective-permute-done.3.edge_own
  26.6 0.0 collective-permute-done.4.edge_other
  26.6 0.0 collective-permute-done.coef_other.block_other
  26.6 0.0 copy-done.2
  26.6 0.0 copy-start
  26.6 1.4 %copy-done = f32[8,12,8,512]{3,2,1,0:T(8,128)S(1)} copy-done((f32[8,12,8,512]{3,2,1,0:T(8,128)S(1)}, f32[8,12,8,512]{3,2,1,0:T(8,128)}, u32[]{:S(2)}) %copy-start) | copy-done | bytes 1572888
  28.0 0.0 copy-start.1
  28.0 3.5 %shard_map.101 = (f32[24,8,512]{2,1,0:T(8,128)S(1)}, f32[24,8,512]{2,1,0:T(8,128)S(1)}, f32[24,8,512]{2,1,0:T(8,128)S(1)}, f32[24,8,512]{2,1,0:T(8,128)S(1)}, f3...) custom-call(f32[4]{0:T(128)S(1)} %copy-done.2, ...), custom_call_target="tpu_custom_call" | custom-call | flops 100000000 | bytes 10682384 | tf_op jit(solution)/shard_map/pallas_call | solution.py:407
  31.5 0.0 collective-permute-done.1.edge_own
  31.5 0.0 collective-permute-done.2.edge_other
  31.5 0.0 copy-done.1
  31.5 6.1 %shard_map.102 = (f32[4,12,8,512]{3,2,1,0:T(8,128)S(1)}, f32[4,6,8,512]{3,2,1,0:T(8,128)S(1)}) custom-call(f32[8,12,8,512]{3,2,1,0:T(8,128)S(1)} %copy-done.1, f32[8,12,8,512]{3,2,1,0:T(8,128)S(1)} %collective-permute-done.coef_other.block_other, f32[12,8,512]{2,1,0:T(8,128)S(1)} %collective-permute-done.1.edge_own, ...), custom_call_target="tpu_custom_call" | custom-call | flops 10000000 | bytes 11796480 | tf_op jit(solution)/shard_map/pallas_call | solution.py:407
  37.6 0.1 collective-permute-start.5
  37.7 1.7 %collective-permute-done.5.received = f32[4,6,8,512]{3,2,1,0:T(8,128)S(1)} collective-permute-done((f32[4,6,8,512]{3,2,1,0:T(8,128)S(1)}, f32[4,6,8,512]{3,2,1,0:T(8,128)S(1)}, u32[]{:S(2)}, u32[]{:S(2)}) %collective-permute-start.5) | collective-permute-done | bytes 393248 | tf_op jit(solution)/shard_map/ppermute | solution.py:499
  39.4 1.0 %shard_map.103 = f32[4,12,8,512]{3,2,1,0:T(8,128)} custom-call(f32[4,12,8,512]{3,2,1,0:T(8,128)S(1)} %get-tuple-element.37.kept, f32[4,6,8,512]{3,2,1,0:T(8,128)S(1)} %collective-permute-done.5.received), custom_call_target="tpu_custom_call" | custom-call | flops 100000 | bytes 1966080 | tf_op jit(solution)/shard_map/pallas_call | solution.py:407
Async XLA Ops:
  0.0 26.6 %copy-start.2 = (f32[4]{0:T(128)S(1)}, f32[4]{0:T(128)}, u32[]{:S(2)}) copy-start(f32[4]{0:T(128)} %factor.1) | copy-start | bytes 52
  3.3 23.3 %collective-permute-start = (f32[8,12,8,512]{3,2,1,0:T(8,128)}, f32[8,12,8,512]{3,2,1,0:T(8,128)S(1)}, u32[]{:S(2)}, u32[]{:S(2)}) collective-permute-start(f32[8,12,8,512]{3,2,1,0:T(8,128)} %get-tuple-element.22.coef_own.block_own), channel_id=1, source_target_pairs={{0,1},{1,0},{2,3},{3,2},{4,5},{5,4},{6,7},{7,6},{8,9},{9,8},{10,11... | collective-permute-start | bytes 4718600 | tf_op jit(solution)/shard_map/ppermute | solution.py:478
  3.8 22.8 %collective-permute-start.3 = (f32[12,8,512]{2,1,0:T(8,128)}, f32[12,8,512]{2,1,0:T(8,128)S(1)}, u32[]{:S(2)}, u32[]{:S(2)}) collective-permute-start(f32[12,8,512]{2,1,0:T(8,128)} %get-tuple-element.25), channel_id=1, source_target_pairs={{0,2},{2,4},{4,6},{6,8},{8,10},{10,12},{12,14},{14,16},{16,18},{18... | collective-permute-start | bytes 589832 | tf_op jit(solution)/shard_map/ppermute | solution.py:474
  6.3 20.3 %collective-permute-start.4 = (f32[12,8,512]{2,1,0:T(8,128)}, f32[12,8,512]{2,1,0:T(8,128)S(1)}, u32[]{:S(2)}, u32[]{:S(2)}) collective-permute-start(f32[12,8,512]{2,1,0:T(8,128)} %get-tuple-element.26), channel_id=1, source_target_pairs={{1,2},{3,4},{5,6},{7,8},{9,10},{11,12},{13,14},{15,16},{17,18},{19... | collective-permute-start | bytes 589832 | tf_op jit(solution)/shard_map/ppermute | solution.py:475
  10.6 20.9 %collective-permute-start.1 = (f32[12,8,512]{2,1,0:T(8,128)}, f32[12,8,512]{2,1,0:T(8,128)S(1)}, u32[]{:S(2)}, u32[]{:S(2)}) collective-permute-start(f32[12,8,512]{2,1,0:T(8,128)} %get-tuple-element.23), channel_id=1, source_target_pairs={{0,2},{2,4},{4,6},{6,8},{8,10},{10,12},{12,14},{14,16},{16,18},{18... | collective-permute-start | bytes 589832 | tf_op jit(solution)/shard_map/ppermute | solution.py:476
  12.1 19.4 %collective-permute-start.2 = (f32[12,8,512]{2,1,0:T(8,128)}, f32[12,8,512]{2,1,0:T(8,128)S(1)}, u32[]{:S(2)}, u32[]{:S(2)}) collective-permute-start(f32[12,8,512]{2,1,0:T(8,128)} %get-tuple-element.24), channel_id=1, source_target_pairs={{1,2},{3,4},{5,6},{7,8},{9,10},{11,12},{13,14},{15,16},{17,18},{19... | collective-permute-start | bytes 589832 | tf_op jit(solution)/shard_map/ppermute | solution.py:477
  26.6 1.4 %copy-start = (f32[8,12,8,512]{3,2,1,0:T(8,128)S(1)}, f32[8,12,8,512]{3,2,1,0:T(8,128)}, u32[]{:S(2)}) copy-start(f32[8,12,8,512]{3,2,1,0:T(8,128)} %get-tuple-element.22.coef_own.block_own) | copy-start | bytes 4718596
  28.0 3.5 %copy-start.1 = (f32[8,12,8,512]{3,2,1,0:T(8,128)S(1)}, f32[8,12,8,512]{3,2,1,0:T(8,128)}, u32[]{:S(2)}) copy-start(f32[8,12,8,512]{3,2,1,0:T(8,128)} %get-tuple-element.22.coef_own.block_own) | copy-start | bytes 4718596
  37.6 1.8 %collective-permute-start.5 = (f32[4,6,8,512]{3,2,1,0:T(8,128)S(1)}, f32[4,6,8,512]{3,2,1,0:T(8,128)S(1)}, u32[]{:S(2)}, u32[]{:S(2)}) collective-permute-start(f32[4,6,8,512]{3,2,1,0:T(8,128)S(1)} %get-tuple-element.38), channel_id=1, source_target_pairs={{0,1},{1,0},{2,3},{3,2},{4,5},{5,4},{6,7},{7,6},{8,9},{9,8},{10,11... | collective-permute-start | bytes 1179656 | tf_op jit(solution)/shard_map/ppermute | solution.py:499

commit v3 on v1

--- a/solution.py
+++ b/solution.py
@@ -35,11 +35,33 @@
     return out
 
 
+def packed_lines(members, columns):
+    place = sublane(members[0].shape)
+    lines = [members[0]]
+    lines += [pltpu.roll(member, q, 0) for q, member in enumerate(members) if q]
+    out = []
+    for c in columns:
+        one = lines[0]
+        for q in range(1, len(members)):
+            one = jnp.where(((place - c) & 7) == q, lines[q], one)
+        out.append(one)
+    return out
+
+
+def turned(tile, by):
+    return pltpu.roll(tile, by % 8, 0) if by % 8 else tile
+
+
 def unpacked_rows(packed, q):
     return packed if q == 0 else pltpu.roll(packed, 2 * q, 0)
 
 
+def first_kernel(out):
+    out[...] = jnp.zeros(out.shape, jnp.float32)
+
+
 def pack_kernel(
+    first,
     conc,
     adj,
     east,
@@ -49,16 +71,24 @@
     value,
     precision,
     weight,
-    coef,
-    coef_one,
-    coef_two,
-    adj_one,
-    adj_two,
+    block,
+    edge_same,
+    edge_cross,
     message,
     fields,
+    done,
 ):
     tracers, levels, cols, rows = conc.shape
     blocks = cell.shape[0]
+    moves = [
+        (diff, block.at[1]),
+        (east, block.at[2]),
+        (north, block.at[3]),
+        (adj, block.at[4 : 4 + tracers]),
+    ]
+    copies = [pltpu.make_async_copy(a, b, done.at[i]) for i, (a, b) in enumerate(moves)]
+    for copy in copies:
+        copy.start()
     for h in range(3):
         for j in range(blocks):
             fields[h, j, 0:4, :] = weight[4 * h : 4 * h + 4, LANES * j : LANES * (j + 1)]
@@ -75,7 +105,7 @@
             fields[h, j, 4:8, :] = jnp.where(at < LANES - HALF, near, after)
     at = lane((8, LANES))
     place = sublane((8, LANES))
-    edge = jnp.where(place < 4, float((cols - 2) * rows), float(2 * rows))
+    edge = jnp.where(place < 4, float((cols - 1) * rows), float(rows))
     is_cell = ((place & 3) == 0) & (at >= 96)
     for t in range(message.shape[0]):
         j, i = t // 8, t % 8
@@ -98,24 +128,21 @@
         message[t] = jnp.where(drop & is_cell, -1.0, both)
 
     band = where_am_i()
-    one = jnp.where(band == 0, cols - 2, 0)
-    two = jnp.where(band == 0, 0, cols - 2)
-
-    def level(at_level, carry):
-        total = conc[0, at_level]
+    first = jnp.where(band == 0, cols - 1, 0)
+    columns = [first, cols - 1 - first]
+
+    def level(j, carry):
+        total = conc[0, j]
         for tr in range(1, tracers):
-            total = total + conc[tr, at_level]
-        members = [total, diff[at_level], east[at_level], north[at_level]]
-        for q in range(4):
-            coef[q, at_level] = members[q]
-        coef_one[at_level] = packed_rows(members, one)
-        coef_two[at_level] = packed_rows(members, two)
-        members = [adj[tr, at_level] for tr in range(tracers)]
-        adj_one[at_level] = packed_rows(members, one)
-        adj_two[at_level] = packed_rows(members, two)
+            total = total + conc[tr, j]
+        block[0, j] = total
+        members = [total, diff[j], east[j]] + [adj[tr, j] for tr in range(tracers)]
+        edge_same[j], edge_cross[j] = packed_lines(members, columns)
         return carry
 
     lax.fori_loop(0, levels, level, 0, unroll=2)
+    for copy in copies:
+        copy.wait()
 
 
 def three_parts(x):
@@ -142,6 +169,7 @@
     edge_other,
     slots,
     forcing,
+    face,
     centre,
     east_part,
     west_part,
@@ -153,21 +181,19 @@
     total,
     diff,
 ):
-    _, band_levels, cols, rows = coef_own.shape
+    band_levels, cols, rows = coef_own.shape[1:]
     levels = 2 * band_levels
     tracers = inverse.shape[0]
     band = where_am_i()
     place = sublane((cols, rows))
     at = lane((cols, rows))
-    outside = (place >> 1) == jnp.where(band == 0, (cols - 2) >> 1, 0)
+    outside = place == jnp.where(band == 0, cols - 1, 0)
 
     def assemble(coef, edge, first):
         def level(j, carry):
             packed = edge[j]
-            t, d, e, n = [
-                jnp.where(outside, unpacked_rows(packed, q), coef[q, j]) for q in range(4)
-            ]
-            n = jnp.where(at == rows - 1, 0.0, n)
+            t, d, e = [jnp.where(outside, turned(packed, -q), coef[q, j]) for q in range(3)]
+            n = jnp.where(at == rows - 1, 0.0, coef[3, j])
             to_east = jnp.maximum(e, 0.0)
             to_west = jnp.minimum(pltpu.roll(e, 1, 0), 0.0)
             to_north = jnp.maximum(n, 0.0)
@@ -175,6 +201,7 @@
             g = first + j
             total[g] = t
             diff[g] = d
+            face[g] = e
             east_part[g] = to_east
             west_part[g] = -to_west
             north_part[g] = to_north
@@ -256,11 +283,12 @@
 
 
 def solve_kernel(
-    adj_own,
-    adj_other,
+    block_own,
+    block_other,
     edge_own,
     edge_other,
     forcing,
+    face,
     centre,
     east_part,
     west_part,
@@ -270,24 +298,27 @@
     lower,
     ratio,
     kept,
-    sent,
+    to_band,
+    to_cross,
+    to_same,
     state,
 ):
-    tracers, band_levels, cols, rows = adj_own.shape
+    tracers = kept.shape[0]
+    band_levels, cols, rows = block_own.shape[1:]
     levels = 2 * band_levels
     band = where_am_i()
     place = sublane((cols, rows))
-    outside = (place >> 1) == jnp.where(band == 0, (cols - 2) >> 1, 0)
+    outside = place == jnp.where(band == 0, cols - 1, 0)
     zeros = tuple(jnp.zeros((cols, rows), jnp.float32) for _ in range(tracers))
 
-    def first_sweep(adj, edge, first, carry):
+    def first_sweep(block, edge, first, carry):
         def level(j, carry):
             g = first + j
             packed = edge[j]
             force = forcing[g]
             out = []
             for tr in range(tracers):
-                a = jnp.where(outside, unpacked_rows(packed, tr), adj[tr, j]) + force
+                a = jnp.where(outside, turned(packed, -3 - tr), block[4 + tr, j]) + force
                 now = a * inverse[tr, g] + lower[tr, g] * carry[tr]
                 state[tr, g] = now
                 out.append(now)
@@ -297,13 +328,13 @@
 
     @pl.when(band == 0)
     def _():
-        carry = first_sweep(adj_own, edge_own, 0, zeros)
-        first_sweep(adj_other, edge_other, band_levels, carry)
+        carry = first_sweep(block_own, edge_own, 0, zeros)
+        first_sweep(block_other, edge_other, band_levels, carry)
 
     @pl.when(band != 0)
     def _():
-        carry = first_sweep(adj_other, edge_other, 0, zeros)
-        first_sweep(adj_own, edge_own, band_levels, carry)
+        carry = first_sweep(block_other, edge_other, 0, zeros)
+        first_sweep(block_own, edge_own, band_levels, carry)
 
     def back_and_advect():
         def level(i, carry):
@@ -318,7 +349,7 @@
                 state[tr, g] = mid * a + (along + across)
             return tuple(out)
 
-        lax.fori_loop(0, levels, level, zeros)
+        lax.fori_loop(0, levels, level, zeros, unroll=4)
 
     def forward():
         def level(g, carry):
@@ -331,49 +362,87 @@
 
         lax.fori_loop(0, levels, level, zeros, unroll=2)
 
+    def back():
+        def level(i, carry):
+            g = levels - 1 - i
+            out = []
+            for tr in range(tracers):
+                now = state[tr, g] + ratio[tr, g] * carry[tr]
+                state[tr, g] = now
+                out.append(now)
+            return tuple(out)
+
+        lax.fori_loop(0, levels, level, zeros, unroll=4)
+
     back_and_advect()
     forward()
-    back_and_advect()
+    back()
 
     half = band_levels // 2
-    mine = (place >> 2) == band
     own_first = band * band_levels
     other_first = (1 - band) * band_levels
+    edge = jnp.where(band == 0, 0, cols - 1)
 
     def hand_out(j, carry):
-        for tr in range(tracers):
-            kept[tr, j] = state[tr, own_first + j]
-            kept[tr, j + half] = state[tr, own_first + j + half]
-            sent[tr, j] = jnp.where(
-                mine,
-                state[tr, other_first + j],
-                pltpu.roll(state[tr, other_first + j + half], 4, 0),
-            )
+        for l in (j, j + half):
+            others = [state[tr, other_first + l] for tr in range(tracers)]
+            to_band[l] = packed_rows(others, jnp.where(band == 0, 0, cols - 2))
+            to_band[band_levels + l] = face[other_first + l]
+            for tr in range(tracers):
+                kept[tr, l] = state[tr, own_first + l]
+        for first, out in ((other_first, to_cross), (own_first, to_same)):
+            members = [state[tr, first + l] for l in (j, j + half) for tr in range(tracers)]
+            out[j] = packed_lines(members, [edge])[0]
         return carry
 
     lax.fori_loop(0, half, hand_out, 0)
 
 
-def join_kernel(kept, received, out):
+def finish_kernel(kept, from_band, from_cross, from_same, block, face, out):
     tracers, band_levels, cols, rows = kept.shape
     half = band_levels // 2
-    mine = (sublane((cols, rows)) >> 2) == where_am_i()
-
-    def level(j, carry):
-        for tr in range(tracers):
-            got = received[tr, j]
-            out[tr, j] = jnp.where(mine, kept[tr, j], got)
-            out[tr, j + half] = jnp.where(mine, kept[tr, j + half], pltpu.roll(got, 4, 0))
+    band = where_am_i()
+    place = sublane((cols, rows))
+    at = lane((cols, rows))
+    outside = (place >> 1) == jnp.where(band == 0, (cols - 2) >> 1, 0)
+    own_first = band * band_levels
+
+    def pair(j, carry):
+        cross, same = from_cross[j], from_same[j]
+        westward = jnp.where(band == 0, cross, same)
+        eastward = jnp.where(band == 0, same, cross)
+        for side in range(2):
+            l = j + side * half
+            e = block[2, l]
+            n = jnp.where(at == rows - 1, 0.0, block[3, l])
+            before = jnp.where(band == 0, face[own_first + l], from_band[band_levels + l])
+            w = pltpu.roll(jnp.where(place == cols - 1, before, e), 1, 0)
+            to_east = jnp.maximum(e, 0.0)
+            to_west = jnp.minimum(w, 0.0)
+            to_north = jnp.maximum(n, 0.0)
+            to_south = jnp.minimum(pltpu.roll(n, 1, 1), 0.0)
+            centre = ((1.0 - to_east) + to_west) + (to_south - to_north)
+            got = from_band[l]
+            for tr in range(tracers):
+                q = tr + 4 * side
+                a = jnp.where(outside, unpacked_rows(got, tr), kept[tr, l])
+                a_east = jnp.where(
+                    place == cols - 1, turned(eastward, -1 - q), pltpu.roll(a, cols - 1, 0)
+                )
+                a_west = jnp.where(place == 0, turned(westward, 1 - q), pltpu.roll(a, 1, 0))
+                along = to_east * a_east - to_west * a_west
+                across = to_north * pltpu.roll(a, rows - 1, 1) - to_south * pltpu.roll(a, 1, 1)
+                out[tr, l] = centre * a + (along + across)
         return carry
 
-    lax.fori_loop(0, half, level, 0)
+    lax.fori_loop(0, half, pair, 0)
 
 
 def f32(*shape):
     return jax.ShapeDtypeStruct(shape, jnp.float32)
 
 
-def call(kernel, outs, scratch, ops, limit, smem=0):
+def call(kernel, outs, scratch, ops, limit, smem=0, space=pltpu.VMEM):
     vmem = pl.BlockSpec(memory_space=pltpu.VMEM)
     scalars = pl.BlockSpec(memory_space=pltpu.SMEM)
 
@@ -382,7 +451,7 @@
         return pl.pallas_call(
             kernel,
             out_shape=outs,
-            in_specs=[scalars] * smem + [vmem] * (len(args) - smem),
+            in_specs=[scalars] * smem + [pl.BlockSpec(memory_space=space)] * (len(args) - smem),
             out_specs=[vmem] * len(outs),
             scratch_shapes=scratch,
             compiler_params=pltpu.CompilerParams(vmem_limit_bytes=limit * MIB),
@@ -412,13 +481,15 @@
     deep = f32(levels, cols, rows)
     full = f32(tracers, levels, cols, rows)
 
-    coef, coef_one, coef_two, adj_one, adj_two, message = call(
+    first = call(first_kernel, [f32(8, LANES)], [], 10**9, 8)()[0]
+    block, edge_same, edge_cross, message = call(
         pack_kernel,
-        [f32(4, band_levels, cols, rows)] + [field] * 4 + [f32(tiles, 8, LANES)],
-        [pltpu.VMEM((4, blocks, 8, LANES), jnp.float32)],
+        [f32(4 + tracers, band_levels, cols, rows), field, field, f32(tiles, 8, LANES)],
+        [pltpu.VMEM((4, blocks, 8, LANES), jnp.float32), pltpu.SemaphoreType.DMA((4,))],
         10**6,
         16,
     )(
+        first,
         concentration,
         adjoint_later,
         courant_east,
@@ -435,36 +506,40 @@
     same += [(2 * t + 1, 2 * ((t - 1) % tiles) + 1) for t in range(tiles)]
     cross = [(2 * t + 1, 2 * ((t + 1) % tiles)) for t in range(tiles)]
     cross += [(2 * t, 2 * ((t - 1) % tiles) + 1) for t in range(tiles)]
+    along = [(2 * t + 1, 2 * ((t + 1) % tiles) + 1) for t in range(tiles)]
+    along += [(2 * t, 2 * ((t - 1) % tiles)) for t in range(tiles)]
     swap = [(0, 1), (1, 0)]
 
-    coef_edge_own = lax.ppermute(coef_one, both, same)
-    coef_edge_other = lax.ppermute(coef_two, both, cross)
-    coef_other = lax.ppermute(coef, "band", swap)
+    edge_own = lax.ppermute(edge_same, both, same)
+    edge_other = lax.ppermute(edge_cross, both, cross)
+    block_other = lax.ppermute(block, "band", swap)
     slots = lax.all_to_all(
         message.reshape(2 * tiles, 4, LANES), both, split_axis=0, concat_axis=0, tiled=True
     ).reshape(tiles, 8, LANES)
-    adj_other = lax.ppermute(adjoint_later, "band", swap)
-    adj_edge_own = lax.ppermute(adj_one, both, same)
-    adj_edge_other = lax.ppermute(adj_two, both, cross)
-
-    ready = call(
+
+    forcing, face, *ready = call(
         prepare_kernel,
-        [deep] * 6 + [full] * 3,
+        [deep] * 7 + [full] * 3,
         [pltpu.VMEM((levels, cols, rows), jnp.float32)] * 2,
         10**8,
         32,
         smem=1,
-    )(tracer_factor, coef, coef_other, coef_edge_own, coef_edge_other, slots)
-
-    kept, sent = call(
+    )(tracer_factor, block, block_other, edge_own, edge_other, slots)
+
+    part = f32(band_levels // 2, cols, rows)
+    kept, to_band, to_cross, to_same = call(
         solve_kernel,
-        [f32(tracers, band_levels, cols, rows), f32(tracers, band_levels // 2, cols, rows)],
+        [f32(tracers, band_levels, cols, rows), deep, part, part],
         [pltpu.VMEM((tracers, levels, cols, rows), jnp.float32)],
         10**7,
         24,
-    )(adjoint_later, adj_other, adj_edge_own, adj_edge_other, *ready)
-    received = lax.ppermute(sent, "band", swap)
-    return call(join_kernel, [f32(tracers, band_levels, cols, rows)], [], 10**5, 8)(kept, received)[0]
+    )(block, block_other, edge_own, edge_other, forcing, face, *ready)
+    from_cross = lax.ppermute(to_cross, both, cross)
+    from_same = lax.ppermute(to_same, both, along)
+    from_band = lax.ppermute(to_band, "band", swap)
+    return call(finish_kernel, [f32(tracers, band_levels, cols, rows)], [], 10**6, 16)(
+        kept, from_band, from_cross, from_same, block, face
+    )[0]
 
 
 def solution(mesh):

time: 49.8 us -> 36.9 us (0.74)
  local copies, waits for them, and re-layouts: 6.68 us -> 1.67 us
  Pallas kernels: 13.2 us -> 10.2 us
  waiting for transfers between devices: 6.68 us -> 4.58 us
  blocking collectives: 10.9 us -> 9.09 us
  starting transfers between devices: 11.8 us -> 10.8 us
    unnamed x18 -> x20, local copies, waits for them, and re-layouts: 6.68 us -> 1.67 us
    pallas_call x4 -> x5, Pallas kernels: 13.2 us -> 10.2 us  [run(): pl.pallas_call(kernel, out_shape=outs, in_specs=[scalars] * smem + [pl.Bl...]
    ppermute x7 -> x6, waiting for transfers between devices: 6.68 us -> 4.58 us  [the longest x1 4.34 us: per_device(): from_cross = lax.ppermute(to_cross, both, cross)]
    all_to_all x1, blocking collectives: 10.9 us -> 9.09 us  [per_device(): lax.all_to_all(message.reshape(2 * tiles, 4, LANES), both, split_axis=0,...]
    ppermute x7 -> x6, starting transfers between devices: 11.8 us -> 10.8 us  [the longest x1 4.3 us: per_device(): edge_other = lax.ppermute(edge_cross, both, cross)]
  transfers between devices with their start and end apart: 7 -> 6, of which waited for: 2 -> 2; matrix products, arithmetic and copies ran while one was open for 0% -> 0% of each run, Pallas kernels for 7% -> 0%
where the time goes in v3:
time: 36.9 us; the launch traced here: 36.5 us
  starting transfers between devices  10.8 us (29%)
  Pallas kernels  10.2 us (28%)
  blocking collectives  9.09 us (25%)
  waiting for transfers between devices  4.58 us (12%)
  local copies, waits for them, and re-layouts  1.67 us (5%)
    pallas_call x5, Pallas kernels, run(): pl.pallas_call(kernel, out_shape=outs, in_specs=[scalars] * smem + [pl.Bl...  10.2 us
    all_to_all x1, blocking collectives, per_device(): lax.all_to_all(message.reshape(2 * tiles, 4, LANES), both, split_axis=0,...  9.09 us
    ppermute x1, waiting for transfers between devices, per_device(): from_cross = lax.ppermute(to_cross, both, cross)  4.34 us
    ppermute x1, starting transfers between devices, per_device(): edge_other = lax.ppermute(edge_cross, both, cross)  4.3 us
    ppermute x1, starting transfers between devices, per_device(): from_cross = lax.ppermute(to_cross, both, cross)  3.25 us
    ppermute x1, starting transfers between devices, per_device(): edge_own = lax.ppermute(edge_same, both, same)  2.55 us
    unnamed x20, local copies, waits for them, and re-layouts  1.67 us
  transfers between devices with their start and end apart: 6, of which 2 were waited for; matrix products, arithmetic and copies ran while one was open for 0% of the time, Pallas kernels for 0%

profile of v3, /device:TPU:0, one launch (start us, length us, event | category | flops | bytes accessed | tf_op | source)
XLA Modules:
  0.0 36.5 jit_solution(17141348991419252249)
XLA Ops:
  0.1 0.0 copy-start.9
  0.1 0.6 %copy-done.5 = f32[256,12]{0,1:T(8,128)S(1)} copy-done((f32[256,12]{0,1:T(8,128)S(1)}, f32[256,12]{0,1:T(8,128)}, u32[]{:S(2)}) %copy-start.5) | copy-done | bytes 12312
  0.7 0.0 copy-done.6
  0.7 0.3 copy-done.4
  1.0 0.1 copy-done.3
  1.1 0.1 copy-done.2
  1.2 0.3 copy-done.1
  1.5 0.2 copy-done
  1.7 1.2 %shard_map.101 = (f32[8,12,8,512]{3,2,1,0:T(8,128)S(1)}, f32[12,8,512]{2,1,0:T(8,128)S(1)}, f32[12,8,512]{2,1,0:T(8,128)S(1)}, f32[16,8,128]{2,1,0:T(8,128)S(1)}) custom-call(f32[8,128]{1,0:T(8,128)S(1)} %shard_map.100.first, f32[4,12,8,512]{3,2,1,0:T(8,128)S(1)} %copy-done, f32[4,12,8,512]{3,2,1,0:T(8,128)S(1)} %copy-done.1, f32[12,8,512]{2,1,0:T(8,128)S(1)} %copy-done.2, ...), custom_call_target="tpu_custom_call" | custom-call | flops 1000000 | bytes 4213760 | tf_op jit(solution)/shard_map/pallas_call | solution.py:451
  3.0 0.5 %collective-permute-start = (f32[8,12,8,512]{3,2,1,0:T(8,128)S(1)}, f32[8,12,8,512]{3,2,1,0:T(8,128)S(1)}, u32[]{:S(2)}, u32[]{:S(2)}) collective-permute-start(f32[8,12,8,512]{3,2,1,0:T(8,128)S(1)} %get-tuple-element.23.coef_own.block_own.block), channel_id=1, source_target_pairs={{0,1},{1,0},{2,3},{3,2},{4,5},{5,4},{6,7},{7,6},{8,9},{9,8},{10,11... | collective-permute-start | bytes 4718600 | tf_op jit(solution)/shard_map/ppermute | solution.py:515
  3.5 2.6 %collective-permute-start.1 = (f32[12,8,512]{2,1,0:T(8,128)S(1)}, f32[12,8,512]{2,1,0:T(8,128)S(1)}, u32[]{:S(2)}, u32[]{:S(2)}) collective-permute-start(f32[12,8,512]{2,1,0:T(8,128)S(1)} %get-tuple-element.24), channel_id=1, source_target_pairs={{0,2},{2,4},{4,6},{6,8},{8,10},{10,12},{12,14},{14,16},{16,18},{18... | collective-permute-start | bytes 589832 | tf_op jit(solution)/shard_map/ppermute | solution.py:513
  6.0 4.3 %collective-permute-start.2 = (f32[12,8,512]{2,1,0:T(8,128)S(1)}, f32[12,8,512]{2,1,0:T(8,128)S(1)}, u32[]{:S(2)}, u32[]{:S(2)}) collective-permute-start(f32[12,8,512]{2,1,0:T(8,128)S(1)} %get-tuple-element.25), channel_id=1, source_target_pairs={{1,2},{3,4},{5,6},{7,8},{9,10},{11,12},{13,14},{15,16},{17,18},{19... | collective-permute-start | bytes 589832 | tf_op jit(solution)/shard_map/ppermute | solution.py:514
  10.3 9.1 %all_to_all.5 = f32[32,4,128]{2,1,0:T(4,128)S(1)} all-to-all(f32[32,4,128]{2,1,0:T(4,128)S(1)} %bitcast.7), channel_id=1, replica_groups=mesh['tile'=16,'band'=2] {'tile','band'}, dimensions={0} | all-to-all | bytes 131072 | tf_op jit(solution)/shard_map/all_to_all | solution.py:516
  19.4 0.0 collective-permute-done.1.edge_own
  19.4 0.0 collective-permute-done.2.edge_other
  19.4 3.4 %shard_map.102 = (f32[24,8,512]{2,1,0:T(8,128)S(1)}, f32[24,8,512]{2,1,0:T(8,128)S(1)}, f32[24,8,512]{2,1,0:T(8,128)S(1)}, f32[24,8,512]{2,1,0:T(8,128)S(1)}, f3...) custom-call(f32[4]{0:T(128)S(1)} %copy-done.9, ...), custom_call_target="tpu_custom_call" | custom-call | flops 100000000 | bytes 11075600 | tf_op jit(solution)/shard_map/pallas_call | solution.py:451
  22.9 3.8 %shard_map.103 = (f32[4,12,8,512]{3,2,1,0:T(8,128)S(1)}, f32[24,8,512]{2,1,0:T(8,128)S(1)}, f32[6,8,512]{2,1,0:T(8,128)S(1)}, f32[6,8,512]{2,1,0:T(8,128)S(1)}) custom-call(f32[8,12,8,512]{3,2,1,0:T(8,128)S(1)} %get-tuple-element.23.coef_own.block_own.block, f32[8,12,8,512]{3,2,1,0:T(8,128)S(1)} %collective-permute-done.coef_other.block_other, ...), custom_call_target="tpu_custom_call" | custom-call | flops 10000000 | bytes 12386304 | tf_op jit(solution)/shard_map/pallas_call | solution.py:451
  26.6 0.2 collective-permute-start.3
  26.8 3.3 %collective-permute-start.4 = (f32[6,8,512]{2,1,0:T(8,128)S(1)}, f32[6,8,512]{2,1,0:T(8,128)S(1)}, u32[]{:S(2)}, u32[]{:S(2)}) collective-permute-start(f32[6,8,512]{2,1,0:T(8,128)S(1)} %get-tuple-element.39), channel_id=1, source_target_pairs={{1,2},{3,4},{5,6},{7,8},{9,10},{11,12},{13,14},{15,16},{17,18},{19... | collective-permute-start | bytes 294920 | tf_op jit(solution)/shard_map/ppermute | solution.py:537
  30.0 0.0 collective-permute-start.5
  30.1 4.3 %collective-permute-done.4.from_cross = f32[6,8,512]{2,1,0:T(8,128)S(1)} collective-permute-done((f32[6,8,512]{2,1,0:T(8,128)S(1)}, f32[6,8,512]{2,1,0:T(8,128)S(1)}, u32[]{:S(2)}, u32[]{:S(2)}) %collective-permute-start.4) | collective-permute-done | bytes 98336 | tf_op jit(solution)/shard_map/ppermute | solution.py:537
  34.4 0.2 collective-permute-done.5.from_same
  34.7 0.0 collective-permute-done.3.from_band
  34.7 1.8 %shard_map.104 = f32[4,12,8,512]{3,2,1,0:T(8,128)} custom-call(f32[4,12,8,512]{3,2,1,0:T(8,128)S(1)} %get-tuple-element.37.kept, f32[24,8,512]{2,1,0:T(8,128)S(1)} %collective-permute-done.3.from_band, f32[6,8,512]{2,1,0:T(8,128)S(1)} %collective-permute-done.4.from_cross, f32[6,8,512]{2,1,0:T(8,128)S(1)} %collective-permute-done.5.from_same, ...), custom_call_target="tpu_custom_call" | custom-call | flops 1000000 | bytes 4128768 | tf_op jit(solution)/shard_map/pallas_call | solution.py:451
  (14 shorter events, 0.0 us)
Async XLA Ops:
  0.0 0.7 %copy-start.5 = (f32[256,12]{0,1:T(8,128)S(1)}, f32[256,12]{0,1:T(8,128)}, u32[]{:S(2)}) copy-start(f32[256,12]{0,1:T(8,128)} %param.19) | copy-start | bytes 36868
  0.0 0.7 %copy-start.8 = (f32[256]{0:T(256)S(1)}, f32[256]{0:T(256)}, u32[]{:S(2)}) copy-start(f32[256]{0:T(256)} %param.18) | copy-start | bytes 3076
  0.0 0.7 %copy-start.7 = (f32[256]{0:T(256)S(1)}, f32[256]{0:T(256)}, u32[]{:S(2)}) copy-start(f32[256]{0:T(256)} %param.17) | copy-start | bytes 3076
  0.0 0.7 %copy-start.6 = (s32[256]{0:T(256)S(1)}, s32[256]{0:T(256)}, u32[]{:S(2)}) copy-start(s32[256]{0:T(256)} %param.16) | copy-start | bytes 3076
  0.0 1.0 %copy-start.4 = (f32[12,8,512]{2,1,0:T(8,128)S(1)}, f32[12,8,512]{2,1,0:T(8,128)}, u32[]{:S(2)}) copy-start(f32[12,8,512]{2,1,0:T(8,128)} %diff.1) | copy-start | bytes 589828
  0.0 1.1 %copy-start.3 = (f32[12,8,512]{2,1,0:T(8,128)S(1)}, f32[12,8,512]{2,1,0:T(8,128)}, u32[]{:S(2)}) copy-start(f32[12,8,512]{2,1,0:T(8,128)} %north.1) | copy-start | bytes 589828
  0.0 1.2 %copy-start.2 = (f32[12,8,512]{2,1,0:T(8,128)S(1)}, f32[12,8,512]{2,1,0:T(8,128)}, u32[]{:S(2)}) copy-start(f32[12,8,512]{2,1,0:T(8,128)} %east.1) | copy-start | bytes 589828
  0.0 1.5 %copy-start.1 = (f32[4,12,8,512]{3,2,1,0:T(8,128)S(1)}, f32[4,12,8,512]{3,2,1,0:T(8,128)}, u32[]{:S(2)}) copy-start(f32[4,12,8,512]{3,2,1,0:T(8,128)} %adj.1) | copy-start | bytes 2359300
  0.0 1.7 %copy-start = (f32[4,12,8,512]{3,2,1,0:T(8,128)S(1)}, f32[4,12,8,512]{3,2,1,0:T(8,128)}, u32[]{:S(2)}) copy-start(f32[4,12,8,512]{3,2,1,0:T(8,128)} %conc.1) | copy-start | bytes 2359300
  0.1 19.4 %copy-start.9 = (f32[4]{0:T(128)S(1)}, f32[4]{0:T(128)}, u32[]{:S(2)}) copy-start(f32[4]{0:T(128)} %factor.1) | copy-start | bytes 52
  3.0 16.5 %collective-permute-start = (f32[8,12,8,512]{3,2,1,0:T(8,128)S(1)}, f32[8,12,8,512]{3,2,1,0:T(8,128)S(1)}, u32[]{:S(2)}, u32[]{:S(2)}) collective-permute-start(f32[8,12,8,512]{3,2,1,0:T(8,128)S(1)} %get-tuple-element.23.coef_own.block_own.block), channel_id=1, source_target_pairs={{0,1},{1,0},{2,3},{3,2},{4,5},{5,4},{6,7},{7,6},{8,9},{9,8},{10,11... | collective-permute-start | bytes 4718600 | tf_op jit(solution)/shard_map/ppermute | solution.py:515
  3.5 15.9 %collective-permute-start.1 = (f32[12,8,512]{2,1,0:T(8,128)S(1)}, f32[12,8,512]{2,1,0:T(8,128)S(1)}, u32[]{:S(2)}, u32[]{:S(2)}) collective-permute-start(f32[12,8,512]{2,1,0:T(8,128)S(1)} %get-tuple-element.24), channel_id=1, source_target_pairs={{0,2},{2,4},{4,6},{6,8},{8,10},{10,12},{12,14},{14,16},{16,18},{18... | collective-permute-start | bytes 589832 | tf_op jit(solution)/shard_map/ppermute | solution.py:513
  6.0 13.4 %collective-permute-start.2 = (f32[12,8,512]{2,1,0:T(8,128)S(1)}, f32[12,8,512]{2,1,0:T(8,128)S(1)}, u32[]{:S(2)}, u32[]{:S(2)}) collective-permute-start(f32[12,8,512]{2,1,0:T(8,128)S(1)} %get-tuple-element.25), channel_id=1, source_target_pairs={{1,2},{3,4},{5,6},{7,8},{9,10},{11,12},{13,14},{15,16},{17,18},{19... | collective-permute-start | bytes 589832 | tf_op jit(solution)/shard_map/ppermute | solution.py:514
  26.6 8.1 %collective-permute-start.3 = (f32[24,8,512]{2,1,0:T(8,128)S(1)}, f32[24,8,512]{2,1,0:T(8,128)S(1)}, u32[]{:S(2)}, u32[]{:S(2)}) collective-permute-start(f32[24,8,512]{2,1,0:T(8,128)S(1)} %get-tuple-element.38), channel_id=1, source_target_pairs={{0,1},{1,0},{2,3},{3,2},{4,5},{5,4},{6,7},{7,6},{8,9},{9,8},{10,11... | collective-permute-start | bytes 1179656 | tf_op jit(solution)/shard_map/ppermute | solution.py:539
  26.8 7.6 %collective-permute-start.4 = (f32[6,8,512]{2,1,0:T(8,128)S(1)}, f32[6,8,512]{2,1,0:T(8,128)S(1)}, u32[]{:S(2)}, u32[]{:S(2)}) collective-permute-start(f32[6,8,512]{2,1,0:T(8,128)S(1)} %get-tuple-element.39), channel_id=1, source_target_pairs={{1,2},{3,4},{5,6},{7,8},{9,10},{11,12},{13,14},{15,16},{17,18},{19... | collective-permute-start | bytes 294920 | tf_op jit(solution)/shard_map/ppermute | solution.py:537
  30.0 4.6 %collective-permute-start.5 = (f32[6,8,512]{2,1,0:T(8,128)S(1)}, f32[6,8,512]{2,1,0:T(8,128)S(1)}, u32[]{:S(2)}, u32[]{:S(2)}) collective-permute-start(f32[6,8,512]{2,1,0:T(8,128)S(1)} %get-tuple-element.40), channel_id=1, source_target_pairs={{1,3},{3,5},{5,7},{7,9},{9,11},{11,13},{13,15},{15,17},{17,19},{19... | collective-permute-start | bytes 294920 | tf_op jit(solution)/shard_map/ppermute | solution.py:538

commit v4 on v3

--- a/solution.py
+++ b/solution.py
@@ -12,6 +12,11 @@
 PAIR = 32
 HALF = 16
 MIB = 1 << 20
+GROUP = 2
+UNROLL_A = 2
+UNROLL_B = 2
+UNROLL_C = 2
+UNROLL_D = 1
 
 
 def where_am_i():
@@ -161,77 +166,9 @@
     return out
 
 
-def prepare_kernel(
-    factor,
-    coef_own,
-    coef_other,
-    edge_own,
-    edge_other,
-    slots,
-    forcing,
-    face,
-    centre,
-    east_part,
-    west_part,
-    north_part,
-    south_part,
-    inverse,
-    lower,
-    ratio,
-    total,
-    diff,
-):
-    band_levels, cols, rows = coef_own.shape[1:]
-    levels = 2 * band_levels
-    tracers = inverse.shape[0]
-    band = where_am_i()
-    place = sublane((cols, rows))
-    at = lane((cols, rows))
-    outside = place == jnp.where(band == 0, cols - 1, 0)
-
-    def assemble(coef, edge, first):
-        def level(j, carry):
-            packed = edge[j]
-            t, d, e = [jnp.where(outside, turned(packed, -q), coef[q, j]) for q in range(3)]
-            n = jnp.where(at == rows - 1, 0.0, coef[3, j])
-            to_east = jnp.maximum(e, 0.0)
-            to_west = jnp.minimum(pltpu.roll(e, 1, 0), 0.0)
-            to_north = jnp.maximum(n, 0.0)
-            to_south = jnp.minimum(pltpu.roll(n, 1, 1), 0.0)
-            g = first + j
-            total[g] = t
-            diff[g] = d
-            face[g] = e
-            east_part[g] = to_east
-            west_part[g] = -to_west
-            north_part[g] = to_north
-            south_part[g] = -to_south
-            centre[g] = ((1.0 - to_east) + to_west) + (to_south - to_north)
-            return carry
-
-        lax.fori_loop(0, band_levels, level, 0, unroll=2)
-
-    assemble(coef_own, edge_own, band * band_levels)
-    assemble(coef_other, edge_other, (1 - band) * band_levels)
-
-    zero = jnp.zeros((cols, rows), jnp.float32)
-
-    def factorise(g, carry):
-        d = jnp.where(g < levels - 1, diff[g], 0.0)
-        out = []
-        for tr in range(tracers):
-            above, before = carry[tr]
-            kappa = factor[tr] * d
-            inv = 1.0 / (((1.0 + above) + kappa) - above * before)
-            now = kappa * inv
-            inverse[tr, g] = inv
-            lower[tr, g] = above * inv
-            ratio[tr, g] = now
-            out.append((kappa, now))
-        return tuple(out)
-
-    lax.fori_loop(0, levels, factorise, tuple((zero, zero) for _ in range(tracers)))
-
+def add_soundings(slots, total, forcing):
+    levels, cols, rows = total.shape
+    band_levels = levels // 2
     sources = slots.shape[0]
     chunk = min(16, sources)
     wide = chunk * PAIR
@@ -282,160 +219,237 @@
         lax.fori_loop(1, sources // chunk, more, 0)
 
 
-def solve_kernel(
+def core_kernel(
+    factor,
     block_own,
     block_other,
     edge_own,
     edge_other,
+    slots,
+    kept,
+    face,
+    to_band,
+    to_cross,
+    to_same,
+    total,
+    diff,
     forcing,
-    face,
-    centre,
-    east_part,
-    west_part,
-    north_part,
-    south_part,
     inverse,
     lower,
     ratio,
-    kept,
-    to_band,
-    to_cross,
-    to_same,
+    middle,
     state,
 ):
-    tracers = kept.shape[0]
-    band_levels, cols, rows = block_own.shape[1:]
-    levels = 2 * band_levels
+    tracers, count, cols, rows = kept.shape
+    levels = 2 * count
     band = where_am_i()
     place = sublane((cols, rows))
+    at = lane((cols, rows))
     outside = place == jnp.where(band == 0, cols - 1, 0)
-    zeros = tuple(jnp.zeros((cols, rows), jnp.float32) for _ in range(tracers))
-
-    def first_sweep(block, edge, first, carry):
-        def level(j, carry):
-            g = first + j
-            packed = edge[j]
-            force = forcing[g]
+    blocks = (block_own, block_other)
+    edges = (edge_own, edge_other)
+
+    def level_of(chain, i):
+        up = band == chain
+        g = jnp.where(up, i, levels - 1 - i)
+        return g, jnp.where(up, i, count - 1 - i)
+
+    def face_of(chain, i):
+        return face[i] if chain == 0 else to_band[count + i]
+
+    def assemble(i, carry):
+        for chain in range(2):
+            g, l = level_of(chain, i)
+            packed = edges[chain][l]
+            t, d, e = [
+                jnp.where(outside, turned(packed, -q), blocks[chain][q, l]) for q in range(3)
+            ]
+            total[g] = t
+            diff[g] = d
+            if chain == 0:
+                face[i] = e
+            else:
+                to_band[count + i] = e
+        return carry
+
+    lax.fori_loop(0, count, assemble, 0, unroll=UNROLL_A)
+
+    add_soundings(slots, total, forcing)
+
+    def coupling(chain, i):
+        return diff[jnp.where(band == chain, i, levels - 2 - i)]
+
+    zero = jnp.zeros((cols, rows), jnp.float32)
+
+    def both(group):
+        return [(chain, tr) for chain in range(2) for tr in group]
+
+    def first_sweep(group):
+        def level(i, carry):
             out = []
-            for tr in range(tracers):
-                a = jnp.where(outside, turned(packed, -3 - tr), block[4 + tr, j]) + force
-                now = a * inverse[tr, g] + lower[tr, g] * carry[tr]
-                state[tr, g] = now
+            for chain in range(2):
+                g, l = level_of(chain, i)
+                inward = coupling(chain, i)
+                outward = jnp.where(i > 0, coupling(chain, jnp.maximum(i - 1, 0)), 0.0)
+                force = forcing[g]
+                packed = edges[chain][l]
+                for tr in group:
+                    rest, before = carry[len(out)]
+                    k_in = factor[tr] * inward
+                    k_out = factor[tr] * outward
+                    left = 1.0 + k_out * rest
+                    inv = 1.0 / (left + k_in)
+                    low = k_out * inv
+                    a = jnp.where(outside, turned(packed, -3 - tr), blocks[chain][4 + tr, l])
+                    now = (a + force) * inv + low * before
+                    inverse[chain, tr, i] = inv
+                    lower[chain, tr, i] = low
+                    ratio[chain, tr, i] = k_in * inv
+                    state[chain, tr, i] = now
+                    out.append((left * inv, now))
+            return tuple(out)
+
+        start = tuple((zero, zero) for _ in both(group))
+        ends = lax.fori_loop(0, count, level, start, unroll=UNROLL_B)
+        for n, tr in enumerate(group):
+            near, far = ends[n][0], ends[n + len(group)][0]
+            middle[tr] = 1.0 / (near + ratio[0, tr, count - 1] * far)
+
+    def meet(group):
+        ends = []
+        for chain, tr in both(group):
+            mine, others = state[chain, tr, count - 1], state[1 - chain, tr, count - 1]
+            ends.append((mine + ratio[chain, tr, count - 1] * others) * middle[tr])
+        return tuple(ends)
+
+    def forward(group):
+        def level(i, carry):
+            out = []
+            for chain, tr in both(group):
+                now = (
+                    state[chain, tr, i] * inverse[chain, tr, i]
+                    + lower[chain, tr, i] * carry[len(out)]
+                )
+                state[chain, tr, i] = now
                 out.append(now)
             return tuple(out)
 
-        return lax.fori_loop(0, band_levels, level, carry, unroll=2)
-
-    @pl.when(band == 0)
-    def _():
-        carry = first_sweep(block_own, edge_own, 0, zeros)
-        first_sweep(block_other, edge_other, band_levels, carry)
-
-    @pl.when(band != 0)
-    def _():
-        carry = first_sweep(block_other, edge_other, 0, zeros)
-        first_sweep(block_own, edge_own, band_levels, carry)
-
-    def back_and_advect():
-        def level(i, carry):
-            g = levels - 1 - i
-            mid, e, w, n, s = centre[g], east_part[g], west_part[g], north_part[g], south_part[g]
+        lax.fori_loop(0, count, level, tuple(zero for _ in both(group)), unroll=UNROLL_C)
+
+    def backward(group):
+        ends = meet(group)
+        for n, (chain, tr) in enumerate(both(group)):
+            state[chain, tr, count - 1] = ends[n]
+
+        def level(step, carry):
+            i = count - 2 - step
             out = []
-            for tr in range(tracers):
-                a = state[tr, g] + ratio[tr, g] * carry[tr]
-                out.append(a)
-                along = e * pltpu.roll(a, cols - 1, 0) + w * pltpu.roll(a, 1, 0)
-                across = n * pltpu.roll(a, rows - 1, 1) + s * pltpu.roll(a, 1, 1)
-                state[tr, g] = mid * a + (along + across)
-            return tuple(out)
-
-        lax.fori_loop(0, levels, level, zeros, unroll=4)
-
-    def forward():
-        def level(g, carry):
-            out = []
-            for tr in range(tracers):
-                now = state[tr, g] * inverse[tr, g] + lower[tr, g] * carry[tr]
-                state[tr, g] = now
+            for chain, tr in both(group):
+                now = state[chain, tr, i] + ratio[chain, tr, i] * carry[len(out)]
+                state[chain, tr, i] = now
                 out.append(now)
             return tuple(out)
 
-        lax.fori_loop(0, levels, level, zeros, unroll=2)
-
-    def back():
-        def level(i, carry):
-            g = levels - 1 - i
-            out = []
+        lax.fori_loop(0, count - 1, level, ends, unroll=UNROLL_C)
+
+    def advect(i, carry):
+        for chain in range(2):
+            _, l = level_of(chain, i)
+            e = face_of(chain, i)
+            n = jnp.where(at == rows - 1, 0.0, blocks[chain][3, l])
+            to_east = jnp.maximum(e, 0.0)
+            to_west = jnp.minimum(pltpu.roll(e, 1, 0), 0.0)
+            to_north = jnp.maximum(n, 0.0)
+            to_south = jnp.minimum(pltpu.roll(n, 1, 1), 0.0)
+            centre = ((1.0 - to_east) + to_west) + (to_south - to_north)
             for tr in range(tracers):
-                now = state[tr, g] + ratio[tr, g] * carry[tr]
-                state[tr, g] = now
-                out.append(now)
-            return tuple(out)
-
-        lax.fori_loop(0, levels, level, zeros, unroll=4)
-
-    back_and_advect()
-    forward()
-    back()
-
-    half = band_levels // 2
-    own_first = band * band_levels
-    other_first = (1 - band) * band_levels
+                a = state[chain, tr, i]
+                along = to_east * pltpu.roll(a, cols - 1, 0) - to_west * pltpu.roll(a, 1, 0)
+                across = to_north * pltpu.roll(a, rows - 1, 1) - to_south * pltpu.roll(a, 1, 1)
+                state[chain, tr, i] = centre * a + (along + across)
+        return carry
+
+    groups = [range(tr, min(tr + GROUP, tracers)) for tr in range(0, tracers, GROUP)]
+    for group in groups:
+        first_sweep(group)
+    for group in groups:
+        backward(group)
+    lax.fori_loop(0, count, advect, 0, unroll=UNROLL_D)
+    for group in groups:
+        forward(group)
+    for group in groups:
+        backward(group)
+
     edge = jnp.where(band == 0, 0, cols - 1)
 
     def hand_out(j, carry):
-        for l in (j, j + half):
-            others = [state[tr, other_first + l] for tr in range(tracers)]
-            to_band[l] = packed_rows(others, jnp.where(band == 0, 0, cols - 2))
-            to_band[band_levels + l] = face[other_first + l]
+        for i in (2 * j, 2 * j + 1):
+            to_band[i] = packed_rows(
+                [state[1, tr, i] for tr in range(tracers)], jnp.where(band == 0, 0, cols - 2)
+            )
             for tr in range(tracers):
-                kept[tr, l] = state[tr, own_first + l]
-        for first, out in ((other_first, to_cross), (own_first, to_same)):
-            members = [state[tr, first + l] for l in (j, j + half) for tr in range(tracers)]
+                kept[tr, i] = state[0, tr, i]
+        for chain, out in ((1, to_cross), (0, to_same)):
+            members = [state[chain, tr, i] for i in (2 * j, 2 * j + 1) for tr in range(tracers)]
             out[j] = packed_lines(members, [edge])[0]
         return carry
 
-    lax.fori_loop(0, half, hand_out, 0)
-
-
-def finish_kernel(kept, from_band, from_cross, from_same, block, face, out):
-    tracers, band_levels, cols, rows = kept.shape
-    half = band_levels // 2
+    lax.fori_loop(0, count // 2, hand_out, 0)
+
+
+def finish_kernel(kept, from_band, block, face, inner, sides):
+    tracers, count, cols, rows = kept.shape
     band = where_am_i()
     place = sublane((cols, rows))
     at = lane((cols, rows))
     outside = (place >> 1) == jnp.where(band == 0, (cols - 2) >> 1, 0)
-    own_first = band * band_levels
+
+    def level(i, carry):
+        l = jnp.where(band == 0, i, count - 1 - i)
+        e = block[2, l]
+        n = jnp.where(at == rows - 1, 0.0, block[3, l])
+        before = jnp.where(band == 0, face[i], from_band[count + i])
+        w = pltpu.roll(jnp.where(place == cols - 1, before, e), 1, 0)
+        to_east = jnp.maximum(e, 0.0)
+        to_west = jnp.minimum(w, 0.0)
+        to_north = jnp.maximum(n, 0.0)
+        to_south = jnp.minimum(pltpu.roll(n, 1, 1), 0.0)
+        centre = ((1.0 - to_east) + to_west) + (to_south - to_north)
+        sides[i] = jnp.where(
+            place == cols - 1, to_east, jnp.where(place == 0, -to_west, 0.0)
+        )
+        to_east = jnp.where(place == cols - 1, 0.0, to_east)
+        to_west = jnp.where(place == 0, 0.0, to_west)
+        got = from_band[i]
+        for tr in range(tracers):
+            a = jnp.where(outside, unpacked_rows(got, tr), kept[tr, i])
+            along = to_east * pltpu.roll(a, cols - 1, 0) - to_west * pltpu.roll(a, 1, 0)
+            across = to_north * pltpu.roll(a, rows - 1, 1) - to_south * pltpu.roll(a, 1, 1)
+            inner[tr, l] = centre * a + (along + across)
+        return carry
+
+    lax.fori_loop(0, count, level, 0, unroll=2)
+
+
+def border_kernel(inner, sides, from_cross, from_same, out):
+    tracers, count, cols, rows = inner.shape
+    band = where_am_i()
+    place = sublane((cols, rows))
 
     def pair(j, carry):
         cross, same = from_cross[j], from_same[j]
         westward = jnp.where(band == 0, cross, same)
         eastward = jnp.where(band == 0, same, cross)
         for side in range(2):
-            l = j + side * half
-            e = block[2, l]
-            n = jnp.where(at == rows - 1, 0.0, block[3, l])
-            before = jnp.where(band == 0, face[own_first + l], from_band[band_levels + l])
-            w = pltpu.roll(jnp.where(place == cols - 1, before, e), 1, 0)
-            to_east = jnp.maximum(e, 0.0)
-            to_west = jnp.minimum(w, 0.0)
-            to_north = jnp.maximum(n, 0.0)
-            to_south = jnp.minimum(pltpu.roll(n, 1, 1), 0.0)
-            centre = ((1.0 - to_east) + to_west) + (to_south - to_north)
-            got = from_band[l]
+            i = 2 * j + side
+            l = jnp.where(band == 0, i, count - 1 - i)
             for tr in range(tracers):
                 q = tr + 4 * side
-                a = jnp.where(outside, unpacked_rows(got, tr), kept[tr, l])
-                a_east = jnp.where(
-                    place == cols - 1, turned(eastward, -1 - q), pltpu.roll(a, cols - 1, 0)
-                )
-                a_west = jnp.where(place == 0, turned(westward, 1 - q), pltpu.roll(a, 1, 0))
-                along = to_east * a_east - to_west * a_west
-                across = to_north * pltpu.roll(a, rows - 1, 1) - to_south * pltpu.roll(a, 1, 1)
-                out[tr, l] = centre * a + (along + across)
+                beyond = jnp.where(place == 0, turned(westward, 1 - q), turned(eastward, -1 - q))
+                out[tr, l] = inner[tr, l] + sides[i] * beyond
         return carry
 
-    lax.fori_loop(0, half, pair, 0)
+    lax.fori_loop(0, count // 2, pair, 0, unroll=2)
 
 
 def f32(*shape):
@@ -479,7 +493,6 @@
     blocks = sounding_cell.shape[0] // LANES
     field = f32(band_levels, cols, rows)
     deep = f32(levels, cols, rows)
-    full = f32(tracers, levels, cols, rows)
 
     first = call(first_kernel, [f32(8, LANES)], [], 10**9, 8)()[0]
     block, edge_same, edge_cross, message = call(
@@ -517,29 +530,26 @@
         message.reshape(2 * tiles, 4, LANES), both, split_axis=0, concat_axis=0, tiled=True
     ).reshape(tiles, 8, LANES)
 
-    forcing, face, *ready = call(
-        prepare_kernel,
-        [deep] * 7 + [full] * 3,
-        [pltpu.VMEM((levels, cols, rows), jnp.float32)] * 2,
+    part = f32(band_levels // 2, cols, rows)
+    whole = f32(tracers, band_levels, cols, rows)
+    chains = pltpu.VMEM((2, tracers, band_levels, cols, rows), jnp.float32)
+    kept, face, to_band, to_cross, to_same = call(
+        core_kernel,
+        [whole, field, deep, part, part],
+        [pltpu.VMEM((levels, cols, rows), jnp.float32)] * 3
+        + [chains] * 3
+        + [pltpu.VMEM((tracers, cols, rows), jnp.float32), chains],
         10**8,
         32,
         smem=1,
     )(tracer_factor, block, block_other, edge_own, edge_other, slots)
-
-    part = f32(band_levels // 2, cols, rows)
-    kept, to_band, to_cross, to_same = call(
-        solve_kernel,
-        [f32(tracers, band_levels, cols, rows), deep, part, part],
-        [pltpu.VMEM((tracers, levels, cols, rows), jnp.float32)],
-        10**7,
-        24,
-    )(block, block_other, edge_own, edge_other, forcing, face, *ready)
     from_cross = lax.ppermute(to_cross, both, cross)
     from_same = lax.ppermute(to_same, both, along)
     from_band = lax.ppermute(to_band, "band", swap)
-    return call(finish_kernel, [f32(tracers, band_levels, cols, rows)], [], 10**6, 16)(
-        kept, from_band, from_cross, from_same, block, face
-    )[0]
+    inner, sides = call(finish_kernel, [whole, field], [], 10**7, 16)(
+        kept, from_band, block, face
+    )
+    return call(border_kernel, [whole], [], 10**6, 16)(inner, sides, from_cross, from_same)[0]
 
 
 def solution(mesh):

time: 36.9 us -> 34.7 us (0.940)
  Pallas kernels: 10.2 us -> 8.85 us
  waiting for transfers between devices: 4.58 us -> 3.66 us
    pallas_call x5, Pallas kernels: 10.2 us -> 8.85 us  [run(): pl.pallas_call(kernel, out_shape=outs, in_specs=[scalars] * smem + [pl.Bl...]
    ppermute x1, waiting for transfers between devices: 4.34 us -> 3.42 us  [per_device(): from_cross = lax.ppermute(to_cross, both, cross)]
  transfers between devices with their start and end apart: 6 -> 6, of which waited for: 2 -> 2; matrix products, arithmetic and copies ran while one was open for 0% -> 0% of each run, Pallas kernels for 0% -> 3%
where the time goes in v4:
time: 34.7 us; the launch traced here: 34.2 us
  starting transfers between devices  10.9 us (31%)
  blocking collectives  9.09 us (26%)
  Pallas kernels  8.85 us (26%)
  waiting for transfers between devices  3.66 us (11%)
  local copies, waits for them, and re-layouts  1.67 us (5%)
    all_to_all x1, blocking collectives, per_device(): lax.all_to_all(message.reshape(2 * tiles, 4, LANES), both, split_axis=0,...  9.09 us
    pallas_call x5, Pallas kernels, run(): pl.pallas_call(kernel, out_shape=outs, in_specs=[scalars] * smem + [pl.Bl...  8.85 us
    ppermute x1, starting transfers between devices, per_device(): edge_other = lax.ppermute(edge_cross, both, cross)  4.3 us
    ppermute x1, waiting for transfers between devices, per_device(): from_cross = lax.ppermute(to_cross, both, cross)  3.42 us
    ppermute x1, starting transfers between devices, per_device(): from_cross = lax.ppermute(to_cross, both, cross)  3.25 us
    ppermute x1, starting transfers between devices, per_device(): edge_own = lax.ppermute(edge_same, both, same)  2.55 us
    unnamed x20, local copies, waits for them, and re-layouts  1.67 us
  transfers between devices with their start and end apart: 6, of which 2 were waited for; matrix products, arithmetic and copies ran while one was open for 0% of the time, Pallas kernels for 3%

profile of v4, /device:TPU:0, one launch (start us, length us, event | category | flops | bytes accessed | tf_op | source)
XLA Modules:
  0.0 34.2 jit_solution(18443813356589252929)
XLA Ops:
  0.1 0.0 copy-start.9
  0.1 0.6 %copy-done.5 = f32[256,12]{0,1:T(8,128)S(1)} copy-done((f32[256,12]{0,1:T(8,128)S(1)}, f32[256,12]{0,1:T(8,128)}, u32[]{:S(2)}) %copy-start.5) | copy-done | bytes 12312
  0.7 0.0 copy-done.6
  0.7 0.3 copy-done.4
  1.0 0.1 copy-done.3
  1.1 0.1 copy-done.2
  1.2 0.3 copy-done.1
  1.5 0.2 copy-done
  1.7 1.2 %shard_map.101 = (f32[8,12,8,512]{3,2,1,0:T(8,128)S(1)}, f32[12,8,512]{2,1,0:T(8,128)S(1)}, f32[12,8,512]{2,1,0:T(8,128)S(1)}, f32[16,8,128]{2,1,0:T(8,128)S(1)}) custom-call(f32[8,128]{1,0:T(8,128)S(1)} %shard_map.100.first, f32[4,12,8,512]{3,2,1,0:T(8,128)S(1)} %copy-done, f32[4,12,8,512]{3,2,1,0:T(8,128)S(1)} %copy-done.1, f32[12,8,512]{2,1,0:T(8,128)S(1)} %copy-done.2, ...), custom_call_target="tpu_custom_call" | custom-call | flops 1000000 | bytes 4213760 | tf_op jit(solution)/shard_map/pallas_call | solution.py:465
  3.0 0.5 %collective-permute-start = (f32[8,12,8,512]{3,2,1,0:T(8,128)S(1)}, f32[8,12,8,512]{3,2,1,0:T(8,128)S(1)}, u32[]{:S(2)}, u32[]{:S(2)}) collective-permute-start(f32[8,12,8,512]{3,2,1,0:T(8,128)S(1)} %get-tuple-element.16.block_own.block), channel_id=1, source_target_pairs={{0,1},{1,0},{2,3},{3,2},{4,5},{5,4},{6,7},{7,6},{8,9},{9,8},{10,11... | collective-permute-start | bytes 4718600 | tf_op jit(solution)/shard_map/ppermute | solution.py:528
  3.5 2.6 %collective-permute-start.1 = (f32[12,8,512]{2,1,0:T(8,128)S(1)}, f32[12,8,512]{2,1,0:T(8,128)S(1)}, u32[]{:S(2)}, u32[]{:S(2)}) collective-permute-start(f32[12,8,512]{2,1,0:T(8,128)S(1)} %get-tuple-element.17), channel_id=1, source_target_pairs={{0,2},{2,4},{4,6},{6,8},{8,10},{10,12},{12,14},{14,16},{16,18},{18... | collective-permute-start | bytes 589832 | tf_op jit(solution)/shard_map/ppermute | solution.py:526
  6.0 4.3 %collective-permute-start.2 = (f32[12,8,512]{2,1,0:T(8,128)S(1)}, f32[12,8,512]{2,1,0:T(8,128)S(1)}, u32[]{:S(2)}, u32[]{:S(2)}) collective-permute-start(f32[12,8,512]{2,1,0:T(8,128)S(1)} %get-tuple-element.18), channel_id=1, source_target_pairs={{1,2},{3,4},{5,6},{7,8},{9,10},{11,12},{13,14},{15,16},{17,18},{19... | collective-permute-start | bytes 589832 | tf_op jit(solution)/shard_map/ppermute | solution.py:527
  10.3 9.1 %all_to_all.5 = f32[32,4,128]{2,1,0:T(4,128)S(1)} all-to-all(f32[32,4,128]{2,1,0:T(4,128)S(1)} %bitcast.7), channel_id=1, replica_groups=mesh['tile'=16,'band'=2] {'tile','band'}, dimensions={0} | all-to-all | bytes 131072 | tf_op jit(solution)/shard_map/all_to_all | solution.py:529
  19.4 0.0 collective-permute-done.1.edge_own
  19.4 0.0 collective-permute-done.2.edge_other
  19.4 5.7 %shard_map.102 = (f32[4,12,8,512]{3,2,1,0:T(8,128)S(1)}, f32[12,8,512]{2,1,0:T(8,128)S(1)}, f32[24,8,512]{2,1,0:T(8,128)S(1)}, f32[6,8,512]{2,1,0:T(8,128)S(1)}, f32[6,8,512]{2,1,0:T(8,128)S(1)}) custom-call(f32[4]{0:T(128)S(1)} %copy-done.9, f32[8,12,8,512]{3,2,1,0:T(8,128)S(1)} %get-tuple-element.16.block_own.block, ...), custom_call_target="tpu_custom_call" | custom-call | flops 100000000 | bytes 5177360 | tf_op jit(solution)/shard_map/pallas_call | solution.py:465
  25.1 0.2 collective-permute-start.3
  25.3 3.3 %collective-permute-start.4 = (f32[6,8,512]{2,1,0:T(8,128)S(1)}, f32[6,8,512]{2,1,0:T(8,128)S(1)}, u32[]{:S(2)}, u32[]{:S(2)}) collective-permute-start(f32[6,8,512]{2,1,0:T(8,128)S(1)} %get-tuple-element.25), channel_id=1, source_target_pairs={{1,2},{3,4},{5,6},{7,8},{9,10},{11,12},{13,14},{15,16},{17,18},{19... | collective-permute-start | bytes 294920 | tf_op jit(solution)/shard_map/ppermute | solution.py:546
  28.5 0.0 collective-permute-start.5
  28.6 0.0 collective-permute-done.3.from_band
  28.6 0.9 %shard_map.103 = (f32[4,12,8,512]{3,2,1,0:T(8,128)S(1)}, f32[12,8,512]{2,1,0:T(8,128)S(1)}) custom-call(f32[4,12,8,512]{3,2,1,0:T(8,128)S(1)} %get-tuple-element.20.kept, f32[24,8,512]{2,1,0:T(8,128)S(1)} %collective-permute-done.3.from_band, f32[8,12,8,512]{3,2,1,0:T(8,128)S(1)} %get-tuple-element.16.block_own.block, f32[12,8,512]{2,1,0:T(8,128)S(1)} %get-tuple-element.22.face), custom_call_target="tpu_custom_call" | custom-call | flops 10000000 | bytes 3932160 | tf_op jit(solution)/shard_map/pallas_call | solution.py:465
  29.5 3.4 %collective-permute-done.4.from_cross = f32[6,8,512]{2,1,0:T(8,128)S(1)} collective-permute-done((f32[6,8,512]{2,1,0:T(8,128)S(1)}, f32[6,8,512]{2,1,0:T(8,128)S(1)}, u32[]{:S(2)}, u32[]{:S(2)}) %collective-permute-start.4) | collective-permute-done | bytes 98336 | tf_op jit(solution)/shard_map/ppermute | solution.py:546
  32.9 0.2 collective-permute-done.5.from_same
  33.2 1.1 %shard_map.104 = f32[4,12,8,512]{3,2,1,0:T(8,128)} custom-call(f32[4,12,8,512]{3,2,1,0:T(8,128)S(1)} %get-tuple-element.23.inner, f32[12,8,512]{2,1,0:T(8,128)S(1)} %get-tuple-element.24.sides, f32[6,8,512]{2,1,0:T(8,128)S(1)} %collective-permute-done.4.from_cross, f32[6,8,512]{2,1,0:T(8,128)S(1)} %collective-permute-done.5.from_same), custom_call_target="tpu_custom_call" | custom-call | flops 1000000 | bytes 1966080 | tf_op jit(solution)/shard_map/pallas_call | solution.py:465
  (14 shorter events, 0.0 us)
Async XLA Ops:
  0.0 0.7 %copy-start.5 = (f32[256,12]{0,1:T(8,128)S(1)}, f32[256,12]{0,1:T(8,128)}, u32[]{:S(2)}) copy-start(f32[256,12]{0,1:T(8,128)} %param.19) | copy-start | bytes 36868
  0.0 0.7 %copy-start.8 = (f32[256]{0:T(256)S(1)}, f32[256]{0:T(256)}, u32[]{:S(2)}) copy-start(f32[256]{0:T(256)} %param.18) | copy-start | bytes 3076
  0.0 0.7 %copy-start.7 = (f32[256]{0:T(256)S(1)}, f32[256]{0:T(256)}, u32[]{:S(2)}) copy-start(f32[256]{0:T(256)} %param.17) | copy-start | bytes 3076
  0.0 0.7 %copy-start.6 = (s32[256]{0:T(256)S(1)}, s32[256]{0:T(256)}, u32[]{:S(2)}) copy-start(s32[256]{0:T(256)} %param.16) | copy-start | bytes 3076
  0.0 1.0 %copy-start.4 = (f32[12,8,512]{2,1,0:T(8,128)S(1)}, f32[12,8,512]{2,1,0:T(8,128)}, u32[]{:S(2)}) copy-start(f32[12,8,512]{2,1,0:T(8,128)} %diff.1) | copy-start | bytes 589828
  0.0 1.1 %copy-start.3 = (f32[12,8,512]{2,1,0:T(8,128)S(1)}, f32[12,8,512]{2,1,0:T(8,128)}, u32[]{:S(2)}) copy-start(f32[12,8,512]{2,1,0:T(8,128)} %north.1) | copy-start | bytes 589828
  0.0 1.2 %copy-start.2 = (f32[12,8,512]{2,1,0:T(8,128)S(1)}, f32[12,8,512]{2,1,0:T(8,128)}, u32[]{:S(2)}) copy-start(f32[12,8,512]{2,1,0:T(8,128)} %east.1) | copy-start | bytes 589828
  0.0 1.5 %copy-start.1 = (f32[4,12,8,512]{3,2,1,0:T(8,128)S(1)}, f32[4,12,8,512]{3,2,1,0:T(8,128)}, u32[]{:S(2)}) copy-start(f32[4,12,8,512]{3,2,1,0:T(8,128)} %adj.1) | copy-start | bytes 2359300
  0.0 1.7 %copy-start = (f32[4,12,8,512]{3,2,1,0:T(8,128)S(1)}, f32[4,12,8,512]{3,2,1,0:T(8,128)}, u32[]{:S(2)}) copy-start(f32[4,12,8,512]{3,2,1,0:T(8,128)} %conc.1) | copy-start | bytes 2359300
  0.1 19.4 %copy-start.9 = (f32[4]{0:T(128)S(1)}, f32[4]{0:T(128)}, u32[]{:S(2)}) copy-start(f32[4]{0:T(128)} %factor.1) | copy-start | bytes 52
  3.0 16.5 %collective-permute-start = (f32[8,12,8,512]{3,2,1,0:T(8,128)S(1)}, f32[8,12,8,512]{3,2,1,0:T(8,128)S(1)}, u32[]{:S(2)}, u32[]{:S(2)}) collective-permute-start(f32[8,12,8,512]{3,2,1,0:T(8,128)S(1)} %get-tuple-element.16.block_own.block), channel_id=1, source_target_pairs={{0,1},{1,0},{2,3},{3,2},{4,5},{5,4},{6,7},{7,6},{8,9},{9,8},{10,11... | collective-permute-start | bytes 4718600 | tf_op jit(solution)/shard_map/ppermute | solution.py:528
  3.5 15.9 %collective-permute-start.1 = (f32[12,8,512]{2,1,0:T(8,128)S(1)}, f32[12,8,512]{2,1,0:T(8,128)S(1)}, u32[]{:S(2)}, u32[]{:S(2)}) collective-permute-start(f32[12,8,512]{2,1,0:T(8,128)S(1)} %get-tuple-element.17), channel_id=1, source_target_pairs={{0,2},{2,4},{4,6},{6,8},{8,10},{10,12},{12,14},{14,16},{16,18},{18... | collective-permute-start | bytes 589832 | tf_op jit(solution)/shard_map/ppermute | solution.py:526
  6.0 13.4 %collective-permute-start.2 = (f32[12,8,512]{2,1,0:T(8,128)S(1)}, f32[12,8,512]{2,1,0:T(8,128)S(1)}, u32[]{:S(2)}, u32[]{:S(2)}) collective-permute-start(f32[12,8,512]{2,1,0:T(8,128)S(1)} %get-tuple-element.18), channel_id=1, source_target_pairs={{1,2},{3,4},{5,6},{7,8},{9,10},{11,12},{13,14},{15,16},{17,18},{19... | collective-permute-start | bytes 589832 | tf_op jit(solution)/shard_map/ppermute | solution.py:527
  25.1 3.5 %collective-permute-start.3 = (f32[24,8,512]{2,1,0:T(8,128)S(1)}, f32[24,8,512]{2,1,0:T(8,128)S(1)}, u32[]{:S(2)}, u32[]{:S(2)}) collective-permute-start(f32[24,8,512]{2,1,0:T(8,128)S(1)} %get-tuple-element.21), channel_id=1, source_target_pairs={{0,1},{1,0},{2,3},{3,2},{4,5},{5,4},{6,7},{7,6},{8,9},{9,8},{10,11... | collective-permute-start | bytes 1179656 | tf_op jit(solution)/shard_map/ppermute | solution.py:548
  25.3 7.6 %collective-permute-start.4 = (f32[6,8,512]{2,1,0:T(8,128)S(1)}, f32[6,8,512]{2,1,0:T(8,128)S(1)}, u32[]{:S(2)}, u32[]{:S(2)}) collective-permute-start(f32[6,8,512]{2,1,0:T(8,128)S(1)} %get-tuple-element.25), channel_id=1, source_target_pairs={{1,2},{3,4},{5,6},{7,8},{9,10},{11,12},{13,14},{15,16},{17,18},{19... | collective-permute-start | bytes 294920 | tf_op jit(solution)/shard_map/ppermute | solution.py:546
  28.5 4.6 %collective-permute-start.5 = (f32[6,8,512]{2,1,0:T(8,128)S(1)}, f32[6,8,512]{2,1,0:T(8,128)S(1)}, u32[]{:S(2)}, u32[]{:S(2)}) collective-permute-start(f32[6,8,512]{2,1,0:T(8,128)S(1)} %get-tuple-element.26), channel_id=1, source_target_pairs={{1,3},{3,5},{5,7},{7,9},{9,11},{11,13},{13,15},{15,17},{17,19},{19... | collective-permute-start | bytes 294920 | tf_op jit(solution)/shard_map/ppermute | solution.py:547

commit v5 on v4

--- a/solution.py
+++ b/solution.py
@@ -12,11 +12,11 @@
 PAIR = 32
 HALF = 16
 MIB = 1 << 20
-GROUP = 2
+GROUP = 4
 UNROLL_A = 2
-UNROLL_B = 2
+UNROLL_B = 4
 UNROLL_C = 2
-UNROLL_D = 1
+UNROLL_D = 6
 
 
 def where_am_i():
@@ -150,17 +150,16 @@
         copy.wait()
 
 
-def three_parts(x):
+def two_parts(x):
     first = x.astype(jnp.bfloat16)
     rest = x - first.astype(jnp.float32)
     second = rest.astype(jnp.bfloat16)
-    third = (rest - second.astype(jnp.float32)).astype(jnp.bfloat16)
-    return first, second, third
-
-
-def exact_dot(x, onehot, dims):
+    return first, second
+
+
+def onehot_dot(x, onehot, dims):
     out = None
-    for part in three_parts(x):
+    for part in two_parts(x):
         term = lax.dot_general(part, onehot, (dims, ((), ())), preferred_element_type=jnp.float32)
         out = term if out is None else out + term
     return out
@@ -199,14 +198,14 @@
         for g in range(levels):
             side, l = g // band_levels, g % band_levels
             weights.append(fields[l // 4][4 * side + l % 4 : 4 * side + l % 4 + 1])
-        picked = exact_dot(total[...].reshape(levels * cols, rows), onehot, ((1,), (0,)))
+        picked = onehot_dot(total[...].reshape(levels * cols, rows), onehot, ((1,), (0,)))
         mean = weights[0] * picked[0:cols]
         for g in range(1, levels):
             mean = mean + weights[g] * picked[g * cols : (g + 1) * cols]
         mean = jnp.sum(mean * on_column, axis=0, keepdims=True)
         misfit = (precision * (mean - value)) * on_column
         spread = jnp.concatenate([weights[g] * misfit for g in range(levels)], axis=0)
-        added = exact_dot(spread, onehot, ((1,), (1,)))
+        added = onehot_dot(spread, onehot, ((1,), (1,)))
         return added.reshape(levels, cols, rows)
 
     forcing[...] = soundings(0)

time: 34.7 us -> 33.5 us (0.965)
  Pallas kernels: 8.85 us -> 7.65 us
    pallas_call x5, Pallas kernels: 8.85 us -> 7.65 us  [run(): pl.pallas_call(kernel, out_shape=outs, in_specs=[scalars] * smem + [pl.Bl...]
where the time goes in v5:
time: 33.5 us; the launch traced here: 33 us
  starting transfers between devices  10.8 us (32%)
  blocking collectives  9.09 us (27%)
  Pallas kernels  7.65 us (23%)
  waiting for transfers between devices  3.66 us (11%)
  local copies, waits for them, and re-layouts  1.67 us (5%)
    all_to_all x1, blocking collectives, per_device(): lax.all_to_all(message.reshape(2 * tiles, 4, LANES), both, split_axis=0,...  9.09 us
    pallas_call x5, Pallas kernels, run(): pl.pallas_call(kernel, out_shape=outs, in_specs=[scalars] * smem + [pl.Bl...  7.65 us
    ppermute x1, starting transfers between devices, per_device(): edge_other = lax.ppermute(edge_cross, both, cross)  4.3 us
    ppermute x1, waiting for transfers between devices, per_device(): from_cross = lax.ppermute(to_cross, both, cross)  3.42 us
    ppermute x1, starting transfers between devices, per_device(): from_cross = lax.ppermute(to_cross, both, cross)  3.25 us
    ppermute x1, starting transfers between devices, per_device(): edge_own = lax.ppermute(edge_same, both, same)  2.55 us
    unnamed x20, local copies, waits for them, and re-layouts  1.67 us
  transfers between devices with their start and end apart: 6, of which 2 were waited for; matrix products, arithmetic and copies ran while one was open for 0% of the time, Pallas kernels for 3%

profile of v5, /device:TPU:0, one launch (start us, length us, event | category | flops | bytes accessed | tf_op | source)
XLA Modules:
  0.0 33.0 jit_solution(6114463615974319996)
XLA Ops:
  0.1 0.0 copy-start.9
  0.1 0.6 %copy-done.5 = f32[256,12]{0,1:T(8,128)S(1)} copy-done((f32[256,12]{0,1:T(8,128)S(1)}, f32[256,12]{0,1:T(8,128)}, u32[]{:S(2)}) %copy-start.5) | copy-done | bytes 12312
  0.7 0.0 copy-done.6
  0.7 0.3 copy-done.4
  1.0 0.1 copy-done.3
  1.1 0.1 copy-done.2
  1.2 0.3 copy-done.1
  1.5 0.2 copy-done
  1.7 1.2 %shard_map.101 = (f32[8,12,8,512]{3,2,1,0:T(8,128)S(1)}, f32[12,8,512]{2,1,0:T(8,128)S(1)}, f32[12,8,512]{2,1,0:T(8,128)S(1)}, f32[16,8,128]{2,1,0:T(8,128)S(1)}) custom-call(f32[8,128]{1,0:T(8,128)S(1)} %shard_map.100.first, f32[4,12,8,512]{3,2,1,0:T(8,128)S(1)} %copy-done, f32[4,12,8,512]{3,2,1,0:T(8,128)S(1)} %copy-done.1, f32[12,8,512]{2,1,0:T(8,128)S(1)} %copy-done.2, ...), custom_call_target="tpu_custom_call" | custom-call | flops 1000000 | bytes 4213760 | tf_op jit(solution)/shard_map/pallas_call | solution.py:464
  3.0 0.5 %collective-permute-start = (f32[8,12,8,512]{3,2,1,0:T(8,128)S(1)}, f32[8,12,8,512]{3,2,1,0:T(8,128)S(1)}, u32[]{:S(2)}, u32[]{:S(2)}) collective-permute-start(f32[8,12,8,512]{3,2,1,0:T(8,128)S(1)} %get-tuple-element.16.block_own.block), channel_id=1, source_target_pairs={{0,1},{1,0},{2,3},{3,2},{4,5},{5,4},{6,7},{7,6},{8,9},{9,8},{10,11... | collective-permute-start | bytes 4718600 | tf_op jit(solution)/shard_map/ppermute | solution.py:527
  3.5 2.6 %collective-permute-start.1 = (f32[12,8,512]{2,1,0:T(8,128)S(1)}, f32[12,8,512]{2,1,0:T(8,128)S(1)}, u32[]{:S(2)}, u32[]{:S(2)}) collective-permute-start(f32[12,8,512]{2,1,0:T(8,128)S(1)} %get-tuple-element.17), channel_id=1, source_target_pairs={{0,2},{2,4},{4,6},{6,8},{8,10},{10,12},{12,14},{14,16},{16,18},{18... | collective-permute-start | bytes 589832 | tf_op jit(solution)/shard_map/ppermute | solution.py:525
  6.0 4.3 %collective-permute-start.2 = (f32[12,8,512]{2,1,0:T(8,128)S(1)}, f32[12,8,512]{2,1,0:T(8,128)S(1)}, u32[]{:S(2)}, u32[]{:S(2)}) collective-permute-start(f32[12,8,512]{2,1,0:T(8,128)S(1)} %get-tuple-element.18), channel_id=1, source_target_pairs={{1,2},{3,4},{5,6},{7,8},{9,10},{11,12},{13,14},{15,16},{17,18},{19... | collective-permute-start | bytes 589832 | tf_op jit(solution)/shard_map/ppermute | solution.py:526
  10.3 9.1 %all_to_all.5 = f32[32,4,128]{2,1,0:T(4,128)S(1)} all-to-all(f32[32,4,128]{2,1,0:T(4,128)S(1)} %bitcast.7), channel_id=1, replica_groups=mesh['tile'=16,'band'=2] {'tile','band'}, dimensions={0} | all-to-all | bytes 131072 | tf_op jit(solution)/shard_map/all_to_all | solution.py:528
  19.4 0.0 collective-permute-done.1.edge_own
  19.4 0.0 collective-permute-done.2.edge_other
  19.4 4.5 %shard_map.102 = (f32[4,12,8,512]{3,2,1,0:T(8,128)S(1)}, f32[12,8,512]{2,1,0:T(8,128)S(1)}, f32[24,8,512]{2,1,0:T(8,128)S(1)}, f32[6,8,512]{2,1,0:T(8,128)S(1)}, f32[6,8,512]{2,1,0:T(8,128)S(1)}) custom-call(f32[4]{0:T(128)S(1)} %copy-done.9, f32[8,12,8,512]{3,2,1,0:T(8,128)S(1)} %get-tuple-element.16.block_own.block, ...), custom_call_target="tpu_custom_call" | custom-call | flops 100000000 | bytes 5177360 | tf_op jit(solution)/shard_map/pallas_call | solution.py:464
  23.9 0.2 collective-permute-start.3
  24.1 3.3 %collective-permute-start.4 = (f32[6,8,512]{2,1,0:T(8,128)S(1)}, f32[6,8,512]{2,1,0:T(8,128)S(1)}, u32[]{:S(2)}, u32[]{:S(2)}) collective-permute-start(f32[6,8,512]{2,1,0:T(8,128)S(1)} %get-tuple-element.25), channel_id=1, source_target_pairs={{1,2},{3,4},{5,6},{7,8},{9,10},{11,12},{13,14},{15,16},{17,18},{19... | collective-permute-start | bytes 294920 | tf_op jit(solution)/shard_map/ppermute | solution.py:545
  27.3 0.0 collective-permute-start.5
  27.4 0.0 collective-permute-done.3.from_band
  27.4 0.9 %shard_map.103 = (f32[4,12,8,512]{3,2,1,0:T(8,128)S(1)}, f32[12,8,512]{2,1,0:T(8,128)S(1)}) custom-call(f32[4,12,8,512]{3,2,1,0:T(8,128)S(1)} %get-tuple-element.20.kept, f32[24,8,512]{2,1,0:T(8,128)S(1)} %collective-permute-done.3.from_band, f32[8,12,8,512]{3,2,1,0:T(8,128)S(1)} %get-tuple-element.16.block_own.block, f32[12,8,512]{2,1,0:T(8,128)S(1)} %get-tuple-element.22.face), custom_call_target="tpu_custom_call" | custom-call | flops 10000000 | bytes 3932160 | tf_op jit(solution)/shard_map/pallas_call | solution.py:464
  28.3 3.4 %collective-permute-done.4.from_cross = f32[6,8,512]{2,1,0:T(8,128)S(1)} collective-permute-done((f32[6,8,512]{2,1,0:T(8,128)S(1)}, f32[6,8,512]{2,1,0:T(8,128)S(1)}, u32[]{:S(2)}, u32[]{:S(2)}) %collective-permute-start.4) | collective-permute-done | bytes 98336 | tf_op jit(solution)/shard_map/ppermute | solution.py:545
  31.7 0.2 collective-permute-done.5.from_same
  32.0 1.1 %shard_map.104 = f32[4,12,8,512]{3,2,1,0:T(8,128)} custom-call(f32[4,12,8,512]{3,2,1,0:T(8,128)S(1)} %get-tuple-element.23.inner, f32[12,8,512]{2,1,0:T(8,128)S(1)} %get-tuple-element.24.sides, f32[6,8,512]{2,1,0:T(8,128)S(1)} %collective-permute-done.4.from_cross, f32[6,8,512]{2,1,0:T(8,128)S(1)} %collective-permute-done.5.from_same), custom_call_target="tpu_custom_call" | custom-call | flops 1000000 | bytes 1966080 | tf_op jit(solution)/shard_map/pallas_call | solution.py:464
  (14 shorter events, 0.0 us)
Async XLA Ops:
  0.0 0.7 %copy-start.5 = (f32[256,12]{0,1:T(8,128)S(1)}, f32[256,12]{0,1:T(8,128)}, u32[]{:S(2)}) copy-start(f32[256,12]{0,1:T(8,128)} %param.19) | copy-start | bytes 36868
  0.0 0.7 %copy-start.8 = (f32[256]{0:T(256)S(1)}, f32[256]{0:T(256)}, u32[]{:S(2)}) copy-start(f32[256]{0:T(256)} %param.18) | copy-start | bytes 3076
  0.0 0.7 %copy-start.7 = (f32[256]{0:T(256)S(1)}, f32[256]{0:T(256)}, u32[]{:S(2)}) copy-start(f32[256]{0:T(256)} %param.17) | copy-start | bytes 3076
  0.0 0.7 %copy-start.6 = (s32[256]{0:T(256)S(1)}, s32[256]{0:T(256)}, u32[]{:S(2)}) copy-start(s32[256]{0:T(256)} %param.16) | copy-start | bytes 3076
  0.0 1.0 %copy-start.4 = (f32[12,8,512]{2,1,0:T(8,128)S(1)}, f32[12,8,512]{2,1,0:T(8,128)}, u32[]{:S(2)}) copy-start(f32[12,8,512]{2,1,0:T(8,128)} %diff.1) | copy-start | bytes 589828
  0.0 1.1 %copy-start.3 = (f32[12,8,512]{2,1,0:T(8,128)S(1)}, f32[12,8,512]{2,1,0:T(8,128)}, u32[]{:S(2)}) copy-start(f32[12,8,512]{2,1,0:T(8,128)} %north.1) | copy-start | bytes 589828
  0.0 1.2 %copy-start.2 = (f32[12,8,512]{2,1,0:T(8,128)S(1)}, f32[12,8,512]{2,1,0:T(8,128)}, u32[]{:S(2)}) copy-start(f32[12,8,512]{2,1,0:T(8,128)} %east.1) | copy-start | bytes 589828
  0.0 1.5 %copy-start.1 = (f32[4,12,8,512]{3,2,1,0:T(8,128)S(1)}, f32[4,12,8,512]{3,2,1,0:T(8,128)}, u32[]{:S(2)}) copy-start(f32[4,12,8,512]{3,2,1,0:T(8,128)} %adj.1) | copy-start | bytes 2359300
  0.0 1.7 %copy-start = (f32[4,12,8,512]{3,2,1,0:T(8,128)S(1)}, f32[4,12,8,512]{3,2,1,0:T(8,128)}, u32[]{:S(2)}) copy-start(f32[4,12,8,512]{3,2,1,0:T(8,128)} %conc.1) | copy-start | bytes 2359300
  0.1 19.4 %copy-start.9 = (f32[4]{0:T(128)S(1)}, f32[4]{0:T(128)}, u32[]{:S(2)}) copy-start(f32[4]{0:T(128)} %factor.1) | copy-start | bytes 52
  3.0 16.5 %collective-permute-start = (f32[8,12,8,512]{3,2,1,0:T(8,128)S(1)}, f32[8,12,8,512]{3,2,1,0:T(8,128)S(1)}, u32[]{:S(2)}, u32[]{:S(2)}) collective-permute-start(f32[8,12,8,512]{3,2,1,0:T(8,128)S(1)} %get-tuple-element.16.block_own.block), channel_id=1, source_target_pairs={{0,1},{1,0},{2,3},{3,2},{4,5},{5,4},{6,7},{7,6},{8,9},{9,8},{10,11... | collective-permute-start | bytes 4718600 | tf_op jit(solution)/shard_map/ppermute | solution.py:527
  3.5 15.9 %collective-permute-start.1 = (f32[12,8,512]{2,1,0:T(8,128)S(1)}, f32[12,8,512]{2,1,0:T(8,128)S(1)}, u32[]{:S(2)}, u32[]{:S(2)}) collective-permute-start(f32[12,8,512]{2,1,0:T(8,128)S(1)} %get-tuple-element.17), channel_id=1, source_target_pairs={{0,2},{2,4},{4,6},{6,8},{8,10},{10,12},{12,14},{14,16},{16,18},{18... | collective-permute-start | bytes 589832 | tf_op jit(solution)/shard_map/ppermute | solution.py:525
  6.0 13.4 %collective-permute-start.2 = (f32[12,8,512]{2,1,0:T(8,128)S(1)}, f32[12,8,512]{2,1,0:T(8,128)S(1)}, u32[]{:S(2)}, u32[]{:S(2)}) collective-permute-start(f32[12,8,512]{2,1,0:T(8,128)S(1)} %get-tuple-element.18), channel_id=1, source_target_pairs={{1,2},{3,4},{5,6},{7,8},{9,10},{11,12},{13,14},{15,16},{17,18},{19... | collective-permute-start | bytes 589832 | tf_op jit(solution)/shard_map/ppermute | solution.py:526
  23.9 3.5 %collective-permute-start.3 = (f32[24,8,512]{2,1,0:T(8,128)S(1)}, f32[24,8,512]{2,1,0:T(8,128)S(1)}, u32[]{:S(2)}, u32[]{:S(2)}) collective-permute-start(f32[24,8,512]{2,1,0:T(8,128)S(1)} %get-tuple-element.21), channel_id=1, source_target_pairs={{0,1},{1,0},{2,3},{3,2},{4,5},{5,4},{6,7},{7,6},{8,9},{9,8},{10,11... | collective-permute-start | bytes 1179656 | tf_op jit(solution)/shard_map/ppermute | solution.py:547
  24.1 7.6 %collective-permute-start.4 = (f32[6,8,512]{2,1,0:T(8,128)S(1)}, f32[6,8,512]{2,1,0:T(8,128)S(1)}, u32[]{:S(2)}, u32[]{:S(2)}) collective-permute-start(f32[6,8,512]{2,1,0:T(8,128)S(1)} %get-tuple-element.25), channel_id=1, source_target_pairs={{1,2},{3,4},{5,6},{7,8},{9,10},{11,12},{13,14},{15,16},{17,18},{19... | collective-permute-start | bytes 294920 | tf_op jit(solution)/shard_map/ppermute | solution.py:545
  27.3 4.6 %collective-permute-start.5 = (f32[6,8,512]{2,1,0:T(8,128)S(1)}, f32[6,8,512]{2,1,0:T(8,128)S(1)}, u32[]{:S(2)}, u32[]{:S(2)}) collective-permute-start(f32[6,8,512]{2,1,0:T(8,128)S(1)} %get-tuple-element.26), channel_id=1, source_target_pairs={{1,3},{3,5},{5,7},{7,9},{9,11},{11,13},{13,15},{15,17},{17,19},{19... | collective-permute-start | bytes 294920 | tf_op jit(solution)/shard_map/ppermute | solution.py:546

commit v6 on v5

--- a/solution.py
+++ b/solution.py
@@ -12,10 +12,7 @@
 PAIR = 32
 HALF = 16
 MIB = 1 << 20
-GROUP = 4
-UNROLL_A = 2
 UNROLL_B = 4
-UNROLL_C = 2
 UNROLL_D = 6
 
 
@@ -29,15 +26,6 @@
 
 def lane(shape):
     return lax.broadcasted_iota(jnp.int32, shape, len(shape) - 1)
-
-
-def packed_rows(members, base):
-    place = sublane(members[0].shape)
-    out = members[0]
-    for q in range(1, 4):
-        pick = (((place + 2 * q) & 7) >> 1) == (base >> 1)
-        out = jnp.where(pick, pltpu.roll(members[q], 8 - 2 * q, 0), out)
-    return out
 
 
 def packed_lines(members, columns):
@@ -55,10 +43,6 @@
 
 def turned(tile, by):
     return pltpu.roll(tile, by % 8, 0) if by % 8 else tile
-
-
-def unpacked_rows(packed, q):
-    return packed if q == 0 else pltpu.roll(packed, 2 * q, 0)
 
 
 def first_kernel(out):
@@ -218,216 +202,323 @@
         lax.fori_loop(1, sources // chunk, more, 0)
 
 
-def core_kernel(
+def face_parts(e, w, n):
+    to_east = jnp.maximum(e, 0.0)
+    to_west = jnp.minimum(w, 0.0)
+    to_north = jnp.maximum(n, 0.0)
+    to_south = jnp.minimum(pltpu.roll(n, 1, 1), 0.0)
+    centre = ((1.0 - to_east) + to_west) + (to_south - to_north)
+    return centre, to_east, to_west, to_north, to_south
+
+
+def advected(a, parts):
+    centre, to_east, to_west, to_north, to_south = parts
+    cols, rows = a.shape
+    along = to_east * pltpu.roll(a, cols - 1, 0) - to_west * pltpu.roll(a, 1, 0)
+    across = to_north * pltpu.roll(a, rows - 1, 1) - to_south * pltpu.roll(a, 1, 1)
+    return centre * a + (along + across)
+
+
+def chain_level(count, chain, i):
+    up = where_am_i() == chain
+    return jnp.where(up, i, 2 * count - 1 - i), jnp.where(up, i, count - 1 - i)
+
+
+def coupling_level(count, chain, i):
+    return jnp.where(where_am_i() == chain, i, 2 * count - 2 - i)
+
+
+class Columns:
+    def __init__(self, count, strengths, kinds, inverse, lower, ratio, middle, state):
+        self.count, self.strengths, self.kinds = count, strengths, kinds
+        self.inverse, self.lower, self.ratio = inverse, lower, ratio
+        self.middle, self.state = middle, state
+        self.zero = jnp.zeros(state.shape[3:], jnp.float32)
+
+    def both(self, members):
+        return [(chain, m) for chain in range(2) for m in range(members)]
+
+    def factorise_and_sweep(self, coupling, source):
+        def level(i, carry):
+            out = []
+            for chain in range(2):
+                inward = coupling(chain, i)
+                outward, pairs = carry[chain]
+                now = []
+                for m, amount in enumerate(source(chain, i)):
+                    rest, before = pairs[m]
+                    k_in = self.strengths[m] * inward[self.kinds[m]]
+                    k_out = self.strengths[m] * outward[self.kinds[m]]
+                    left = 1.0 + k_out * rest
+                    inv = 1.0 / (left + k_in)
+                    low = k_out * inv
+                    swept = amount * inv + low * before
+                    self.inverse[chain, m, i] = inv
+                    self.lower[chain, m, i] = low
+                    self.ratio[chain, m, i] = k_in * inv
+                    self.state[chain, m, i] = swept
+                    now.append((left * inv, swept))
+                out.append((tuple(inward), tuple(now)))
+            return tuple(out)
+
+        zero = self.zero
+        outward = tuple(zero for _ in range(max(self.kinds) + 1))
+        start = (outward, tuple((zero, zero) for _ in self.strengths))
+        ends = lax.fori_loop(0, self.count, level, (start, start), unroll=UNROLL_B)
+        for m in range(len(self.strengths)):
+            near, far = ends[0][1][m][0], ends[1][1][m][0]
+            self.middle[m] = 1.0 / (near + self.ratio[0, m, self.count - 1] * far)
+
+    def sweep(self, members):
+        every = self.both(members)
+
+        def level(i, carry):
+            out = []
+            for chain, m in every:
+                before = self.lower[chain, m, i] * carry[len(out)]
+                out.append(self.state[chain, m, i] * self.inverse[chain, m, i] + before)
+                self.state[chain, m, i] = out[-1]
+            return tuple(out)
+
+        lax.fori_loop(0, self.count, level, tuple(self.zero for _ in every), unroll=2)
+
+    def back(self, members):
+        last = self.count - 1
+        every = self.both(members)
+        ends = []
+        for chain, m in every:
+            mine, others = self.state[chain, m, last], self.state[1 - chain, m, last]
+            ends.append((mine + self.ratio[chain, m, last] * others) * self.middle[m])
+        for end, (chain, m) in zip(ends, every):
+            self.state[chain, m, last] = end
+
+        def level(step, carry):
+            i = last - 1 - step
+            out = []
+            for chain, m in every:
+                after = self.ratio[chain, m, i] * carry[len(out)]
+                out.append(self.state[chain, m, i] + after)
+                self.state[chain, m, i] = out[-1]
+            return tuple(out)
+
+        lax.fori_loop(0, last, level, tuple(ends), unroll=2)
+
+
+def boundary_kernel(
     factor,
     block_own,
     block_other,
     edge_own,
     edge_other,
     slots,
-    kept,
-    face,
-    to_band,
+    forcing,
+    outer,
     to_cross,
     to_same,
     total,
     diff,
-    forcing,
+    faces,
     inverse,
     lower,
     ratio,
     middle,
     state,
 ):
-    tracers, count, cols, rows = kept.shape
-    levels = 2 * count
+    count, cols, rows = block_own.shape[1:]
+    tracers = block_own.shape[0] - 4
     band = where_am_i()
     place = sublane((cols, rows))
     at = lane((cols, rows))
-    outside = place == jnp.where(band == 0, cols - 1, 0)
+    beyond = jnp.where(band == 0, cols - 1, 0)
+    outside = place == beyond
+    edge = cols - 1 - beyond
+    first = ((place - edge + 1) & 7) < 4
     blocks = (block_own, block_other)
     edges = (edge_own, edge_other)
 
-    def level_of(chain, i):
-        up = band == chain
-        g = jnp.where(up, i, levels - 1 - i)
-        return g, jnp.where(up, i, count - 1 - i)
-
-    def face_of(chain, i):
-        return face[i] if chain == 0 else to_band[count + i]
+    def joined(x, y):
+        return jnp.where(first, x, pltpu.roll(y, 4, 0))
 
     def assemble(i, carry):
         for chain in range(2):
-            g, l = level_of(chain, i)
+            g, l = chain_level(count, chain, i)
             packed = edges[chain][l]
             t, d, e = [
                 jnp.where(outside, turned(packed, -q), blocks[chain][q, l]) for q in range(3)
             ]
             total[g] = t
             diff[g] = d
-            if chain == 0:
-                face[i] = e
-            else:
-                to_band[count + i] = e
-        return carry
-
-    lax.fori_loop(0, count, assemble, 0, unroll=UNROLL_A)
+            faces[count * chain + i] = e
+        return carry
+
+    lax.fori_loop(0, count, assemble, 0, unroll=2)
 
     add_soundings(slots, total, forcing)
 
     def coupling(chain, i):
-        return diff[jnp.where(band == chain, i, levels - 2 - i)]
-
-    zero = jnp.zeros((cols, rows), jnp.float32)
-
-    def both(group):
-        return [(chain, tr) for chain in range(2) for tr in group]
-
-    def first_sweep(group):
-        def level(i, carry):
-            out = []
-            for chain in range(2):
-                g, l = level_of(chain, i)
-                inward = coupling(chain, i)
-                outward = jnp.where(i > 0, coupling(chain, jnp.maximum(i - 1, 0)), 0.0)
-                force = forcing[g]
-                packed = edges[chain][l]
-                for tr in group:
-                    rest, before = carry[len(out)]
-                    k_in = factor[tr] * inward
-                    k_out = factor[tr] * outward
-                    left = 1.0 + k_out * rest
-                    inv = 1.0 / (left + k_in)
-                    low = k_out * inv
-                    a = jnp.where(outside, turned(packed, -3 - tr), blocks[chain][4 + tr, l])
-                    now = (a + force) * inv + low * before
-                    inverse[chain, tr, i] = inv
-                    lower[chain, tr, i] = low
-                    ratio[chain, tr, i] = k_in * inv
-                    state[chain, tr, i] = now
-                    out.append((left * inv, now))
-            return tuple(out)
-
-        start = tuple((zero, zero) for _ in both(group))
-        ends = lax.fori_loop(0, count, level, start, unroll=UNROLL_B)
-        for n, tr in enumerate(group):
-            near, far = ends[n][0], ends[n + len(group)][0]
-            middle[tr] = 1.0 / (near + ratio[0, tr, count - 1] * far)
-
-    def meet(group):
-        ends = []
-        for chain, tr in both(group):
-            mine, others = state[chain, tr, count - 1], state[1 - chain, tr, count - 1]
-            ends.append((mine + ratio[chain, tr, count - 1] * others) * middle[tr])
-        return tuple(ends)
-
-    def forward(group):
-        def level(i, carry):
-            out = []
-            for chain, tr in both(group):
-                now = (
-                    state[chain, tr, i] * inverse[chain, tr, i]
-                    + lower[chain, tr, i] * carry[len(out)]
-                )
-                state[chain, tr, i] = now
-                out.append(now)
-            return tuple(out)
-
-        lax.fori_loop(0, count, level, tuple(zero for _ in both(group)), unroll=UNROLL_C)
-
-    def backward(group):
-        ends = meet(group)
-        for n, (chain, tr) in enumerate(both(group)):
-            state[chain, tr, count - 1] = ends[n]
-
-        def level(step, carry):
-            i = count - 2 - step
-            out = []
-            for chain, tr in both(group):
-                now = state[chain, tr, i] + ratio[chain, tr, i] * carry[len(out)]
-                state[chain, tr, i] = now
-                out.append(now)
-            return tuple(out)
-
-        lax.fori_loop(0, count - 1, level, ends, unroll=UNROLL_C)
+        d = diff[coupling_level(count, chain, i)]
+        return [joined(d, d)]
+
+    def source(chain, i):
+        g, l = chain_level(count, chain, i)
+        packed = edges[chain][l]
+        force = forcing[g]
+        amounts = [
+            jnp.where(outside, turned(packed, -3 - tr), blocks[chain][4 + tr, l]) + force
+            for tr in range(tracers)
+        ]
+        return [joined(amounts[tr], amounts[tr + 1]) for tr in range(0, tracers, 2)]
+
+    pairs = tracers // 2
+    strengths = [jnp.where(first, factor[2 * m], factor[2 * m + 1]) for m in range(pairs)]
+    columns = Columns(count, strengths, [0] * pairs, inverse, lower, ratio, middle, state)
 
     def advect(i, carry):
         for chain in range(2):
-            _, l = level_of(chain, i)
-            e = face_of(chain, i)
+            _, l = chain_level(count, chain, i)
+            e = faces[count * chain + i]
             n = jnp.where(at == rows - 1, 0.0, blocks[chain][3, l])
-            to_east = jnp.maximum(e, 0.0)
-            to_west = jnp.minimum(pltpu.roll(e, 1, 0), 0.0)
-            to_north = jnp.maximum(n, 0.0)
-            to_south = jnp.minimum(pltpu.roll(n, 1, 1), 0.0)
-            centre = ((1.0 - to_east) + to_west) + (to_south - to_north)
-            for tr in range(tracers):
-                a = state[chain, tr, i]
-                along = to_east * pltpu.roll(a, cols - 1, 0) - to_west * pltpu.roll(a, 1, 0)
-                across = to_north * pltpu.roll(a, rows - 1, 1) - to_south * pltpu.roll(a, 1, 1)
-                state[chain, tr, i] = centre * a + (along + across)
-        return carry
-
-    groups = [range(tr, min(tr + GROUP, tracers)) for tr in range(0, tracers, GROUP)]
-    for group in groups:
-        first_sweep(group)
-    for group in groups:
-        backward(group)
+            e, n = joined(e, e), joined(n, n)
+            parts = face_parts(e, pltpu.roll(e, 1, 0), n)
+            for m in range(pairs):
+                state[chain, m, i] = advected(state[chain, m, i], parts)
+        return carry
+
+    columns.factorise_and_sweep(coupling, source)
+    columns.back(pairs)
     lax.fori_loop(0, count, advect, 0, unroll=UNROLL_D)
-    for group in groups:
-        forward(group)
-    for group in groups:
-        backward(group)
-
-    edge = jnp.where(band == 0, 0, cols - 1)
+    columns.sweep(pairs)
+    columns.back(pairs)
 
     def hand_out(j, carry):
-        for i in (2 * j, 2 * j + 1):
-            to_band[i] = packed_rows(
-                [state[1, tr, i] for tr in range(tracers)], jnp.where(band == 0, 0, cols - 2)
-            )
-            for tr in range(tracers):
-                kept[tr, i] = state[0, tr, i]
         for chain, out in ((1, to_cross), (0, to_same)):
-            members = [state[chain, tr, i] for i in (2 * j, 2 * j + 1) for tr in range(tracers)]
-            out[j] = packed_lines(members, [edge])[0]
-        return carry
-
-    lax.fori_loop(0, count // 2, hand_out, 0)
-
-
-def finish_kernel(kept, from_band, block, face, inner, sides):
-    tracers, count, cols, rows = kept.shape
+            one = state[chain, 0, 2 * j]
+            for q, (m, side) in enumerate(((0, 0), (0, 1), (1, 0), (1, 1))):
+                if q:
+                    row = pltpu.roll(state[chain, m, 2 * j + side], q, 0)
+                    one = jnp.where(((place - edge) & 3) == q, row, one)
+            out[j] = one
+        return carry
+
+    lax.fori_loop(0, count // 2, hand_out, 0, unroll=2)
+
+    slot = (place - beyond) & 7
+
+    def hand_over(i, carry):
+        for chain in range(2):
+            g, l = chain_level(count, chain, i)
+            force = forcing[g]
+            row = jnp.where(band == 0, force[cols - 1 : cols], force[0:1])
+            tile = turned(edges[chain][l], -3)
+            tile = jnp.where(slot < tracers, tile + row, tile)
+            tile = jnp.where(slot == 4, turned(diff[coupling_level(count, chain, i)], 4), tile)
+            near = jnp.where(band == 0, turned(force, 4), turned(force, 6))
+            outer[count * chain + i] = jnp.where(slot == 5, near, tile)
+        return carry
+
+    lax.fori_loop(0, count, hand_over, 0, unroll=2)
+
+
+def column_kernel(
+    factor,
+    block_own,
+    block_other,
+    forcing,
+    outer,
+    outer_other,
+    inner,
+    sides,
+    inverse,
+    lower,
+    ratio,
+    middle,
+    state,
+):
+    tracers, count, cols, rows = inner.shape
     band = where_am_i()
     place = sublane((cols, rows))
     at = lane((cols, rows))
-    outside = (place >> 1) == jnp.where(band == 0, (cols - 2) >> 1, 0)
-
-    def level(i, carry):
-        l = jnp.where(band == 0, i, count - 1 - i)
-        e = block[2, l]
-        n = jnp.where(at == rows - 1, 0.0, block[3, l])
-        before = jnp.where(band == 0, face[i], from_band[count + i])
-        w = pltpu.roll(jnp.where(place == cols - 1, before, e), 1, 0)
-        to_east = jnp.maximum(e, 0.0)
-        to_west = jnp.minimum(w, 0.0)
-        to_north = jnp.maximum(n, 0.0)
-        to_south = jnp.minimum(pltpu.roll(n, 1, 1), 0.0)
-        centre = ((1.0 - to_east) + to_west) + (to_south - to_north)
+    beyond = jnp.where(band == 0, cols - 1, 0)
+    slot = (place - beyond) & 7
+    mine = slot < 4
+    blocks = (block_own, block_other)
+
+    def outers(chain, i):
+        return outer[count * chain + i], outer_other[count * (1 - chain) + i]
+
+    def coupling(chain, i):
+        up = band == chain
+        here = blocks[chain][1, jnp.where(up, i, jnp.maximum(count - 2 - i, 0))]
+        across = jnp.logical_and(jnp.logical_not(up), i == count - 1)
+        d = jnp.where(across, blocks[1 - chain][1, count - 1], here)
+        own, got = outers(chain, i)
+        d_own = jnp.where(band == 0, own[3:4], own[4:5])
+        d_got = jnp.where(band == 0, got[4:5], got[3:4])
+        return [d, jnp.where(mine, d_own, d_got)]
+
+    def source(chain, i):
+        g, l = chain_level(count, chain, i)
+        own, got = outers(chain, i)
+        force = jnp.where(
+            place == beyond, jnp.where(band == 0, turned(got, 2), turned(got, 4)), forcing[g]
+        )
+        moved = jnp.where(band == 0, turned(got, 3), turned(got, 5))
+        return [blocks[chain][4 + tr, l] + force for tr in range(tracers)] + [
+            jnp.where(mine, own, moved)
+        ]
+
+    by_row = factor[0]
+    for tr in range(1, tracers):
+        by_row = jnp.where((slot & 3) == tr, factor[tr], by_row)
+    strengths = [factor[tr] for tr in range(tracers)] + [by_row]
+    kinds = [0] * tracers + [1]
+    columns = Columns(count, strengths, kinds, inverse, lower, ratio, middle, state)
+
+    def parts_of(chain, i):
+        _, l = chain_level(count, chain, i)
+        own, got = outers(chain, i)
+        e = blocks[chain][2, l]
+        n = jnp.where(at == rows - 1, 0.0, blocks[chain][3, l])
+        before = turned(jnp.where(band == 0, own, got), 2)
+        return face_parts(e, jnp.where(place == 0, before, pltpu.roll(e, 1, 0)), n)
+
+    def advect(i, carry):
+        for chain in range(2):
+            centre, to_east, to_west, to_north, to_south = parts_of(chain, i)
+            around = state[chain, tracers, i]
+            west = jnp.where(band == 0, around, turned(around, 3))
+            east = jnp.where(band == 0, turned(around, 5), around)
+            for tr in range(tracers):
+                a = state[chain, tr, i]
+                a_east = jnp.where(
+                    place == cols - 1, turned(east, -1 - tr), pltpu.roll(a, cols - 1, 0)
+                )
+                a_west = jnp.where(place == 0, turned(west, 1 - tr), pltpu.roll(a, 1, 0))
+                along = to_east * a_east - to_west * a_west
+                across = to_north * pltpu.roll(a, rows - 1, 1) - to_south * pltpu.roll(a, 1, 1)
+                state[chain, tr, i] = centre * a + (along + across)
+        return carry
+
+    columns.factorise_and_sweep(coupling, source)
+    columns.back(tracers + 1)
+    lax.fori_loop(0, count, advect, 0, unroll=2)
+    columns.sweep(tracers)
+    columns.back(tracers)
+
+    def last(i, carry):
+        _, l = chain_level(count, 0, i)
+        centre, to_east, to_west, to_north, to_south = parts_of(0, i)
         sides[i] = jnp.where(
             place == cols - 1, to_east, jnp.where(place == 0, -to_west, 0.0)
         )
         to_east = jnp.where(place == cols - 1, 0.0, to_east)
         to_west = jnp.where(place == 0, 0.0, to_west)
-        got = from_band[i]
         for tr in range(tracers):
-            a = jnp.where(outside, unpacked_rows(got, tr), kept[tr, i])
-            along = to_east * pltpu.roll(a, cols - 1, 0) - to_west * pltpu.roll(a, 1, 0)
-            across = to_north * pltpu.roll(a, rows - 1, 1) - to_south * pltpu.roll(a, 1, 1)
-            inner[tr, l] = centre * a + (along + across)
-        return carry
-
-    lax.fori_loop(0, count, level, 0, unroll=2)
+            parts = (centre, to_east, to_west, to_north, to_south)
+            inner[tr, l] = advected(state[0, tr, i], parts)
+        return carry
+
+    lax.fori_loop(0, count, last, 0, unroll=3)
 
 
 def border_kernel(inner, sides, from_cross, from_same, out):
@@ -443,7 +534,7 @@
             i = 2 * j + side
             l = jnp.where(band == 0, i, count - 1 - i)
             for tr in range(tracers):
-                q = tr + 4 * side
+                q = 4 * (tr & 1) + 2 * (tr >> 1) + side
                 beyond = jnp.where(place == 0, turned(westward, 1 - q), turned(eastward, -1 - q))
                 out[tr, l] = inner[tr, l] + sides[i] * beyond
         return carry
@@ -455,20 +546,20 @@
     return jax.ShapeDtypeStruct(shape, jnp.float32)
 
 
-def call(kernel, outs, scratch, ops, limit, smem=0, space=pltpu.VMEM):
+def call(kernel, outs, scratch, ops, limit, smem=0, moved=None):
     vmem = pl.BlockSpec(memory_space=pltpu.VMEM)
     scalars = pl.BlockSpec(memory_space=pltpu.SMEM)
 
     def run(*args):
-        moved = sum(4 * a.size for a in args) + sum(4 * o.size for o in outs)
+        size = moved or sum(4 * a.size for a in args) + sum(4 * o.size for o in outs)
         return pl.pallas_call(
             kernel,
             out_shape=outs,
-            in_specs=[scalars] * smem + [pl.BlockSpec(memory_space=space)] * (len(args) - smem),
+            in_specs=[scalars] * smem + [vmem] * (len(args) - smem),
             out_specs=[vmem] * len(outs),
             scratch_shapes=scratch,
             compiler_params=pltpu.CompilerParams(vmem_limit_bytes=limit * MIB),
-            cost_estimate=pl.CostEstimate(flops=ops, bytes_accessed=moved, transcendentals=0),
+            cost_estimate=pl.CostEstimate(flops=ops, bytes_accessed=size, transcendentals=0),
         )(*args)
 
     return run
@@ -531,23 +622,25 @@
 
     part = f32(band_levels // 2, cols, rows)
     whole = f32(tracers, band_levels, cols, rows)
-    chains = pltpu.VMEM((2, tracers, band_levels, cols, rows), jnp.float32)
-    kept, face, to_band, to_cross, to_same = call(
-        core_kernel,
-        [whole, field, deep, part, part],
-        [pltpu.VMEM((levels, cols, rows), jnp.float32)] * 3
-        + [chains] * 3
-        + [pltpu.VMEM((tracers, cols, rows), jnp.float32), chains],
+
+    def room(members):
+        chains = pltpu.VMEM((2, members, band_levels, cols, rows), jnp.float32)
+        return [chains] * 3 + [pltpu.VMEM((members, cols, rows), jnp.float32), chains]
+
+    forcing, outer, to_cross, to_same = call(
+        boundary_kernel,
+        [deep, deep, part, part],
+        [pltpu.VMEM((levels, cols, rows), jnp.float32)] * 3 + room(tracers // 2),
         10**8,
-        32,
+        24,
         smem=1,
     )(tracer_factor, block, block_other, edge_own, edge_other, slots)
     from_cross = lax.ppermute(to_cross, both, cross)
     from_same = lax.ppermute(to_same, both, along)
-    from_band = lax.ppermute(to_band, "band", swap)
-    inner, sides = call(finish_kernel, [whole, field], [], 10**7, 16)(
-        kept, from_band, block, face
-    )
+    outer_other = lax.ppermute(outer, "band", swap)
+    inner, sides = call(
+        column_kernel, [whole, field], room(tracers + 1), 10**9, 24, smem=1
+    )(tracer_factor, block, block_other, forcing, outer, outer_other)
     return call(border_kernel, [whole], [], 10**6, 16)(inner, sides, from_cross, from_same)[0]
 
 

time: 33.5 us -> 32.6 us (0.973)
  waiting for transfers between devices: 3.66 us -> 0.02 us
  Pallas kernels: 7.65 us -> 10.6 us
    ppermute x1, waiting for transfers between devices: 3.42 us -> 0.01 us  [per_device(): from_cross = lax.ppermute(to_cross, both, cross)]
    pallas_call x5, Pallas kernels: 7.65 us -> 10.6 us  [run(): pl.pallas_call(kernel, out_shape=outs, in_specs=[scalars] * smem + [vmem]...]
  transfers between devices with their start and end apart: 6 -> 6, of which waited for: 2 -> 0; matrix products, arithmetic and copies ran while one was open for 0% -> 0% of each run, Pallas kernels for 3% -> 15%
where the time goes in v6:
time: 32.6 us; the launch traced here: 32.3 us
  starting transfers between devices  10.8 us (33%)
  Pallas kernels  10.6 us (33%)
  blocking collectives  9.09 us (28%)
  local copies, waits for them, and re-layouts  1.67 us (5%)
    pallas_call x5, Pallas kernels, run(): pl.pallas_call(kernel, out_shape=outs, in_specs=[scalars] * smem + [vmem]...  10.6 us
    all_to_all x1, blocking collectives, per_device(): lax.all_to_all(message.reshape(2 * tiles, 4, LANES), both, split_axis=0,...  9.09 us
    ppermute x1, starting transfers between devices, per_device(): edge_other = lax.ppermute(edge_cross, both, cross)  4.3 us
    ppermute x1, starting transfers between devices, per_device(): from_cross = lax.ppermute(to_cross, both, cross)  3.25 us
    ppermute x1, starting transfers between devices, per_device(): edge_own = lax.ppermute(edge_same, both, same)  2.55 us
    unnamed x20, local copies, waits for them, and re-layouts  1.67 us
  transfers between devices with their start and end apart: 6, of which 0 were waited for; matrix products, arithmetic and copies ran while one was open for 0% of the time, Pallas kernels for 15%

profile of v6, /device:TPU:0, one launch (start us, length us, event | category | flops | bytes accessed | tf_op | source)
XLA Modules:
  0.0 32.3 jit_solution(3567490170085477079)
XLA Ops:
  0.1 0.0 copy-start.6
  0.1 0.6 %copy-done.5 = f32[256,12]{0,1:T(8,128)S(1)} copy-done((f32[256,12]{0,1:T(8,128)S(1)}, f32[256,12]{0,1:T(8,128)}, u32[]{:S(2)}) %copy-start.5) | copy-done | bytes 12312
  0.7 0.0 copy-done.7
  0.7 0.3 copy-done.4
  1.0 0.1 copy-done.3
  1.1 0.1 copy-done.2
  1.2 0.3 copy-done.1
  1.5 0.2 copy-done
  1.7 1.2 %shard_map.101 = (f32[8,12,8,512]{3,2,1,0:T(8,128)S(1)}, f32[12,8,512]{2,1,0:T(8,128)S(1)}, f32[12,8,512]{2,1,0:T(8,128)S(1)}, f32[16,8,128]{2,1,0:T(8,128)S(1)}) custom-call(f32[8,128]{1,0:T(8,128)S(1)} %shard_map.100.first, f32[4,12,8,512]{3,2,1,0:T(8,128)S(1)} %copy-done, f32[4,12,8,512]{3,2,1,0:T(8,128)S(1)} %copy-done.1, f32[12,8,512]{2,1,0:T(8,128)S(1)} %copy-done.2, ...), custom_call_target="tpu_custom_call" | custom-call | flops 1000000 | bytes 4213760 | tf_op jit(solution)/shard_map/pallas_call | solution.py:555
  3.0 0.5 %collective-permute-start = (f32[8,12,8,512]{3,2,1,0:T(8,128)S(1)}, f32[8,12,8,512]{3,2,1,0:T(8,128)S(1)}, u32[]{:S(2)}, u32[]{:S(2)}) collective-permute-start(f32[8,12,8,512]{3,2,1,0:T(8,128)S(1)} %get-tuple-element.15.block_own), channel_id=1, source_target_pairs={{0,1},{1,0},{2,3},{3,2},{4,5},{5,4},{6,7},{7,6},{8,9},{9,8},{10,11... | collective-permute-start | bytes 4718600 | tf_op jit(solution)/shard_map/ppermute | solution.py:618
  3.5 2.6 %collective-permute-start.1 = (f32[12,8,512]{2,1,0:T(8,128)S(1)}, f32[12,8,512]{2,1,0:T(8,128)S(1)}, u32[]{:S(2)}, u32[]{:S(2)}) collective-permute-start(f32[12,8,512]{2,1,0:T(8,128)S(1)} %get-tuple-element.16), channel_id=1, source_target_pairs={{0,2},{2,4},{4,6},{6,8},{8,10},{10,12},{12,14},{14,16},{16,18},{18... | collective-permute-start | bytes 589832 | tf_op jit(solution)/shard_map/ppermute | solution.py:616
  6.0 4.3 %collective-permute-start.2 = (f32[12,8,512]{2,1,0:T(8,128)S(1)}, f32[12,8,512]{2,1,0:T(8,128)S(1)}, u32[]{:S(2)}, u32[]{:S(2)}) collective-permute-start(f32[12,8,512]{2,1,0:T(8,128)S(1)} %get-tuple-element.17), channel_id=1, source_target_pairs={{1,2},{3,4},{5,6},{7,8},{9,10},{11,12},{13,14},{15,16},{17,18},{19... | collective-permute-start | bytes 589832 | tf_op jit(solution)/shard_map/ppermute | solution.py:617
  10.3 9.1 %all_to_all.5 = f32[32,4,128]{2,1,0:T(4,128)S(1)} all-to-all(f32[32,4,128]{2,1,0:T(4,128)S(1)} %bitcast.7), channel_id=1, replica_groups=mesh['tile'=16,'band'=2] {'tile','band'}, dimensions={0} | all-to-all | bytes 131072 | tf_op jit(solution)/shard_map/all_to_all | solution.py:619
  19.4 0.0 collective-permute-done.1.edge_own
  19.4 0.0 collective-permute-done.2.edge_other
  19.4 0.0 collective-permute-done.block_other
  19.4 3.5 %shard_map.102 = (f32[24,8,512]{2,1,0:T(8,128)S(1)}, f32[24,8,512]{2,1,0:T(8,128)S(1)}, f32[6,8,512]{2,1,0:T(8,128)S(1)}, f32[6,8,512]{2,1,0:T(8,128)S(1)}) custom-call(f32[4]{0:T(128)S(1)} %copy-done.6, f32[8,12,8,512]{3,2,1,0:T(8,128)S(1)} %get-tuple-element.15.block_own, f32[8,12,8,512]{3,2,1,0:T(8,128)S(1)} %collective-permute-done.block_other, ...), custom_call_target="tpu_custom_call" | custom-call | flops 100000000 | bytes 4587536 | tf_op jit(solution)/shard_map/pallas_call | solution.py:555
  22.9 0.2 collective-permute-start.3
  23.1 3.3 %collective-permute-start.4 = (f32[6,8,512]{2,1,0:T(8,128)S(1)}, f32[6,8,512]{2,1,0:T(8,128)S(1)}, u32[]{:S(2)}, u32[]{:S(2)}) collective-permute-start(f32[6,8,512]{2,1,0:T(8,128)S(1)} %get-tuple-element.23), channel_id=1, source_target_pairs={{1,2},{3,4},{5,6},{7,8},{9,10},{11,12},{13,14},{15,16},{17,18},{19... | collective-permute-start | bytes 294920 | tf_op jit(solution)/shard_map/ppermute | solution.py:638
  26.4 0.0 collective-permute-start.5
  26.4 0.0 collective-permute-done.3.outer_other
  26.4 4.8 %shard_map.103 = (f32[4,12,8,512]{3,2,1,0:T(8,128)S(1)}, f32[12,8,512]{2,1,0:T(8,128)S(1)}) custom-call(f32[4]{0:T(128)S(1)} %copy-done.6, f32[8,12,8,512]{3,2,1,0:T(8,128)S(1)} %get-tuple-element.15.block_own, f32[8,12,8,512]{3,2,1,0:T(8,128)S(1)} %collective-permute-done.block_other, f32[24,8,512]{2,1,0:T(8,128)S(1)} %get-tuple-element.19.forcing, ...), custom_call_target="tpu_custom_call" | custom-call | flops 1000000000 | bytes 5308432 | tf_op jit(solution)/shard_map/pallas_call | solution.py:555
  31.2 0.0 collective-permute-done.4.from_cross
  31.2 1.1 %shard_map.104 = f32[4,12,8,512]{3,2,1,0:T(8,128)} custom-call(f32[4,12,8,512]{3,2,1,0:T(8,128)S(1)} %get-tuple-element.21.inner, f32[12,8,512]{2,1,0:T(8,128)S(1)} %get-tuple-element.22.sides, f32[6,8,512]{2,1,0:T(8,128)S(1)} %collective-permute-done.4.from_cross, f32[6,8,512]{2,1,0:T(8,128)S(1)} %collective-permute-done.5.from_same), custom_call_target="tpu_custom_call" | custom-call | flops 1000000 | bytes 1966080 | tf_op jit(solution)/shard_map/pallas_call | solution.py:555
  (14 shorter events, 0.0 us)
Async XLA Ops:
  0.0 0.7 %copy-start.5 = (f32[256,12]{0,1:T(8,128)S(1)}, f32[256,12]{0,1:T(8,128)}, u32[]{:S(2)}) copy-start(f32[256,12]{0,1:T(8,128)} %param.19) | copy-start | bytes 36868
  0.0 0.7 %copy-start.9 = (f32[256]{0:T(256)S(1)}, f32[256]{0:T(256)}, u32[]{:S(2)}) copy-start(f32[256]{0:T(256)} %param.18) | copy-start | bytes 3076
  0.0 0.7 %copy-start.8 = (f32[256]{0:T(256)S(1)}, f32[256]{0:T(256)}, u32[]{:S(2)}) copy-start(f32[256]{0:T(256)} %param.17) | copy-start | bytes 3076
  0.0 0.7 %copy-start.7 = (s32[256]{0:T(256)S(1)}, s32[256]{0:T(256)}, u32[]{:S(2)}) copy-start(s32[256]{0:T(256)} %param.16) | copy-start | bytes 3076
  0.0 1.0 %copy-start.4 = (f32[12,8,512]{2,1,0:T(8,128)S(1)}, f32[12,8,512]{2,1,0:T(8,128)}, u32[]{:S(2)}) copy-start(f32[12,8,512]{2,1,0:T(8,128)} %diff.1) | copy-start | bytes 589828
  0.0 1.1 %copy-start.3 = (f32[12,8,512]{2,1,0:T(8,128)S(1)}, f32[12,8,512]{2,1,0:T(8,128)}, u32[]{:S(2)}) copy-start(f32[12,8,512]{2,1,0:T(8,128)} %north.1) | copy-start | bytes 589828
  0.0 1.2 %copy-start.2 = (f32[12,8,512]{2,1,0:T(8,128)S(1)}, f32[12,8,512]{2,1,0:T(8,128)}, u32[]{:S(2)}) copy-start(f32[12,8,512]{2,1,0:T(8,128)} %east.1) | copy-start | bytes 589828
  0.0 1.5 %copy-start.1 = (f32[4,12,8,512]{3,2,1,0:T(8,128)S(1)}, f32[4,12,8,512]{3,2,1,0:T(8,128)}, u32[]{:S(2)}) copy-start(f32[4,12,8,512]{3,2,1,0:T(8,128)} %adj.1) | copy-start | bytes 2359300
  0.0 1.7 %copy-start = (f32[4,12,8,512]{3,2,1,0:T(8,128)S(1)}, f32[4,12,8,512]{3,2,1,0:T(8,128)}, u32[]{:S(2)}) copy-start(f32[4,12,8,512]{3,2,1,0:T(8,128)} %conc.1) | copy-start | bytes 2359300
  0.1 19.4 %copy-start.6 = (f32[4]{0:T(128)S(1)}, f32[4]{0:T(128)}, u32[]{:S(2)}) copy-start(f32[4]{0:T(128)} %factor.3) | copy-start | bytes 52
  3.0 16.5 %collective-permute-start = (f32[8,12,8,512]{3,2,1,0:T(8,128)S(1)}, f32[8,12,8,512]{3,2,1,0:T(8,128)S(1)}, u32[]{:S(2)}, u32[]{:S(2)}) collective-permute-start(f32[8,12,8,512]{3,2,1,0:T(8,128)S(1)} %get-tuple-element.15.block_own), channel_id=1, source_target_pairs={{0,1},{1,0},{2,3},{3,2},{4,5},{5,4},{6,7},{7,6},{8,9},{9,8},{10,11... | collective-permute-start | bytes 4718600 | tf_op jit(solution)/shard_map/ppermute | solution.py:618
  3.5 15.9 %collective-permute-start.1 = (f32[12,8,512]{2,1,0:T(8,128)S(1)}, f32[12,8,512]{2,1,0:T(8,128)S(1)}, u32[]{:S(2)}, u32[]{:S(2)}) collective-permute-start(f32[12,8,512]{2,1,0:T(8,128)S(1)} %get-tuple-element.16), channel_id=1, source_target_pairs={{0,2},{2,4},{4,6},{6,8},{8,10},{10,12},{12,14},{14,16},{16,18},{18... | collective-permute-start | bytes 589832 | tf_op jit(solution)/shard_map/ppermute | solution.py:616
  6.0 13.4 %collective-permute-start.2 = (f32[12,8,512]{2,1,0:T(8,128)S(1)}, f32[12,8,512]{2,1,0:T(8,128)S(1)}, u32[]{:S(2)}, u32[]{:S(2)}) collective-permute-start(f32[12,8,512]{2,1,0:T(8,128)S(1)} %get-tuple-element.17), channel_id=1, source_target_pairs={{1,2},{3,4},{5,6},{7,8},{9,10},{11,12},{13,14},{15,16},{17,18},{19... | collective-permute-start | bytes 589832 | tf_op jit(solution)/shard_map/ppermute | solution.py:617
  22.9 3.5 %collective-permute-start.3 = (f32[24,8,512]{2,1,0:T(8,128)S(1)}, f32[24,8,512]{2,1,0:T(8,128)S(1)}, u32[]{:S(2)}, u32[]{:S(2)}) collective-permute-start(f32[24,8,512]{2,1,0:T(8,128)S(1)} %get-tuple-element.20.outer), channel_id=1, source_target_pairs={{0,1},{1,0},{2,3},{3,2},{4,5},{5,4},{6,7},{7,6},{8,9},{9,8},{10,11... | collective-permute-start | bytes 1179656 | tf_op jit(solution)/shard_map/ppermute | solution.py:640
  23.1 8.1 %collective-permute-start.4 = (f32[6,8,512]{2,1,0:T(8,128)S(1)}, f32[6,8,512]{2,1,0:T(8,128)S(1)}, u32[]{:S(2)}, u32[]{:S(2)}) collective-permute-start(f32[6,8,512]{2,1,0:T(8,128)S(1)} %get-tuple-element.23), channel_id=1, source_target_pairs={{1,2},{3,4},{5,6},{7,8},{9,10},{11,12},{13,14},{15,16},{17,18},{19... | collective-permute-start | bytes 294920 | tf_op jit(solution)/shard_map/ppermute | solution.py:638
  26.4 4.9 %collective-permute-start.5 = (f32[6,8,512]{2,1,0:T(8,128)S(1)}, f32[6,8,512]{2,1,0:T(8,128)S(1)}, u32[]{:S(2)}, u32[]{:S(2)}) collective-permute-start(f32[6,8,512]{2,1,0:T(8,128)S(1)} %get-tuple-element.24), channel_id=1, source_target_pairs={{1,3},{3,5},{5,7},{7,9},{9,11},{11,13},{13,15},{15,17},{17,19},{19... | collective-permute-start | bytes 294920 | tf_op jit(solution)/shard_map/ppermute | solution.py:639

commit v7 on v6

--- a/solution.py
+++ b/solution.py
@@ -13,7 +13,7 @@
 HALF = 16
 MIB = 1 << 20
 UNROLL_B = 4
-UNROLL_D = 6
+UNROLL_D = 12
 
 
 def where_am_i():
@@ -65,19 +65,9 @@
     edge_cross,
     message,
     fields,
-    done,
 ):
     tracers, levels, cols, rows = conc.shape
     blocks = cell.shape[0]
-    moves = [
-        (diff, block.at[1]),
-        (east, block.at[2]),
-        (north, block.at[3]),
-        (adj, block.at[4 : 4 + tracers]),
-    ]
-    copies = [pltpu.make_async_copy(a, b, done.at[i]) for i, (a, b) in enumerate(moves)]
-    for copy in copies:
-        copy.start()
     for h in range(3):
         for j in range(blocks):
             fields[h, j, 0:4, :] = weight[4 * h : 4 * h + 4, LANES * j : LANES * (j + 1)]
@@ -125,13 +115,15 @@
         for tr in range(1, tracers):
             total = total + conc[tr, j]
         block[0, j] = total
+        for q, field in enumerate((diff, east, north)):
+            block[1 + q, j] = field[j]
+        for tr in range(tracers):
+            block[4 + tr, j] = adj[tr, j]
         members = [total, diff[j], east[j]] + [adj[tr, j] for tr in range(tracers)]
         edge_same[j], edge_cross[j] = packed_lines(members, columns)
         return carry
 
-    lax.fori_loop(0, levels, level, 0, unroll=2)
-    for copy in copies:
-        copy.wait()
+    lax.fori_loop(0, levels, level, 0, unroll=12)
 
 
 def two_parts(x):
@@ -280,7 +272,7 @@
                 self.state[chain, m, i] = out[-1]
             return tuple(out)
 
-        lax.fori_loop(0, self.count, level, tuple(self.zero for _ in every), unroll=2)
+        lax.fori_loop(0, self.count, level, tuple(self.zero for _ in every), unroll=4)
 
     def back(self, members):
         last = self.count - 1
@@ -301,7 +293,7 @@
                 self.state[chain, m, i] = out[-1]
             return tuple(out)
 
-        lax.fori_loop(0, last, level, tuple(ends), unroll=2)
+        lax.fori_loop(0, last, level, tuple(ends), unroll=4)
 
 
 def boundary_kernel(
@@ -400,7 +392,7 @@
             out[j] = one
         return carry
 
-    lax.fori_loop(0, count // 2, hand_out, 0, unroll=2)
+    lax.fori_loop(0, count // 2, hand_out, 0, unroll=6)
 
     slot = (place - beyond) & 7
 
@@ -416,7 +408,7 @@
             outer[count * chain + i] = jnp.where(slot == 5, near, tile)
         return carry
 
-    lax.fori_loop(0, count, hand_over, 0, unroll=2)
+    lax.fori_loop(0, count, hand_over, 0, unroll=6)
 
 
 def column_kernel(
@@ -501,7 +493,7 @@
 
     columns.factorise_and_sweep(coupling, source)
     columns.back(tracers + 1)
-    lax.fori_loop(0, count, advect, 0, unroll=2)
+    lax.fori_loop(0, count, advect, 0, unroll=4)
     columns.sweep(tracers)
     columns.back(tracers)
 
@@ -521,12 +513,12 @@
     lax.fori_loop(0, count, last, 0, unroll=3)
 
 
-def border_kernel(inner, sides, from_cross, from_same, out):
+def border_kernel(inner, sides, from_cross, from_same, out, ready, done):
     tracers, count, cols, rows = inner.shape
     band = where_am_i()
     place = sublane((cols, rows))
-
-    def pair(j, carry):
+    copies = []
+    for j in range(count // 2):
         cross, same = from_cross[j], from_same[j]
         westward = jnp.where(band == 0, cross, same)
         eastward = jnp.where(band == 0, same, cross)
@@ -536,17 +528,20 @@
             for tr in range(tracers):
                 q = 4 * (tr & 1) + 2 * (tr >> 1) + side
                 beyond = jnp.where(place == 0, turned(westward, 1 - q), turned(eastward, -1 - q))
-                out[tr, l] = inner[tr, l] + sides[i] * beyond
-        return carry
-
-    lax.fori_loop(0, count // 2, pair, 0, unroll=2)
+                ready[tr, l] = inner[tr, l] + sides[i] * beyond
+        low = jnp.where(band == 0, 2 * j, count - 2 - 2 * j)
+        part = (slice(None), pl.ds(low, 2))
+        copies.append(pltpu.make_async_copy(ready.at[part], out.at[part], done.at[j]))
+        copies[-1].start()
+    for copy in copies:
+        copy.wait()
 
 
 def f32(*shape):
     return jax.ShapeDtypeStruct(shape, jnp.float32)
 
 
-def call(kernel, outs, scratch, ops, limit, smem=0, moved=None):
+def call(kernel, outs, scratch, ops, limit, smem=0, moved=None, out_space=pltpu.VMEM):
     vmem = pl.BlockSpec(memory_space=pltpu.VMEM)
     scalars = pl.BlockSpec(memory_space=pltpu.SMEM)
 
@@ -556,7 +551,7 @@
             kernel,
             out_shape=outs,
             in_specs=[scalars] * smem + [vmem] * (len(args) - smem),
-            out_specs=[vmem] * len(outs),
+            out_specs=[pl.BlockSpec(memory_space=out_space)] * len(outs),
             scratch_shapes=scratch,
             compiler_params=pltpu.CompilerParams(vmem_limit_bytes=limit * MIB),
             cost_estimate=pl.CostEstimate(flops=ops, bytes_accessed=size, transcendentals=0),
@@ -588,7 +583,7 @@
     block, edge_same, edge_cross, message = call(
         pack_kernel,
         [f32(4 + tracers, band_levels, cols, rows), field, field, f32(tiles, 8, LANES)],
-        [pltpu.VMEM((4, blocks, 8, LANES), jnp.float32), pltpu.SemaphoreType.DMA((4,))],
+        [pltpu.VMEM((4, blocks, 8, LANES), jnp.float32)],
         10**6,
         16,
     )(
@@ -641,7 +636,11 @@
     inner, sides = call(
         column_kernel, [whole, field], room(tracers + 1), 10**9, 24, smem=1
     )(tracer_factor, block, block_other, forcing, outer, outer_other)
-    return call(border_kernel, [whole], [], 10**6, 16)(inner, sides, from_cross, from_same)[0]
+    ready = pltpu.VMEM((tracers, band_levels, cols, rows), jnp.float32)
+    done = pltpu.SemaphoreType.DMA((band_levels // 2,))
+    return call(border_kernel, [whole], [ready, done], 10**6, 16, out_space=pl.ANY)(
+        inner, sides, from_cross, from_same
+    )[0]
 
 
 def solution(mesh):

time: 32.6 us -> 31.4 us (0.963)
  Pallas kernels: 10.6 us -> 9.2 us
    pallas_call x5, Pallas kernels: 10.6 us -> 9.2 us  [run(): pl.pallas_call(kernel, out_shape=outs, in_specs=[scalars] * smem + [vmem]...]
where the time goes in v7:
time: 31.4 us; the launch traced here: 31 us
  starting transfers between devices  10.8 us (34%)
  Pallas kernels  9.2 us (29%)
  blocking collectives  9.09 us (29%)
  local copies, waits for them, and re-layouts  1.67 us (5%)
    pallas_call x5, Pallas kernels, run(): pl.pallas_call(kernel, out_shape=outs, in_specs=[scalars] * smem + [vmem]...  9.2 us
    all_to_all x1, blocking collectives, per_device(): lax.all_to_all(message.reshape(2 * tiles, 4, LANES), both, split_axis=0,...  9.09 us
    ppermute x1, starting transfers between devices, per_device(): edge_other = lax.ppermute(edge_cross, both, cross)  4.3 us
    ppermute x1, starting transfers between devices, per_device(): from_cross = lax.ppermute(to_cross, both, cross)  3.25 us
    ppermute x1, starting transfers between devices, per_device(): edge_own = lax.ppermute(edge_same, both, same)  2.55 us
    unnamed x20, local copies, waits for them, and re-layouts  1.67 us
  transfers between devices with their start and end apart: 6, of which 0 were waited for; matrix products, arithmetic and copies ran while one was open for 0% of the time, Pallas kernels for 15%

profile of v7, /device:TPU:0, one launch (start us, length us, event | category | flops | bytes accessed | tf_op | source)
XLA Modules:
  0.0 31.0 jit_solution(3848646238779425639)
XLA Ops:
  0.1 0.0 copy-start.6
  0.1 0.6 %copy-done.5 = f32[256,12]{0,1:T(8,128)S(1)} copy-done((f32[256,12]{0,1:T(8,128)S(1)}, f32[256,12]{0,1:T(8,128)}, u32[]{:S(2)}) %copy-start.5) | copy-done | bytes 12312
  0.7 0.0 copy-done.7
  0.7 0.3 copy-done.4
  1.0 0.1 copy-done.3
  1.1 0.1 copy-done.2
  1.2 0.3 copy-done.1
  1.5 0.2 copy-done
  1.7 0.4 %shard_map.101 = (f32[8,12,8,512]{3,2,1,0:T(8,128)S(1)}, f32[12,8,512]{2,1,0:T(8,128)S(1)}, f32[12,8,512]{2,1,0:T(8,128)S(1)}, f32[16,8,128]{2,1,0:T(8,128)S(1)}) custom-call(f32[8,128]{1,0:T(8,128)S(1)} %shard_map.100.first, f32[4,12,8,512]{3,2,1,0:T(8,128)S(1)} %copy-done, f32[4,12,8,512]{3,2,1,0:T(8,128)S(1)} %copy-done.1, f32[12,8,512]{2,1,0:T(8,128)S(1)} %copy-done.2, ...), custom_call_target="tpu_custom_call" | custom-call | flops 1000000 | bytes 4213760 | tf_op jit(solution)/shard_map/pallas_call | solution.py:550
  2.1 0.5 %collective-permute-start = (f32[8,12,8,512]{3,2,1,0:T(8,128)S(1)}, f32[8,12,8,512]{3,2,1,0:T(8,128)S(1)}, u32[]{:S(2)}, u32[]{:S(2)}) collective-permute-start(f32[8,12,8,512]{3,2,1,0:T(8,128)S(1)} %get-tuple-element.15.block_own), channel_id=1, source_target_pairs={{0,1},{1,0},{2,3},{3,2},{4,5},{5,4},{6,7},{7,6},{8,9},{9,8},{10,11... | collective-permute-start | bytes 4718600 | tf_op jit(solution)/shard_map/ppermute | solution.py:613
  2.7 2.6 %collective-permute-start.1 = (f32[12,8,512]{2,1,0:T(8,128)S(1)}, f32[12,8,512]{2,1,0:T(8,128)S(1)}, u32[]{:S(2)}, u32[]{:S(2)}) collective-permute-start(f32[12,8,512]{2,1,0:T(8,128)S(1)} %get-tuple-element.16), channel_id=1, source_target_pairs={{0,2},{2,4},{4,6},{6,8},{8,10},{10,12},{12,14},{14,16},{16,18},{18... | collective-permute-start | bytes 589832 | tf_op jit(solution)/shard_map/ppermute | solution.py:611
  5.2 4.3 %collective-permute-start.2 = (f32[12,8,512]{2,1,0:T(8,128)S(1)}, f32[12,8,512]{2,1,0:T(8,128)S(1)}, u32[]{:S(2)}, u32[]{:S(2)}) collective-permute-start(f32[12,8,512]{2,1,0:T(8,128)S(1)} %get-tuple-element.17), channel_id=1, source_target_pairs={{1,2},{3,4},{5,6},{7,8},{9,10},{11,12},{13,14},{15,16},{17,18},{19... | collective-permute-start | bytes 589832 | tf_op jit(solution)/shard_map/ppermute | solution.py:612
  9.5 9.1 %all_to_all.5 = f32[32,4,128]{2,1,0:T(4,128)S(1)} all-to-all(f32[32,4,128]{2,1,0:T(4,128)S(1)} %bitcast.7), channel_id=1, replica_groups=mesh['tile'=16,'band'=2] {'tile','band'}, dimensions={0} | all-to-all | bytes 131072 | tf_op jit(solution)/shard_map/all_to_all | solution.py:614
  18.6 0.0 collective-permute-done.1.edge_own
  18.6 0.0 collective-permute-done.2.edge_other
  18.6 0.0 collective-permute-done.block_other
  18.6 3.3 %shard_map.102 = (f32[24,8,512]{2,1,0:T(8,128)S(1)}, f32[24,8,512]{2,1,0:T(8,128)S(1)}, f32[6,8,512]{2,1,0:T(8,128)S(1)}, f32[6,8,512]{2,1,0:T(8,128)S(1)}) custom-call(f32[4]{0:T(128)S(1)} %copy-done.6, f32[8,12,8,512]{3,2,1,0:T(8,128)S(1)} %get-tuple-element.15.block_own, f32[8,12,8,512]{3,2,1,0:T(8,128)S(1)} %collective-permute-done.block_other, ...), custom_call_target="tpu_custom_call" | custom-call | flops 100000000 | bytes 4587536 | tf_op jit(solution)/shard_map/pallas_call | solution.py:550
  22.0 0.2 collective-permute-start.3
  22.1 3.3 %collective-permute-start.4 = (f32[6,8,512]{2,1,0:T(8,128)S(1)}, f32[6,8,512]{2,1,0:T(8,128)S(1)}, u32[]{:S(2)}, u32[]{:S(2)}) collective-permute-start(f32[6,8,512]{2,1,0:T(8,128)S(1)} %get-tuple-element.23), channel_id=1, source_target_pairs={{1,2},{3,4},{5,6},{7,8},{9,10},{11,12},{13,14},{15,16},{17,18},{19... | collective-permute-start | bytes 294920 | tf_op jit(solution)/shard_map/ppermute | solution.py:633
  25.4 0.0 collective-permute-start.5
  25.4 0.0 collective-permute-done.3.outer_other
  25.4 4.5 %shard_map.103 = (f32[4,12,8,512]{3,2,1,0:T(8,128)S(1)}, f32[12,8,512]{2,1,0:T(8,128)S(1)}) custom-call(f32[4]{0:T(128)S(1)} %copy-done.6, f32[8,12,8,512]{3,2,1,0:T(8,128)S(1)} %get-tuple-element.15.block_own, f32[8,12,8,512]{3,2,1,0:T(8,128)S(1)} %collective-permute-done.block_other, f32[24,8,512]{2,1,0:T(8,128)S(1)} %get-tuple-element.19.forcing, ...), custom_call_target="tpu_custom_call" | custom-call | flops 1000000000 | bytes 5308432 | tf_op jit(solution)/shard_map/pallas_call | solution.py:550
  30.0 0.0 collective-permute-done.5.from_same
  30.0 0.9 %shard_map.104 = f32[4,12,8,512]{3,2,1,0:T(8,128)} custom-call(f32[4,12,8,512]{3,2,1,0:T(8,128)S(1)} %get-tuple-element.21.inner, f32[12,8,512]{2,1,0:T(8,128)S(1)} %get-tuple-element.22.sides, f32[6,8,512]{2,1,0:T(8,128)S(1)} %collective-permute-done.4.from_cross, f32[6,8,512]{2,1,0:T(8,128)S(1)} %collective-permute-done.5.from_same), custom_call_target="tpu_custom_call" | custom-call | flops 1000000 | bytes 1966080 | tf_op jit(solution)/shard_map/pallas_call | solution.py:550
  (14 shorter events, 0.0 us)
Async XLA Ops:
  0.0 0.7 %copy-start.5 = (f32[256,12]{0,1:T(8,128)S(1)}, f32[256,12]{0,1:T(8,128)}, u32[]{:S(2)}) copy-start(f32[256,12]{0,1:T(8,128)} %param.19) | copy-start | bytes 36868
  0.0 0.7 %copy-start.9 = (f32[256]{0:T(256)S(1)}, f32[256]{0:T(256)}, u32[]{:S(2)}) copy-start(f32[256]{0:T(256)} %param.18) | copy-start | bytes 3076
  0.0 0.7 %copy-start.8 = (f32[256]{0:T(256)S(1)}, f32[256]{0:T(256)}, u32[]{:S(2)}) copy-start(f32[256]{0:T(256)} %param.17) | copy-start | bytes 3076
  0.0 0.7 %copy-start.7 = (s32[256]{0:T(256)S(1)}, s32[256]{0:T(256)}, u32[]{:S(2)}) copy-start(s32[256]{0:T(256)} %param.16) | copy-start | bytes 3076
  0.0 1.0 %copy-start.4 = (f32[12,8,512]{2,1,0:T(8,128)S(1)}, f32[12,8,512]{2,1,0:T(8,128)}, u32[]{:S(2)}) copy-start(f32[12,8,512]{2,1,0:T(8,128)} %diff.1) | copy-start | bytes 589828
  0.0 1.1 %copy-start.3 = (f32[12,8,512]{2,1,0:T(8,128)S(1)}, f32[12,8,512]{2,1,0:T(8,128)}, u32[]{:S(2)}) copy-start(f32[12,8,512]{2,1,0:T(8,128)} %north.1) | copy-start | bytes 589828
  0.0 1.2 %copy-start.2 = (f32[12,8,512]{2,1,0:T(8,128)S(1)}, f32[12,8,512]{2,1,0:T(8,128)}, u32[]{:S(2)}) copy-start(f32[12,8,512]{2,1,0:T(8,128)} %east.1) | copy-start | bytes 589828
  0.0 1.5 %copy-start.1 = (f32[4,12,8,512]{3,2,1,0:T(8,128)S(1)}, f32[4,12,8,512]{3,2,1,0:T(8,128)}, u32[]{:S(2)}) copy-start(f32[4,12,8,512]{3,2,1,0:T(8,128)} %adj.1) | copy-start | bytes 2359300
  0.0 1.7 %copy-start = (f32[4,12,8,512]{3,2,1,0:T(8,128)S(1)}, f32[4,12,8,512]{3,2,1,0:T(8,128)}, u32[]{:S(2)}) copy-start(f32[4,12,8,512]{3,2,1,0:T(8,128)} %conc.1) | copy-start | bytes 2359300
  0.1 18.5 %copy-start.6 = (f32[4]{0:T(128)S(1)}, f32[4]{0:T(128)}, u32[]{:S(2)}) copy-start(f32[4]{0:T(128)} %factor.3) | copy-start | bytes 52
  2.1 16.5 %collective-permute-start = (f32[8,12,8,512]{3,2,1,0:T(8,128)S(1)}, f32[8,12,8,512]{3,2,1,0:T(8,128)S(1)}, u32[]{:S(2)}, u32[]{:S(2)}) collective-permute-start(f32[8,12,8,512]{3,2,1,0:T(8,128)S(1)} %get-tuple-element.15.block_own), channel_id=1, source_target_pairs={{0,1},{1,0},{2,3},{3,2},{4,5},{5,4},{6,7},{7,6},{8,9},{9,8},{10,11... | collective-permute-start | bytes 4718600 | tf_op jit(solution)/shard_map/ppermute | solution.py:613
  2.7 15.9 %collective-permute-start.1 = (f32[12,8,512]{2,1,0:T(8,128)S(1)}, f32[12,8,512]{2,1,0:T(8,128)S(1)}, u32[]{:S(2)}, u32[]{:S(2)}) collective-permute-start(f32[12,8,512]{2,1,0:T(8,128)S(1)} %get-tuple-element.16), channel_id=1, source_target_pairs={{0,2},{2,4},{4,6},{6,8},{8,10},{10,12},{12,14},{14,16},{16,18},{18... | collective-permute-start | bytes 589832 | tf_op jit(solution)/shard_map/ppermute | solution.py:611
  5.2 13.4 %collective-permute-start.2 = (f32[12,8,512]{2,1,0:T(8,128)S(1)}, f32[12,8,512]{2,1,0:T(8,128)S(1)}, u32[]{:S(2)}, u32[]{:S(2)}) collective-permute-start(f32[12,8,512]{2,1,0:T(8,128)S(1)} %get-tuple-element.17), channel_id=1, source_target_pairs={{1,2},{3,4},{5,6},{7,8},{9,10},{11,12},{13,14},{15,16},{17,18},{19... | collective-permute-start | bytes 589832 | tf_op jit(solution)/shard_map/ppermute | solution.py:612
  22.0 3.5 %collective-permute-start.3 = (f32[24,8,512]{2,1,0:T(8,128)S(1)}, f32[24,8,512]{2,1,0:T(8,128)S(1)}, u32[]{:S(2)}, u32[]{:S(2)}) collective-permute-start(f32[24,8,512]{2,1,0:T(8,128)S(1)} %get-tuple-element.20.outer), channel_id=1, source_target_pairs={{0,1},{1,0},{2,3},{3,2},{4,5},{5,4},{6,7},{7,6},{8,9},{9,8},{10,11... | collective-permute-start | bytes 1179656 | tf_op jit(solution)/shard_map/ppermute | solution.py:635
  22.1 7.8 %collective-permute-start.4 = (f32[6,8,512]{2,1,0:T(8,128)S(1)}, f32[6,8,512]{2,1,0:T(8,128)S(1)}, u32[]{:S(2)}, u32[]{:S(2)}) collective-permute-start(f32[6,8,512]{2,1,0:T(8,128)S(1)} %get-tuple-element.23), channel_id=1, source_target_pairs={{1,2},{3,4},{5,6},{7,8},{9,10},{11,12},{13,14},{15,16},{17,18},{19... | collective-permute-start | bytes 294920 | tf_op jit(solution)/shard_map/ppermute | solution.py:633
  25.4 4.6 %collective-permute-start.5 = (f32[6,8,512]{2,1,0:T(8,128)S(1)}, f32[6,8,512]{2,1,0:T(8,128)S(1)}, u32[]{:S(2)}, u32[]{:S(2)}) collective-permute-start(f32[6,8,512]{2,1,0:T(8,128)S(1)} %get-tuple-element.24), channel_id=1, source_target_pairs={{1,3},{3,5},{5,7},{7,9},{9,11},{11,13},{13,15},{15,17},{17,19},{19... | collective-permute-start | bytes 294920 | tf_op jit(solution)/shard_map/ppermute | solution.py:634

commit v8 on v7

--- a/solution.py
+++ b/solution.py
@@ -12,8 +12,6 @@
 PAIR = 32
 HALF = 16
 MIB = 1 << 20
-UNROLL_B = 4
-UNROLL_D = 12
 
 
 def where_am_i():
@@ -123,7 +121,7 @@
         edge_same[j], edge_cross[j] = packed_lines(members, columns)
         return carry
 
-    lax.fori_loop(0, levels, level, 0, unroll=12)
+    lax.fori_loop(0, levels, level, 0, unroll=levels)
 
 
 def two_parts(x):
@@ -134,11 +132,10 @@
 
 
 def onehot_dot(x, onehot, dims):
-    out = None
-    for part in two_parts(x):
-        term = lax.dot_general(part, onehot, (dims, ((), ())), preferred_element_type=jnp.float32)
-        out = term if out is None else out + term
-    return out
+    many = x.shape[0]
+    parts = jnp.concatenate(two_parts(x), axis=0)
+    out = lax.dot_general(parts, onehot, (dims, ((), ())), preferred_element_type=jnp.float32)
+    return out[:many] + out[many:]
 
 
 def add_soundings(slots, total, forcing):
@@ -256,7 +253,7 @@
         zero = self.zero
         outward = tuple(zero for _ in range(max(self.kinds) + 1))
         start = (outward, tuple((zero, zero) for _ in self.strengths))
-        ends = lax.fori_loop(0, self.count, level, (start, start), unroll=UNROLL_B)
+        ends = lax.fori_loop(0, self.count, level, (start, start), unroll=self.count)
         for m in range(len(self.strengths)):
             near, far = ends[0][1][m][0], ends[1][1][m][0]
             self.middle[m] = 1.0 / (near + self.ratio[0, m, self.count - 1] * far)
@@ -272,7 +269,7 @@
                 self.state[chain, m, i] = out[-1]
             return tuple(out)
 
-        lax.fori_loop(0, self.count, level, tuple(self.zero for _ in every), unroll=4)
+        lax.fori_loop(0, self.count, level, tuple(self.zero for _ in every), unroll=self.count)
 
     def back(self, members):
         last = self.count - 1
@@ -293,7 +290,7 @@
                 self.state[chain, m, i] = out[-1]
             return tuple(out)
 
-        lax.fori_loop(0, last, level, tuple(ends), unroll=4)
+        lax.fori_loop(0, last, level, tuple(ends), unroll=last)
 
 
 def boundary_kernel(
@@ -325,6 +322,7 @@
     outside = place == beyond
     edge = cols - 1 - beyond
     first = ((place - edge + 1) & 7) < 4
+    outside_far = ((place - beyond) & 7) == 4
     blocks = (block_own, block_other)
     edges = (edge_own, edge_other)
 
@@ -343,7 +341,7 @@
             faces[count * chain + i] = e
         return carry
 
-    lax.fori_loop(0, count, assemble, 0, unroll=2)
+    lax.fori_loop(0, count, assemble, 0, unroll=count)
 
     add_soundings(slots, total, forcing)
 
@@ -355,11 +353,14 @@
         g, l = chain_level(count, chain, i)
         packed = edges[chain][l]
         force = forcing[g]
-        amounts = [
-            jnp.where(outside, turned(packed, -3 - tr), blocks[chain][4 + tr, l]) + force
-            for tr in range(tracers)
-        ]
-        return [joined(amounts[tr], amounts[tr + 1]) for tr in range(0, tracers, 2)]
+        force = joined(force, force)
+        amounts = []
+        for tr in range(0, tracers, 2):
+            near = jnp.where(outside, turned(packed, -3 - tr), blocks[chain][4 + tr, l])
+            far = pltpu.roll(blocks[chain][5 + tr, l], 4, 0)
+            far = jnp.where(outside_far, turned(packed, -tr), far)
+            amounts.append(jnp.where(first, near, far) + force)
+        return amounts
 
     pairs = tracers // 2
     strengths = [jnp.where(first, factor[2 * m], factor[2 * m + 1]) for m in range(pairs)]
@@ -378,7 +379,7 @@
 
     columns.factorise_and_sweep(coupling, source)
     columns.back(pairs)
-    lax.fori_loop(0, count, advect, 0, unroll=UNROLL_D)
+    lax.fori_loop(0, count, advect, 0, unroll=count)
     columns.sweep(pairs)
     columns.back(pairs)
 
@@ -392,7 +393,7 @@
             out[j] = one
         return carry
 
-    lax.fori_loop(0, count // 2, hand_out, 0, unroll=6)
+    lax.fori_loop(0, count // 2, hand_out, 0, unroll=count // 2)
 
     slot = (place - beyond) & 7
 
@@ -408,7 +409,7 @@
             outer[count * chain + i] = jnp.where(slot == 5, near, tile)
         return carry
 
-    lax.fori_loop(0, count, hand_over, 0, unroll=6)
+    lax.fori_loop(0, count, hand_over, 0, unroll=count)
 
 
 def column_kernel(
@@ -493,7 +494,7 @@
 
     columns.factorise_and_sweep(coupling, source)
     columns.back(tracers + 1)
-    lax.fori_loop(0, count, advect, 0, unroll=4)
+    lax.fori_loop(0, count, advect, 0, unroll=count)
     columns.sweep(tracers)
     columns.back(tracers)
 
@@ -510,7 +511,7 @@
             inner[tr, l] = advected(state[0, tr, i], parts)
         return carry
 
-    lax.fori_loop(0, count, last, 0, unroll=3)
+    lax.fori_loop(0, count, last, 0, unroll=count)
 
 
 def border_kernel(inner, sides, from_cross, from_same, out, ready, done):

time: 31.4 us -> 31 us (0.987)
  Pallas kernels: 9.2 us -> 8.13 us
  waiting for transfers between devices: 0.05 us -> 0.75 us
    pallas_call x5, Pallas kernels: 9.2 us -> 8.13 us  [run(): pl.pallas_call(kernel, out_shape=outs, in_specs=[scalars] * smem + [vmem]...]
    ppermute x1, waiting for transfers between devices: 0.01 us -> 0.51 us  [per_device(): from_cross = lax.ppermute(to_cross, both, cross)]
  transfers between devices with their start and end apart: 6 -> 6, of which waited for: 0 -> 2; matrix products, arithmetic and copies ran while one was open for 0% -> 0% of each run, Pallas kernels for 15% -> 12%
where the time goes in v8:
time: 31 us; the launch traced here: 30.6 us
  starting transfers between devices  10.9 us (35%)
  blocking collectives  9.09 us (29%)
  Pallas kernels  8.13 us (26%)
  local copies, waits for them, and re-layouts  1.67 us (5%)
  waiting for transfers between devices  0.75 us (2%)
    all_to_all x1, blocking collectives, per_device(): lax.all_to_all(message.reshape(2 * tiles, 4, LANES), both, split_axis=0,...  9.09 us
    pallas_call x5, Pallas kernels, run(): pl.pallas_call(kernel, out_shape=outs, in_specs=[scalars] * smem + [vmem]...  8.13 us
    ppermute x1, starting transfers between devices, per_device(): edge_other = lax.ppermute(edge_cross, both, cross)  4.3 us
    ppermute x1, starting transfers between devices, per_device(): from_cross = lax.ppermute(to_cross, both, cross)  3.25 us
    ppermute x1, starting transfers between devices, per_device(): edge_own = lax.ppermute(edge_same, both, same)  2.55 us
    unnamed x20, local copies, waits for them, and re-layouts  1.67 us
  transfers between devices with their start and end apart: 6, of which 2 were waited for; matrix products, arithmetic and copies ran while one was open for 0% of the time, Pallas kernels for 12%

profile of v8, /device:TPU:0, one launch (start us, length us, event | category | flops | bytes accessed | tf_op | source)
XLA Modules:
  0.0 30.6 jit_solution(15198637146728756465)
XLA Ops:
  0.1 0.0 copy-start.6
  0.1 0.6 %copy-done.5 = f32[256,12]{0,1:T(8,128)S(1)} copy-done((f32[256,12]{0,1:T(8,128)S(1)}, f32[256,12]{0,1:T(8,128)}, u32[]{:S(2)}) %copy-start.5) | copy-done | bytes 12312
  0.7 0.0 copy-done.7
  0.7 0.3 copy-done.4
  1.0 0.1 copy-done.3
  1.1 0.1 copy-done.2
  1.2 0.3 %copy-done.1 = f32[4,12,8,512]{3,2,1,0:T(8,128)S(1)} copy-done((f32[4,12,8,512]{3,2,1,0:T(8,128)S(1)}, f32[4,12,8,512]{3,2,1,0:T(8,128)}, u32[]{:S(2)}) %copy-start.1) | copy-done | bytes 786456
  1.5 0.2 copy-done
  1.7 0.4 %shard_map.101 = (f32[8,12,8,512]{3,2,1,0:T(8,128)S(1)}, f32[12,8,512]{2,1,0:T(8,128)S(1)}, f32[12,8,512]{2,1,0:T(8,128)S(1)}, f32[16,8,128]{2,1,0:T(8,128)S(1)}) custom-call(f32[8,128]{1,0:T(8,128)S(1)} %shard_map.100.first, f32[4,12,8,512]{3,2,1,0:T(8,128)S(1)} %copy-done, f32[4,12,8,512]{3,2,1,0:T(8,128)S(1)} %copy-done.1, f32[12,8,512]{2,1,0:T(8,128)S(1)} %copy-done.2, ...), custom_call_target="tpu_custom_call" | custom-call | flops 1000000 | bytes 4213760 | tf_op jit(solution)/shard_map/pallas_call | solution.py:551
  2.1 0.5 %collective-permute-start = (f32[8,12,8,512]{3,2,1,0:T(8,128)S(1)}, f32[8,12,8,512]{3,2,1,0:T(8,128)S(1)}, u32[]{:S(2)}, u32[]{:S(2)}) collective-permute-start(f32[8,12,8,512]{3,2,1,0:T(8,128)S(1)} %get-tuple-element.15.block_own), channel_id=1, source_target_pairs={{0,1},{1,0},{2,3},{3,2},{4,5},{5,4},{6,7},{7,6},{8,9},{9,8},{10,11... | collective-permute-start | bytes 4718600 | tf_op jit(solution)/shard_map/ppermute | solution.py:614
  2.7 2.6 %collective-permute-start.1 = (f32[12,8,512]{2,1,0:T(8,128)S(1)}, f32[12,8,512]{2,1,0:T(8,128)S(1)}, u32[]{:S(2)}, u32[]{:S(2)}) collective-permute-start(f32[12,8,512]{2,1,0:T(8,128)S(1)} %get-tuple-element.16), channel_id=1, source_target_pairs={{0,2},{2,4},{4,6},{6,8},{8,10},{10,12},{12,14},{14,16},{16,18},{18... | collective-permute-start | bytes 589832 | tf_op jit(solution)/shard_map/ppermute | solution.py:612
  5.2 4.3 %collective-permute-start.2 = (f32[12,8,512]{2,1,0:T(8,128)S(1)}, f32[12,8,512]{2,1,0:T(8,128)S(1)}, u32[]{:S(2)}, u32[]{:S(2)}) collective-permute-start(f32[12,8,512]{2,1,0:T(8,128)S(1)} %get-tuple-element.17), channel_id=1, source_target_pairs={{1,2},{3,4},{5,6},{7,8},{9,10},{11,12},{13,14},{15,16},{17,18},{19... | collective-permute-start | bytes 589832 | tf_op jit(solution)/shard_map/ppermute | solution.py:613
  9.5 9.1 %all_to_all.5 = f32[32,4,128]{2,1,0:T(4,128)S(1)} all-to-all(f32[32,4,128]{2,1,0:T(4,128)S(1)} %bitcast.7), channel_id=1, replica_groups=mesh['tile'=16,'band'=2] {'tile','band'}, dimensions={0} | all-to-all | bytes 131072 | tf_op jit(solution)/shard_map/all_to_all | solution.py:615
  18.6 0.0 collective-permute-done.1.edge_own
  18.6 0.0 collective-permute-done.2.edge_other
  18.6 0.0 collective-permute-done.block_other
  18.6 3.0 %shard_map.102 = (f32[24,8,512]{2,1,0:T(8,128)S(1)}, f32[24,8,512]{2,1,0:T(8,128)S(1)}, f32[6,8,512]{2,1,0:T(8,128)S(1)}, f32[6,8,512]{2,1,0:T(8,128)S(1)}) custom-call(f32[4]{0:T(128)S(1)} %copy-done.6, f32[8,12,8,512]{3,2,1,0:T(8,128)S(1)} %get-tuple-element.15.block_own, f32[8,12,8,512]{3,2,1,0:T(8,128)S(1)} %collective-permute-done.block_other, ...), custom_call_target="tpu_custom_call" | custom-call | flops 100000000 | bytes 4587536 | tf_op jit(solution)/shard_map/pallas_call | solution.py:551
  21.6 0.2 collective-permute-start.3
  21.8 3.2 %collective-permute-start.4 = (f32[6,8,512]{2,1,0:T(8,128)S(1)}, f32[6,8,512]{2,1,0:T(8,128)S(1)}, u32[]{:S(2)}, u32[]{:S(2)}) collective-permute-start(f32[6,8,512]{2,1,0:T(8,128)S(1)} %get-tuple-element.23), channel_id=1, source_target_pairs={{1,2},{3,4},{5,6},{7,8},{9,10},{11,12},{13,14},{15,16},{17,18},{19... | collective-permute-start | bytes 294920 | tf_op jit(solution)/shard_map/ppermute | solution.py:634
  25.0 0.0 collective-permute-start.5
  25.1 3.8 %shard_map.103 = (f32[4,12,8,512]{3,2,1,0:T(8,128)S(1)}, f32[12,8,512]{2,1,0:T(8,128)S(1)}) custom-call(f32[4]{0:T(128)S(1)} %copy-done.6, f32[8,12,8,512]{3,2,1,0:T(8,128)S(1)} %get-tuple-element.15.block_own, f32[8,12,8,512]{3,2,1,0:T(8,128)S(1)} %collective-permute-done.block_other, f32[24,8,512]{2,1,0:T(8,128)S(1)} %get-tuple-element.19.forcing, ...), custom_call_target="tpu_custom_call" | custom-call | flops 1000000000 | bytes 5308432 | tf_op jit(solution)/shard_map/pallas_call | solution.py:551
  28.9 0.5 %collective-permute-done.4.from_cross = f32[6,8,512]{2,1,0:T(8,128)S(1)} collective-permute-done((f32[6,8,512]{2,1,0:T(8,128)S(1)}, f32[6,8,512]{2,1,0:T(8,128)S(1)}, u32[]{:S(2)}, u32[]{:S(2)}) %collective-permute-start.4) | collective-permute-done | bytes 98336 | tf_op jit(solution)/shard_map/ppermute | solution.py:634
  29.4 0.2 collective-permute-done.5.from_same
  29.6 0.9 %shard_map.104 = f32[4,12,8,512]{3,2,1,0:T(8,128)} custom-call(f32[4,12,8,512]{3,2,1,0:T(8,128)S(1)} %get-tuple-element.21.inner, f32[12,8,512]{2,1,0:T(8,128)S(1)} %get-tuple-element.22.sides, f32[6,8,512]{2,1,0:T(8,128)S(1)} %collective-permute-done.4.from_cross, f32[6,8,512]{2,1,0:T(8,128)S(1)} %collective-permute-done.5.from_same), custom_call_target="tpu_custom_call" | custom-call | flops 1000000 | bytes 1966080 | tf_op jit(solution)/shard_map/pallas_call | solution.py:551
  (14 shorter events, 0.0 us)
Async XLA Ops:
  0.0 0.7 %copy-start.5 = (f32[256,12]{0,1:T(8,128)S(1)}, f32[256,12]{0,1:T(8,128)}, u32[]{:S(2)}) copy-start(f32[256,12]{0,1:T(8,128)} %param.19) | copy-start | bytes 36868
  0.0 0.7 %copy-start.9 = (f32[256]{0:T(256)S(1)}, f32[256]{0:T(256)}, u32[]{:S(2)}) copy-start(f32[256]{0:T(256)} %param.18) | copy-start | bytes 3076
  0.0 0.7 %copy-start.8 = (f32[256]{0:T(256)S(1)}, f32[256]{0:T(256)}, u32[]{:S(2)}) copy-start(f32[256]{0:T(256)} %param.17) | copy-start | bytes 3076
  0.0 0.7 %copy-start.7 = (s32[256]{0:T(256)S(1)}, s32[256]{0:T(256)}, u32[]{:S(2)}) copy-start(s32[256]{0:T(256)} %param.16) | copy-start | bytes 3076
  0.0 1.0 %copy-start.4 = (f32[12,8,512]{2,1,0:T(8,128)S(1)}, f32[12,8,512]{2,1,0:T(8,128)}, u32[]{:S(2)}) copy-start(f32[12,8,512]{2,1,0:T(8,128)} %diff.1) | copy-start | bytes 589828
  0.0 1.1 %copy-start.3 = (f32[12,8,512]{2,1,0:T(8,128)S(1)}, f32[12,8,512]{2,1,0:T(8,128)}, u32[]{:S(2)}) copy-start(f32[12,8,512]{2,1,0:T(8,128)} %north.1) | copy-start | bytes 589828
  0.0 1.2 %copy-start.2 = (f32[12,8,512]{2,1,0:T(8,128)S(1)}, f32[12,8,512]{2,1,0:T(8,128)}, u32[]{:S(2)}) copy-start(f32[12,8,512]{2,1,0:T(8,128)} %east.1) | copy-start | bytes 589828
  0.0 1.5 %copy-start.1 = (f32[4,12,8,512]{3,2,1,0:T(8,128)S(1)}, f32[4,12,8,512]{3,2,1,0:T(8,128)}, u32[]{:S(2)}) copy-start(f32[4,12,8,512]{3,2,1,0:T(8,128)} %adj.1) | copy-start | bytes 2359300
  0.0 1.7 %copy-start = (f32[4,12,8,512]{3,2,1,0:T(8,128)S(1)}, f32[4,12,8,512]{3,2,1,0:T(8,128)}, u32[]{:S(2)}) copy-start(f32[4,12,8,512]{3,2,1,0:T(8,128)} %conc.1) | copy-start | bytes 2359300
  0.1 18.5 %copy-start.6 = (f32[4]{0:T(128)S(1)}, f32[4]{0:T(128)}, u32[]{:S(2)}) copy-start(f32[4]{0:T(128)} %factor.3) | copy-start | bytes 52
  2.1 16.5 %collective-permute-start = (f32[8,12,8,512]{3,2,1,0:T(8,128)S(1)}, f32[8,12,8,512]{3,2,1,0:T(8,128)S(1)}, u32[]{:S(2)}, u32[]{:S(2)}) collective-permute-start(f32[8,12,8,512]{3,2,1,0:T(8,128)S(1)} %get-tuple-element.15.block_own), channel_id=1, source_target_pairs={{0,1},{1,0},{2,3},{3,2},{4,5},{5,4},{6,7},{7,6},{8,9},{9,8},{10,11... | collective-permute-start | bytes 4718600 | tf_op jit(solution)/shard_map/ppermute | solution.py:614
  2.7 15.9 %collective-permute-start.1 = (f32[12,8,512]{2,1,0:T(8,128)S(1)}, f32[12,8,512]{2,1,0:T(8,128)S(1)}, u32[]{:S(2)}, u32[]{:S(2)}) collective-permute-start(f32[12,8,512]{2,1,0:T(8,128)S(1)} %get-tuple-element.16), channel_id=1, source_target_pairs={{0,2},{2,4},{4,6},{6,8},{8,10},{10,12},{12,14},{14,16},{16,18},{18... | collective-permute-start | bytes 589832 | tf_op jit(solution)/shard_map/ppermute | solution.py:612
  5.2 13.4 %collective-permute-start.2 = (f32[12,8,512]{2,1,0:T(8,128)S(1)}, f32[12,8,512]{2,1,0:T(8,128)S(1)}, u32[]{:S(2)}, u32[]{:S(2)}) collective-permute-start(f32[12,8,512]{2,1,0:T(8,128)S(1)} %get-tuple-element.17), channel_id=1, source_target_pairs={{1,2},{3,4},{5,6},{7,8},{9,10},{11,12},{13,14},{15,16},{17,18},{19... | collective-permute-start | bytes 589832 | tf_op jit(solution)/shard_map/ppermute | solution.py:613
  21.6 3.5 %collective-permute-start.3 = (f32[24,8,512]{2,1,0:T(8,128)S(1)}, f32[24,8,512]{2,1,0:T(8,128)S(1)}, u32[]{:S(2)}, u32[]{:S(2)}) collective-permute-start(f32[24,8,512]{2,1,0:T(8,128)S(1)} %get-tuple-element.20.outer), channel_id=1, source_target_pairs={{0,1},{1,0},{2,3},{3,2},{4,5},{5,4},{6,7},{7,6},{8,9},{9,8},{10,11... | collective-permute-start | bytes 1179656 | tf_op jit(solution)/shard_map/ppermute | solution.py:636
  21.8 7.6 %collective-permute-start.4 = (f32[6,8,512]{2,1,0:T(8,128)S(1)}, f32[6,8,512]{2,1,0:T(8,128)S(1)}, u32[]{:S(2)}, u32[]{:S(2)}) collective-permute-start(f32[6,8,512]{2,1,0:T(8,128)S(1)} %get-tuple-element.23), channel_id=1, source_target_pairs={{1,2},{3,4},{5,6},{7,8},{9,10},{11,12},{13,14},{15,16},{17,18},{19... | collective-permute-start | bytes 294920 | tf_op jit(solution)/shard_map/ppermute | solution.py:634
  25.0 4.6 %collective-permute-start.5 = (f32[6,8,512]{2,1,0:T(8,128)S(1)}, f32[6,8,512]{2,1,0:T(8,128)S(1)}, u32[]{:S(2)}, u32[]{:S(2)}) collective-permute-start(f32[6,8,512]{2,1,0:T(8,128)S(1)} %get-tuple-element.24), channel_id=1, source_target_pairs={{1,3},{3,5},{5,7},{7,9},{9,11},{11,13},{13,15},{15,17},{17,19},{19... | collective-permute-start | bytes 294920 | tf_op jit(solution)/shard_map/ppermute | solution.py:635
